TPU v7x, 512 devices: a whole 4x4x16 slice. The times are simulated.
512 devices in a mesh: expert: 32 (over y, x, core), dp: 16 (over z).
Axes of the slice: x: 4, y: 4, z: 16, core: 2. Of those that a mesh axis runs over, the one named last changes fastest.
Arguments:
- tokens: bfloat16 [4096, 7168], P('expert', 'dp'), may hold values from -6 to 6
- routes: int32 [4096, 2], P('expert'), may hold values from 0 to 15, all different within a row; in each aligned block of 128 rows (0 to 127, 128 to 255, ...) at most 32 rows name the same one
- route_weight: float32 [4096, 2], P('expert'), may hold values from 0.1 to 1
- w_gate: bfloat16 [7168, 16384], P('dp', 'expert'), may hold values from -0.0625 to 0.0625
- w_up: bfloat16 [7168, 16384], P('dp', 'expert'), may hold values from -0.0625 to 0.0625
- w_down: bfloat16 [16384, 7168], P('expert', 'dp'), may hold values from -0.1875 to 0.1875
- cotangent: bfloat16 [4096, 7168], P('expert', 'dp'), may hold values from -1.1953125 to 1.1953125
Outputs:
- output: bfloat16 [4096, 7168], P('expert', 'dp')
- grad_tokens: bfloat16 [4096, 7168], P('expert', 'dp')
- grad_gate: bfloat16 [7168, 16384], P('dp', 'expert')
- grad_up: bfloat16 [7168, 16384], P('dp', 'expert')
- grad_down: bfloat16 [16384, 7168], P('expert', 'dp')
Inputs may be any that keep to these rules, and one draw needn't show every extreme that they name: `routes`: each token names 2 different experts. Among the 128 tokens of one index of expert no expert is named more than 32 times, and in every draw some expert is named exactly 32 times by the tokens of some index.
All inputs are finite; a program needn't handle non-finite values.
Results may differ from a plain program's by a relative error of at most 0.035.
Values may be sent and summed in bfloat16 or wider, within the bound.
No kernel may reach another device: no remote copies, remote signals or barrier semaphores. Data moves between devices by JAX's collectives and lax.ppermute only.
A program may use at most 64 MiB of HBM per device.

v0:
```python
import jax
import jax.numpy as jnp
from jax import lax
from jax.sharding import PartitionSpec as P


def contract_last(left, right):
    return lax.dot_general(
        left, right, (((1,), (1,)), ((), ())), preferred_element_type=jnp.float32
    )


def contract_first(left, right):
    return lax.dot_general(
        left, right, (((0,), (0,)), ((), ())), preferred_element_type=jnp.float32
    )


def per_device(tokens, routes, route_weight, w_gate, w_up, w_down, cotangent):
    ntok, dsl = tokens.shape
    top = routes.shape[1]
    n_expert = lax.axis_size("expert")
    experts = n_expert // 2
    half = w_gate.shape[1]
    cap = 2 * max(1, ntok * top // experts)
    flat = routes.reshape(-1)
    onehot = (flat[:, None] == jnp.arange(experts, dtype=jnp.int32)[None, :]).astype(jnp.int32)
    earlier = jnp.cumsum(onehot, axis=0) - onehot
    slot = jnp.sum(earlier * onehot, axis=1)
    place = flat * cap + slot
    picker = (jnp.arange(experts * cap, dtype=jnp.int32)[:, None] == place[None, :]).astype(
        jnp.bfloat16
    )
    tok_rep = jnp.repeat(tokens, top, axis=0)
    scaled = (
        jnp.repeat(cotangent, top, axis=0).astype(jnp.float32) * route_weight.reshape(-1, 1)
    ).astype(jnp.bfloat16)
    rows_x = jnp.dot(picker, tok_rep, preferred_element_type=jnp.float32).astype(jnp.bfloat16)
    rows_dy = jnp.dot(picker, scaled, preferred_element_type=jnp.float32).astype(jnp.bfloat16)
    send_x = jnp.repeat(rows_x.reshape(experts, cap, dsl), 2, axis=0)
    send_dy = jnp.repeat(rows_dy.reshape(experts, cap, dsl), 2, axis=0)
    got_x, got_dy = (
        lax.all_to_all(send_x, "expert", split_axis=0, concat_axis=0, tiled=True),
        lax.all_to_all(send_dy, "expert", split_axis=0, concat_axis=0, tiled=True),
    )
    slot_x = got_x.reshape(-1, dsl)
    slot_dy = got_dy.reshape(-1, dsl)
    terms = jnp.concatenate(
        [
            jnp.dot(slot_x, w_gate, preferred_element_type=jnp.float32),
            jnp.dot(slot_x, w_up, preferred_element_type=jnp.float32),
            contract_last(slot_dy, w_down),
        ],
        axis=1,
    )
    sums = lax.psum_scatter(
        terms.astype(jnp.bfloat16), "dp", scatter_dimension=0, tiled=True
    ).astype(jnp.float32)
    gate_pre = sums[:, :half]
    up_pre = sums[:, half : 2 * half]
    down_back = sums[:, 2 * half :]
    sig = jax.nn.sigmoid(gate_pre)
    active = gate_pre * sig
    hidden = (active * up_pre).astype(jnp.bfloat16)
    grad_gp = (down_back * up_pre * sig * (1.0 + gate_pre * (1.0 - sig))).astype(jnp.bfloat16)
    grad_up = (down_back * active).astype(jnp.bfloat16)
    hid = lax.all_gather(hidden, "dp", axis=0, tiled=True)
    ggp = lax.all_gather(grad_gp, "dp", axis=0, tiled=True)
    gup = lax.all_gather(grad_up, "dp", axis=0, tiled=True)
    out_part = jnp.dot(hid, w_down, preferred_element_type=jnp.float32)
    back = contract_last(ggp, w_gate) + contract_last(gup, w_up)
    back_part = back
    acc_down = contract_first(hid, slot_dy)
    acc_gate = contract_first(slot_x, ggp)
    acc_up = contract_first(slot_x, gup)
    out_part, back_part, acc_down, acc_gate, acc_up = (
        out_part,
        back_part,
        acc_down,
        acc_gate,
        acc_up,
    )
    half_out = out_part.astype(jnp.bfloat16).reshape(n_expert, cap, dsl)
    half_back = back_part.astype(jnp.bfloat16).reshape(n_expert, cap, dsl)
    ret_out, ret_back = (
        lax.all_to_all(half_out, "expert", split_axis=0, concat_axis=0, tiled=True),
        lax.all_to_all(half_back, "expert", split_axis=0, concat_axis=0, tiled=True),
    )
    pair_out = ret_out.reshape(experts, 2, cap, dsl).astype(jnp.float32)
    pair_back = ret_back.reshape(experts, 2, cap, dsl).astype(jnp.float32)
    expert_out = (pair_out[:, 0] + pair_out[:, 1]).astype(jnp.bfloat16)
    expert_back = (pair_back[:, 0] + pair_back[:, 1]).astype(jnp.bfloat16)
    picked_out = jnp.dot(
        picker.T, expert_out.reshape(experts * cap, dsl), preferred_element_type=jnp.float32
    )
    picked_back = jnp.dot(
        picker.T, expert_back.reshape(experts * cap, dsl), preferred_element_type=jnp.float32
    )
    output = jnp.sum(picked_out.reshape(ntok, top, dsl) * route_weight[:, :, None], axis=1).astype(
        jnp.bfloat16
    )
    grad_tokens = jnp.sum(picked_back.reshape(ntok, top, dsl), axis=1).astype(jnp.bfloat16)
    return (
        output,
        grad_tokens,
        acc_gate.astype(jnp.bfloat16),
        acc_up.astype(jnp.bfloat16),
        acc_down.astype(jnp.bfloat16),
    )


def solution(mesh):
    return jax.shard_map(
        per_device,
        mesh=mesh,
        in_specs=(
            P("expert", "dp"),
            P("expert", None),
            P("expert", None),
            P("dp", "expert"),
            P("dp", "expert"),
            P("expert", "dp"),
            P("expert", "dp"),
        ),
        out_specs=(
            P("expert", "dp"),
            P("expert", "dp"),
            P("dp", "expert"),
            P("dp", "expert"),
            P("expert", "dp"),
        ),
        check_vma=False,
    )
```

profile of v0, /device:TPU:1, one launch (start us, length us, event | category | flops | bytes accessed | tf_op | source)
XLA Modules:
  0.0 395.4 jit_solution(5962546642505927577)
XLA Ops:
  12.3 10.6 %all-to-all-start = ((bf16[32,32,448]{2,1,0:T(8,128)(2,1)}), bf16[32,32,448]{2,1,0:T(8,128)(2,1)S(1)}, u32[]{:S(2)}, u32[]{:S(2)}) async-start(bf16[32,32,448]{2,1,0:T(8,128)(2,1)} %bitcast.2), calls=%async_computation | async-start | bytes 2097152 | tf_op jit(solution)/shard_map/all_to_all | solution.py:43
  24.5 15.7 %all-to-all-done = bf16[32,32,448]{2,1,0:T(8,128)(2,1)S(1)} async-done(((bf16[32,32,448]{2,1,0:T(8,128)(2,1)}), bf16[32,32,448]{2,1,0:T(8,128)(2,1)S(1)}, u32[]{:S(2)}, u32[]{:S(2)}) %all-to-all-start) | async-done | bytes 917536 | tf_op jit(solution)/shard_map/all_to_all | solution.py:43
  40.2 1.2 broadcast_in_dim.19
  41.4 4.0 %all-to-all-start.1 = ((bf16[32,32,448]{2,1,0:T(8,128)(2,1)}), bf16[32,32,448]{2,1,0:T(8,128)(2,1)S(1)}, u32[]{:S(2)}, u32[]{:S(2)}) async-start(bf16[32,32,448]{2,1,0:T(8,128)(2,1)} %bitcast.5), calls=%async_computation.1 | async-start | bytes 2097152 | tf_op jit(solution)/shard_map/all_to_all | solution.py:44
  45.4 1.7 convolution_convert_fusion.1
  47.2 1.8 convolution_convert_fusion.2
  48.9 13.7 %all-to-all-done.1 = bf16[32,32,448]{2,1,0:T(8,128)(2,1)S(1)} async-done(((bf16[32,32,448]{2,1,0:T(8,128)(2,1)}), bf16[32,32,448]{2,1,0:T(8,128)(2,1)S(1)}, u32[]{:S(2)}, u32[]{:S(2)}) %all-to-all-start.1) | async-done | bytes 917536 | tf_op jit(solution)/shard_map/all_to_all | solution.py:44
  64.3 1.9 pad_maximum_fusion
  66.2 4.7 %copy.82 = bf16[1024,1536]{1,0:T(8,128)(2,1)} copy(bf16[1024,1536]{0,1:T(8,128)(2,1)} %pad_maximum_fusion) | data formatting | bytes 6291456
  70.9 66.0 %reduce-scatter.4.cloned.1.call-done = bf16[64,1536]{1,0:T(8,128)(2,1)} async-done(((bf16[1024,1536]{1,0:T(8,128)(2,1)}), bf16[64,1536]{1,0:T(8,128)(2,1)}) %reduce-scatter.4.cloned.1.call-update) | async-done | bytes 196624 | tf_op jit(solution)/shard_map/reduce_scatter | solution.py:56
  140.0 67.8 %all-gather.6.cloned.1.call-done = bf16[1024,512]{1,0:T(8,128)(2,1)} async-done(((bf16[64,512]{1,0:T(8,128)(2,1)}), bf16[1024,512]{1,0:T(8,128)(2,1)}) %all-gather.6.cloned.1.call-update) | async-done | bytes 1048592 | tf_op jit(solution)/shard_map/all_gather | solution.py:68
  207.8 1.9 fusion.15
  209.7 68.8 %all-gather.8.cloned.1.call-done = bf16[1024,512]{1,0:T(8,128)(2,1)} async-done(((bf16[64,512]{1,0:T(8,128)(2,1)}), bf16[1024,512]{1,0:T(8,128)(2,1)}) %all-gather.8.cloned.1.call-update) | async-done | bytes 1048592 | tf_op jit(solution)/shard_map/all_gather | solution.py:69
  278.5 2.0 add_convert_fusion
  280.5 1.3 copy.73
  281.8 17.0 %all-to-all-start.3 = ((bf16[32,32,448]{2,1,0:T(8,128)(2,1)}), bf16[32,32,448]{2,1,0:T(8,128)(2,1)S(1)}, u32[]{:S(2)}, u32[]{:S(2)}) async-start(bf16[32,32,448]{2,1,0:T(8,128)(2,1)} %bitcast.12), calls=%async_computation.3 | async-start | bytes 2097152 | tf_op jit(solution)/shard_map/all_to_all | solution.py:87
  299.1 50.1 %all-gather.4.cloned.1.call-done = bf16[1024,512]{1,0:T(8,128)(2,1)} async-done(((bf16[64,512]{1,0:T(8,128)(2,1)}), bf16[1024,512]{1,0:T(8,128)(2,1)}) %all-gather.4.cloned.1.call-update) | async-done | bytes 1048592 | tf_op jit(solution)/shard_map/all_gather | solution.py:67
  349.2 2.0 convolution_convert_fusion.3
  351.3 1.3 copy.68
  352.6 16.7 %all-to-all-start.2 = ((bf16[32,32,448]{2,1,0:T(8,128)(2,1)}), bf16[32,32,448]{2,1,0:T(8,128)(2,1)S(1)}, u32[]{:S(2)}, u32[]{:S(2)}) async-start(bf16[32,32,448]{2,1,0:T(8,128)(2,1)} %bitcast.81), calls=%async_computation.2 | async-start | bytes 2097152 | tf_op jit(solution)/shard_map/all_to_all | solution.py:86
  369.3 3.1 convolution_convert_fusion.7
  372.5 1.4 convolution_convert_fusion.8
  374.0 1.5 convolution_convert_fusion.6
  375.9 10.6 %all-to-all-done.2 = bf16[32,32,448]{2,1,0:T(8,128)(2,1)S(1)} async-done(((bf16[32,32,448]{2,1,0:T(8,128)(2,1)}), bf16[32,32,448]{2,1,0:T(8,128)(2,1)S(1)}, u32[]{:S(2)}, u32[]{:S(2)}) %all-to-all-start.2) | async-done | bytes 917536 | tf_op jit(solution)/shard_map/all_to_all | solution.py:86
  (69 shorter events, 14.5 us)
Async XLA Ops:
  7.2 40.0 %copy-start = (bf16[448,512]{1,0:T(8,128)(2,1)S(1)}, bf16[448,512]{1,0:T(8,128)(2,1)}, u32[]{:S(2)}) copy-start(bf16[448,512]{1,0:T(8,128)(2,1)} %param.10) | copy-start | bytes 1376260
  11.0 11.9 %copy-start.9 = (bf16[128,448]{0,1:T(8,128)(2,1)S(1)}, bf16[128,448]{0,1:T(8,128)(2,1)}, u32[]{:S(2)}) copy-start(bf16[128,448]{0,1:T(8,128)(2,1)} %param.13) | copy-start | bytes 344068
  12.3 11.3 %copy-start.10 = (f32[128,2]{0,1:T(2,128)S(1)}, f32[128,2]{0,1:T(2,128)}, u32[]{:S(2)}) copy-start(f32[128,2]{0,1:T(2,128)} %param.9) | copy-start | bytes 3076
  12.3 27.9 %all-to-all-start = ((bf16[32,32,448]{2,1,0:T(8,128)(2,1)}), bf16[32,32,448]{2,1,0:T(8,128)(2,1)S(1)}, u32[]{:S(2)}, u32[]{:S(2)}) async-start(bf16[32,32,448]{2,1,0:T(8,128)(2,1)} %bitcast.2), calls=%async_computation | async-start | bytes 2097152 | tf_op jit(solution)/shard_map/all_to_all | solution.py:43
  24.3 21.2 %copy-start.8 = (bf16[448,512]{1,0:T(8,128)(2,1)S(1)}, bf16[448,512]{1,0:T(8,128)(2,1)}, u32[]{:S(2)}) copy-start(bf16[448,512]{1,0:T(8,128)(2,1)} %param.11) | copy-start | bytes 1376260
  40.2 7.0 %copy-start.2 = (bf16[32,32,448]{2,1,0:T(8,128)(2,1)}, bf16[32,32,448]{2,1,0:T(8,128)(2,1)S(1)}, u32[]{:S(2)}) copy-start(bf16[32,32,448]{2,1,0:T(8,128)(2,1)S(1)} %all-to-all-done) | copy-start | bytes 2752516
  41.4 21.3 %all-to-all-start.1 = ((bf16[32,32,448]{2,1,0:T(8,128)(2,1)}), bf16[32,32,448]{2,1,0:T(8,128)(2,1)S(1)}, u32[]{:S(2)}, u32[]{:S(2)}) async-start(bf16[32,32,448]{2,1,0:T(8,128)(2,1)} %bitcast.5), calls=%async_computation.1 | async-start | bytes 2097152 | tf_op jit(solution)/shard_map/all_to_all | solution.py:44
  45.4 91.5 %reduce-scatter.4.cloned.1.call-start = ((), (), s32[]{:S(2)}) async-start(), calls=%async_computation.8 | async-start | bytes 3342336 | tf_op jit(solution)/shard_map/reduce_scatter | solution.py:56
  47.2 15.5 %copy-start.12 = (bf16[512,448]{0,1:T(8,128)(2,1)S(1)}, bf16[512,448]{0,1:T(8,128)(2,1)}, u32[]{:S(2)}) copy-start(bf16[512,448]{0,1:T(8,128)(2,1)} %param.12) | copy-start | bytes 1376260
  48.9 14.5 %copy-start.6 = (bf16[1024,512]{0,1:T(8,128)(2,1)S(1)}, bf16[1024,512]{0,1:T(8,128)(2,1)}, u32[]{:S(2)}) copy-start(bf16[1024,512]{0,1:T(8,128)(2,1)} %convolution_convert_fusion.1) | copy-start | bytes 3145732
  62.6 3.5 copy-start.4
  62.7 1.6 copy-start.7
  70.8 137.0 %all-gather.6.cloned.1.call-start = ((), (), s32[]{:S(2)}) async-start(), calls=%async_computation.6 | async-start | bytes 1114112 | tf_op jit(solution)/shard_map/all_gather | solution.py:68
  138.6 139.8 %all-gather.8.cloned.1.call-start = ((), (), s32[]{:S(2)}) async-start(), calls=%async_computation.7 | async-start | bytes 1114112 | tf_op jit(solution)/shard_map/all_gather | solution.py:69
  139.4 209.9 %all-gather.4.cloned.1.call-start = ((), (), s32[]{:S(2)}) async-start(), calls=%async_computation.5 | async-start | bytes 1114112 | tf_op jit(solution)/shard_map/all_gather | solution.py:67
  281.8 70.8 %all-to-all-start.3 = ((bf16[32,32,448]{2,1,0:T(8,128)(2,1)}), bf16[32,32,448]{2,1,0:T(8,128)(2,1)S(1)}, u32[]{:S(2)}, u32[]{:S(2)}) async-start(bf16[32,32,448]{2,1,0:T(8,128)(2,1)} %bitcast.12), calls=%async_computation.3 | async-start | bytes 2097152 | tf_op jit(solution)/shard_map/all_to_all | solution.py:87
  352.6 33.9 %all-to-all-start.2 = ((bf16[32,32,448]{2,1,0:T(8,128)(2,1)}), bf16[32,32,448]{2,1,0:T(8,128)(2,1)S(1)}, u32[]{:S(2)}, u32[]{:S(2)}) async-start(bf16[32,32,448]{2,1,0:T(8,128)(2,1)} %bitcast.81), calls=%async_computation.2 | async-start | bytes 2097152 | tf_op jit(solution)/shard_map/all_to_all | solution.py:86
  369.3 3.1 copy-start.1
  369.3 3.1 copy-start.3
  372.4 1.5 copy-start.5
  372.4 1.5 copy-start.11
Sparse Core Ops, SparseCore 0:
  71.0 65.8 reduce-scatter.3
  139.6 68.1 all-gather.5
  210.5 67.9 all-gather.7
  281.0 68.1 all-gather.3
where the time goes:
time: 396 us; the launch traced here: 395 us
  waiting for transfers between devices  294 us (74%)
  starting transfers between devices  48.4 us (12%)
  matrix products  18.9 us (5%)
  local copies, waits for them, and re-layouts  14.7 us (4%)
  between operations  14.1 us (4%)
  other arithmetic  5.34 us (1%)
    all_gather x1, waiting for transfers between devices, per_device(): gup = lax.all_gather(grad_up, 'dp', axis=0, tiled=True)  68.8 us
    all_gather x1, waiting for transfers between devices, per_device(): ggp = lax.all_gather(grad_gp, 'dp', axis=0, tiled=True)  67.8 us
    reduce_scatter x1, waiting for transfers between devices, per_device(): lax.psum_scatter(terms.astype(jnp.bfloat16), 'dp', scatter_dimension=0, t...  66 us
    all_gather x1, waiting for transfers between devices, per_device(): hid = lax.all_gather(hidden, 'dp', axis=0, tiled=True)  50.1 us
    all_to_all x1, starting transfers between devices, per_device(): lax.all_to_all(half_back, 'expert', split_axis=0, concat_axis=0, tiled=True)  17 us
    all_to_all x1, starting transfers between devices, per_device(): lax.all_to_all(half_out, 'expert', split_axis=0, concat_axis=0, tiled=True)  16.7 us
    all_to_all x1, waiting for transfers between devices, per_device(): lax.all_to_all(send_x, 'expert', split_axis=0, concat_axis=0, tiled=True)  15.7 us
    all_to_all x1, waiting for transfers between devices, per_device(): lax.all_to_all(send_dy, 'expert', split_axis=0, concat_axis=0, tiled=True)  13.7 us
  transfers between devices with their start and end apart: 8, of which 7 were waited for; matrix products, arithmetic and copies ran while one was open for 5% of the time, Pallas kernels for 0%

commit v1 on v0

v1 whole, which is shorter than its diff:
```python
import functools

import jax
import jax.numpy as jnp
from jax import lax
from jax.experimental import pallas as pl
from jax.experimental.pallas import tpu as pltpu
from jax.sharding import PartitionSpec as P

BF = jnp.bfloat16
F32 = jnp.float32
VMEM_BYTES = 48 * 1024 * 1024


def dot_nn(a, b):
    return lax.dot_general(a, b, (((1,), (0,)), ((), ())), preferred_element_type=F32)


def dot_nt(a, b):
    return lax.dot_general(a, b, (((1,), (1,)), ((), ())), preferred_element_type=F32)


def dot_tn(a, b):
    return lax.dot_general(a, b, (((0,), (0,)), ((), ())), preferred_element_type=F32)


def params(**more):
    return pltpu.CompilerParams(vmem_limit_bytes=VMEM_BYTES, **more)


def cost(flops, moved):
    return pl.CostEstimate(flops=flops, bytes_accessed=moved, transcendentals=0)


def pickers(routes, experts, cap):
    top, ntok = routes.shape
    names = lax.broadcasted_iota(jnp.int32, (experts, ntok), 0)
    hits = [routes[k : k + 1, :] == names for k in range(top)]
    mask = sum(jnp.where(h, 1.0, 0.0) for h in hits)
    before = lax.broadcasted_iota(jnp.int32, (ntok, ntok), 0) < lax.broadcasted_iota(
        jnp.int32, (ntok, ntok), 1
    )
    slot = dot_nn(mask.astype(BF), jnp.where(before, 1.0, 0.0).astype(BF))
    want = lax.broadcasted_iota(jnp.int32, (experts, cap, ntok), 1).astype(F32)
    picks = []
    for h in hits:
        own = jnp.where(h, slot, -1.0)
        own = jnp.broadcast_to(own[:, None, :], (experts, cap, ntok))
        pick = jnp.where(own == want, 1.0, 0.0)
        picks.append(pick.reshape(experts * cap, ntok).astype(BF))
    return picks


def send_kernel(experts, cap, tok_ref, cot_ref, routes_ref, weight_ref, out_ref):
    dsl, ntok = tok_ref.shape
    picks = pickers(routes_ref[...], experts, cap)
    x = dot_nt(picks[0] + picks[1], tok_ref[...]).astype(BF)
    out_ref[:, :cap, :] = x.reshape(experts, cap, dsl)
    cot = cot_ref[...].astype(F32)
    weight = weight_ref[...]
    dy = sum(
        dot_nt(picks[k], (cot * weight[k : k + 1, :]).astype(BF)) for k in range(2)
    ).astype(BF)
    out_ref[:, cap:, :] = dy.reshape(experts, cap, dsl)


def terms_kernel(cap, rows_ref, wg_ref, wu_ref, wd_ref, *rest):
    sources, _, dsl = rows_ref.shape
    outs, (held, sems) = rest[:-2], rest[-2:]
    half = wg_ref.shape[1]
    step = 256 // cap
    copies = []
    for lo in range(0, sources, step):
        x = rows_ref[lo : lo + step, :cap, :].reshape(step * cap, dsl)
        dy = rows_ref[lo : lo + step, cap:, :].reshape(step * cap, dsl)
        at = slice(lo * cap, (lo + step) * cap)
        for j, (left, w_ref) in enumerate(((x, wg_ref), (x, wu_ref), (dy, wd_ref))):
            held[at, j * half : (j + 1) * half] = dot_nn(left, w_ref[...]).astype(BF)
            for i in range(lo, lo + step):
                k = 3 * i + j
                copies.append(
                    pltpu.make_async_copy(
                        held.at[pl.ds(i * cap, cap), pl.ds(j * half, half)],
                        outs[k],
                        sems.at[k],
                    )
                )
                copies[-1].start()
    for c in copies:
        c.wait()


def back_kernel(cap, n, *refs):
    pieces, (wg_ref, wu_ref, wd_ref, acts_ref, ret_ref, held, sems) = refs[:n], refs[n:]
    sources = n // 3
    half = wg_ref.shape[1]
    dsl = wg_ref.shape[0]

    def copy(k):
        i, j = divmod(k, 3)
        return pltpu.make_async_copy(
            pieces[k],
            held.at[pl.ds(i * cap, cap), pl.ds(j * half, half)],
            sems.at[k],
        )

    for k in range(n):
        copy(k).start()
    step = 256 // cap
    for lo in range(0, sources, step):
        for k in range(3 * lo, 3 * (lo + step)):
            copy(k).wait()
        at = slice(lo * cap, (lo + step) * cap)
        gate = held[at, :half].astype(F32)
        up = held[at, half : 2 * half].astype(F32)
        down = held[at, 2 * half :].astype(F32)
        sig = jax.nn.sigmoid(gate)
        active = gate * sig
        hid = (active * up).astype(BF)
        ggp = (down * up * sig * (1.0 + gate * (1.0 - sig))).astype(BF)
        gup = (down * active).astype(BF)
        acts_ref[at, :half] = hid
        acts_ref[at, half : 2 * half] = ggp
        acts_ref[at, 2 * half :] = gup
        out = dot_nt(hid, wd_ref[...]).astype(BF)
        back = (dot_nt(ggp, wg_ref[...]) + dot_nt(gup, wu_ref[...])).astype(BF)
        ret_ref[lo : lo + step, :cap, :] = out.reshape(step, cap, dsl)
        ret_ref[lo : lo + step, cap:, :] = back.reshape(step, cap, dsl)


def grads_kernel(cap, own_ref, other_ref, acts_own, acts_other, gg_ref, gu_ref, gd_ref):
    sources, _, dsl = own_ref.shape
    half = gg_ref.shape[1]
    rows = sources * cap

    def both(first, lo):
        a = own_ref[:, first : first + cap, :].reshape(rows, dsl)
        b = other_ref[:, first : first + cap, :].reshape(rows, dsl)
        return dot_tn(a, acts_own[:, lo : lo + half]) + dot_tn(
            b, acts_other[:, lo : lo + half]
        )

    gg_ref[...] = both(0, half).astype(BF)
    gu_ref[...] = both(0, 2 * half).astype(BF)
    gd_ref[...] = both(cap, 0).astype(BF)


def combine_kernel(experts, cap, ret_ref, routes_ref, weight_ref, out_ref, grad_ref):
    dsl = out_ref.shape[0]
    picks = pickers(routes_ref[...], experts, cap)
    weight = weight_ref[...]
    out = ret_ref[:, :cap, :].reshape(experts * cap, dsl)
    back = ret_ref[:, cap:, :].reshape(experts * cap, dsl)
    out_ref[...] = sum(
        dot_tn(out, picks[k]) * weight[k : k + 1, :] for k in range(2)
    ).astype(BF)
    grad_ref[...] = dot_tn(back, picks[0] + picks[1]).astype(BF)


def per_device(tokens, routes, route_weight, w_gate, w_up, w_down, cotangent):
    ntok, dsl = tokens.shape
    top = routes.shape[1]
    n_expert = lax.axis_size("expert")
    experts = n_expert // 2
    half = w_gate.shape[1]
    cap = 2 * max(1, ntok * top // experts)
    rows = experts * cap
    shape = jax.ShapeDtypeStruct
    any_space = pl.BlockSpec(memory_space=pl.ANY)
    vmem = pl.BlockSpec(memory_space=pltpu.VMEM)
    cores = [list(range(c, n_expert, 2)) for c in range(2)]
    swap = [(i, i ^ 1) for i in range(n_expert)]
    flops = 2 * rows * dsl * half

    def exchange(a):
        return lax.all_to_all(
            a, "expert", 0, 0, axis_index_groups=cores, tiled=True
        )

    routes_t, weight_t, w_down_t = routes.T, route_weight.T, w_down.T
    block = shape((experts, 2 * cap, dsl), BF)
    send = pl.pallas_call(
        functools.partial(send_kernel, experts, cap),
        out_shape=block,
        compiler_params=params(),
        cost_estimate=cost(4 * rows * ntok * dsl, 2 * rows * dsl * 4),
    )(tokens.T, cotangent.T, routes_t, weight_t)
    own = exchange(send)
    other = lax.ppermute(own, "expert", swap)

    n = 3 * experts

    def terms(block_rows):
        return pl.pallas_call(
            functools.partial(terms_kernel, cap),
            out_shape=[shape((cap, half), BF)] * n,
            in_specs=[vmem] * 4,
            out_specs=[any_space] * n,
            scratch_shapes=[
                pltpu.VMEM((rows, 3 * half), BF),
                pltpu.SemaphoreType.DMA((n,)),
            ],
            compiler_params=params(),
            cost_estimate=cost(3 * flops, 2 * rows * (dsl * 2 + 3 * half)),
        )(block_rows, w_gate, w_up, w_down_t)

    sums = lax.psum(list(terms(own)) + list(terms(other)), "dp")

    def back(pieces):
        return pl.pallas_call(
            functools.partial(back_kernel, cap, n),
            out_shape=[shape((rows, 3 * half), BF), block],
            in_specs=[any_space] * n + [vmem] * 3,
            out_specs=[vmem] * 2,
            scratch_shapes=[
                pltpu.VMEM((rows, 3 * half), BF),
                pltpu.SemaphoreType.DMA((n,)),
            ],
            compiler_params=params(),
            cost_estimate=cost(3 * flops, 2 * rows * (dsl * 2 + 6 * half)),
        )(*pieces, w_gate, w_up, w_down_t)

    acts_other, ret_other = back(sums[n:])
    theirs = lax.ppermute(ret_other, "expert", swap)
    acts_own, ret_own = back(sums[:n])
    both = (ret_own.astype(F32) + theirs.astype(F32)).astype(BF)
    ret = exchange(both)
    grad_gate, grad_up, grad_down_t = pl.pallas_call(
        functools.partial(grads_kernel, cap),
        out_shape=[shape((dsl, half), BF)] * 3,
        compiler_params=params(),
        cost_estimate=cost(6 * flops, 4 * rows * (dsl * 2 + 3 * half)),
    )(own, other, acts_own, acts_other)
    output_t, grad_tokens_t = pl.pallas_call(
        functools.partial(combine_kernel, experts, cap),
        out_shape=[shape((dsl, ntok), BF)] * 2,
        compiler_params=params(),
        cost_estimate=cost(6 * rows * ntok * dsl, 2 * rows * dsl * 4),
    )(ret, routes_t, weight_t)
    return output_t.T, grad_tokens_t.T, grad_gate, grad_up, grad_down_t.T


def solution(mesh):
    return jax.shard_map(
        per_device,
        mesh=mesh,
        in_specs=(
            P("expert", "dp"),
            P("expert", None),
            P("expert", None),
            P("dp", "expert"),
            P("dp", "expert"),
            P("expert", "dp"),
            P("expert", "dp"),
        ),
        out_specs=(
            P("expert", "dp"),
            P("expert", "dp"),
            P("dp", "expert"),
            P("dp", "expert"),
            P("expert", "dp"),
        ),
        check_vma=False,
    )
```

time: 396 us -> 242 us (0.61); the launches traced: 395 us -> 237 us
  waiting for transfers between devices: 294 us -> 14 us
  blocking collectives: 0 us -> 102 us
  local copies, waits for them, and re-layouts: 14.7 us -> 83.9 us
  starting transfers between devices: 48.4 us -> 19.3 us
  matrix products: 18.9 us -> 0 us
  Pallas kernels: 0 us -> 14.8 us
  between operations: 14.1 us -> 2.08 us
  other arithmetic: 5.34 us -> 1.31 us
    all_gather x3 -> x0, waiting for transfers between devices: 187 us -> none  [the longest x1 68.8 us: per_device(): gup = lax.all_gather(grad_up, 'dp', axis=0, tiled=True)]
    psum x0 -> x1, blocking collectives: none -> 79.1 us  [per_device(): sums = lax.psum(list(terms(own)) + list(terms(other)), 'dp')]
    unnamed x30 -> x406, local copies, waits for them, and re-layouts: 7.58 us -> 83.9 us
    reduce_scatter x1 -> x0, waiting for transfers between devices: 66 us -> none  [per_device(): lax.psum_scatter(terms.astype(jnp.bfloat16), 'dp', scatter_dimension=0, t...]
    all_to_all x4 -> x1, starting transfers between devices: 48.3 us -> 3.65 us  [exchange(): lax.all_to_all(a, 'expert', 0, 0, axis_index_groups=cores, tiled=True)]
    all_to_all x4 -> x1, waiting for transfers between devices: 40 us -> 14 us  [exchange(): lax.all_to_all(a, 'expert', 0, 0, axis_index_groups=cores, tiled=True)]
    all_to_all x0 -> x1, blocking collectives: none -> 22.8 us  [exchange(): lax.all_to_all(a, 'expert', 0, 0, axis_index_groups=cores, tiled=True)]
    dot_general x13 -> x0, matrix products: 18.9 us -> none  [the longest x3 6.02 us: contract_first(): lax.dot_general(left, right, (((0,), (0,)), ((), ())), preferred_element_...]
  transfers between devices with their start and end apart: 8 -> 3, of which waited for: 7 -> 1; matrix products, arithmetic and copies ran while one was open for 5% -> 0% of each run, Pallas kernels for 0% -> 3%
where the time goes in v1:
time: 242 us; the launch traced here: 237 us
  blocking collectives  102 us (42%)
  local copies, waits for them, and re-layouts  83.9 us (35%)
  starting transfers between devices  19.3 us (8%)
  Pallas kernels  14.8 us (6%)
  waiting for transfers between devices  14 us (6%)
    unnamed x406, local copies, waits for them, and re-layouts  83.9 us
    psum x1, blocking collectives, per_device(): sums = lax.psum(list(terms(own)) + list(terms(other)), 'dp')  79.1 us
    all_to_all x1, blocking collectives, exchange(): lax.all_to_all(a, 'expert', 0, 0, axis_index_groups=cores, tiled=True)  22.8 us
    all_to_all x1, waiting for transfers between devices, exchange(): lax.all_to_all(a, 'expert', 0, 0, axis_index_groups=cores, tiled=True)  14 us
    ppermute x1, starting transfers between devices, per_device(): theirs = lax.ppermute(ret_other, 'expert', swap)  10.9 us
    pallas_call x2, Pallas kernels, terms(): pl.pallas_call(functools.partial(terms_kernel, cap), out_shape=[shape((ca...  5.7 us
  transfers between devices with their start and end apart: 3, of which 1 were waited for; matrix products, arithmetic and copies ran while one was open for 0% of the time, Pallas kernels for 3%

profile of v1, /device:TPU:1, one launch (start us, length us, event | category | flops | bytes accessed | tf_op | source)
XLA Modules:
  0.0 237.4 jit_solution(17791841941280976004)
XLA Ops:
  0.6 0.9 copy-done.7
  1.5 0.9 copy-done.8
  4.5 22.8 %all_to_all.10.rows_ref.own_ref = bf16[16,64,448]{2,1,0:T(8,128)(2,1)S(1)} all-to-all(bf16[16,64,448]{2,1,0:T(8,128)(2,1)S(1)} %shard_map.110), channel_id=1, replica_groups={{0,32,64,96,128,160,192,224,256,288,320,352,384,416,448,480},{16,48,80,..., dimensions={0} | all-to-all | bytes 1835008 | tf_op jit(solution)/shard_map/all_to_all | solution.py:176
  27.3 4.8 %collective-permute-start = (bf16[16,64,448]{2,1,0:T(8,128)(2,1)S(1)}, bf16[16,64,448]{2,1,0:T(8,128)(2,1)S(1)}, u32[]{:S(2)}, u32[]{:S(2)}) collective-permute-start(bf16[16,64,448]{2,1,0:T(8,128)(2,1)S(1)} %all_to_all.10.rows_ref.own_ref), channel_id=1, source_target_pairs={{0,16},{16,0},{32,48},{48,32},{64,80},{80,64},{96,112},{112,96},{1... | collective-permute-start | bytes 2752520 | tf_op jit(solution)/shard_map/ppermute | solution.py:189
  32.2 2.8 %shard_map.111 = (bf16[32,512]{1,0:T(8,128)(2,1)S(1)}, bf16[32,512]{1,0:T(8,128)(2,1)S(1)}, bf16[32,512]{1,0:T(8,128)(2,1)S(1)}, bf16[32,512]{1,0:T(8,128)(2,1)S...) custom-call(bf16[16,64,448]{2,1,0:T(8,128)(2,1)S(1)} %all_to_all.10., ...), custom_call_target="tpu_custom_call" | custom-call | flops 704643072 | bytes 2490368 | tf_op jit(solution)/shard_map/pallas_call | solution.py:194
  40.9 2.9 %shard_map.113 = (bf16[32,512]{1,0:T(8,128)(2,1)S(1)}, bf16[32,512]{1,0:T(8,128)(2,1)S(1)}, bf16[32,512]{1,0:T(8,128)(2,1)S(1)}, bf16[32,512]{1,0:T(8,128)(2,1)S...) custom-call(bf16[16,64,448]{2,1,0:T(8,128)(2,1)S(1)} %collective-per, ...), custom_call_target="tpu_custom_call" | custom-call | flops 704643072 | bytes 2490368 | tf_op jit(solution)/shard_map/pallas_call | solution.py:194
  73.0 79.1 %all-reduce.2 = (bf16[32,512]{1,0:T(8,128)(2,1)}, bf16[32,512]{1,0:T(8,128)(2,1)}, bf16[32,512]{1,0:T(8,128)(2,1)}, bf16[32,512]{1,0:T(8,128)(2,1)}, bf16[32,512...) all-reduce(bf16[32,512]{1,0:T(8,128)(2,1)} %copy-done.151, ...), channel_id=1, replica_groups=mesh['expert'=32,'dp'=16] {'dp'}, use_global_device_ids=true, to_apply=%region_48.0 | all-reduce | flops 1572864 | bytes 6291456 | tf_op jit(solution)/shard_map/psum | solution.py:207
  152.5 0.9 copy-done.103
  153.4 0.8 copy-done.104
  161.7 0.8 copy-done.115
  162.5 0.8 copy-done.116
  163.3 0.8 copy-done.117
  189.1 2.4 shard_map.114
  191.4 1.1 copy-done.3
  192.6 10.9 %collective-permute-start.1 = (bf16[16,64,448]{2,1,0:T(8,128)(2,1)S(1)}, bf16[16,64,448]{2,1,0:T(8,128)(2,1)S(1)}, u32[]{:S(2)}, u32[]{:S(2)}) collective-permute-start(bf16[16,64,448]{2,1,0:T(8,128)(2,1)S(1)} %get-tuple-element.207), channel_id=1, source_target_pairs={{0,16},{16,0},{32,48},{48,32},{64,80},{80,64},{96,112},{112,96},{1... | collective-permute-start | bytes 2752520 | tf_op jit(solution)/shard_map/ppermute | solution.py:224
  208.4 2.4 shard_map.112
  210.8 1.2 copy-done.5
  212.0 1.3 add_convert_fusion
  213.3 3.7 %all-to-all-start.1 = ((bf16[16,64,448]{2,1,0:T(8,128)(2,1)}), bf16[16,64,448]{2,1,0:T(8,128)(2,1)S(1)}, u32[]{:S(2)}, u32[]{:S(2)}) async-start(bf16[16,64,448]{2,1,0:T(8,128)(2,1)} %add_convert_fusion), calls=%async_computation.1 | async-start | bytes 2097152 | tf_op jit(solution)/shard_map/all_to_all | solution.py:176
  216.9 1.4 copy-done.4
  218.3 1.4 copy-done.6
  219.8 2.4 %shard_map.116 = (bf16[448,512]{1,0:T(8,128)(2,1)}, bf16[448,512]{1,0:T(8,128)(2,1)}, bf16[448,512]{1,0:T(8,128)(2,1)}) custom-call(bf16[16,64,448]{2,1,0:T(8,128)(2,1)S(1)} %all_to_all.10.rows_ref.own_ref, bf16[16,64,448]{2,1,0:T(8,128)(2,1)S(1)} %collective-permute-done.rows_ref.other_ref, bf16[512,1536]{1,0:T(8,128)(2,1)S(1)} %copy-done.6, ...), custom_call_target="tpu_custom_call" | custom-call | flops 1409286144 | bytes 4980736 | tf_op jit(solution)/shard_map/pallas_call | solution.py:228
  222.1 14.0 %all-to-all-done.1.ret_ref = bf16[16,64,448]{2,1,0:T(8,128)(2,1)S(1)} async-done(((bf16[16,64,448]{2,1,0:T(8,128)(2,1)}), bf16[16,64,448]{2,1,0:T(8,128)(2,1)S(1)}, u32[]{:S(2)}, u32[]{:S(2)}) %all-to-all-start.1) | async-done | bytes 917536 | tf_op jit(solution)/shard_map/all_to_all | solution.py:176
  236.1 1.3 shard_map.115
  (398 shorter events, 73.8 us)
Async XLA Ops:
  27.3 13.5 %collective-permute-start = (bf16[16,64,448]{2,1,0:T(8,128)(2,1)S(1)}, bf16[16,64,448]{2,1,0:T(8,128)(2,1)S(1)}, u32[]{:S(2)}, u32[]{:S(2)}) collective-permute-start(bf16[16,64,448]{2,1,0:T(8,128)(2,1)S(1)} %all_to_all.10.rows_ref.own_ref), channel_id=1, source_target_pairs={{0,16},{16,0},{32,48},{48,32},{64,80},{80,64},{96,112},{112,96},{1... | collective-permute-start | bytes 2752520 | tf_op jit(solution)/shard_map/ppermute | solution.py:189
  152.2 51.3 %copy-start.14 = (bf16[32,512]{1,0:T(8,128)(2,1)S(1)}, bf16[32,512]{1,0:T(8,128)(2,1)}, u32[]{:S(2)}) copy-start(bf16[32,512]{1,0:T(8,128)(2,1)} %get-tuple-element.270.refs_7_) | copy-start | bytes 98308
  152.2 51.3 %copy-start.15 = (bf16[32,512]{1,0:T(8,128)(2,1)S(1)}, bf16[32,512]{1,0:T(8,128)(2,1)}, u32[]{:S(2)}) copy-start(bf16[32,512]{1,0:T(8,128)(2,1)} %get-tuple-element.271.refs_8_) | copy-start | bytes 98308
  152.2 51.3 %copy-start.16 = (bf16[32,512]{1,0:T(8,128)(2,1)S(1)}, bf16[32,512]{1,0:T(8,128)(2,1)}, u32[]{:S(2)}) copy-start(bf16[32,512]{1,0:T(8,128)(2,1)} %get-tuple-element.272.refs_9_) | copy-start | bytes 98308
  152.2 51.3 %copy-start.17 = (bf16[32,512]{1,0:T(8,128)(2,1)S(1)}, bf16[32,512]{1,0:T(8,128)(2,1)}, u32[]{:S(2)}) copy-start(bf16[32,512]{1,0:T(8,128)(2,1)} %get-tuple-element.273.refs_10_) | copy-start | bytes 98308
  152.2 51.3 %copy-start.18 = (bf16[32,512]{1,0:T(8,128)(2,1)S(1)}, bf16[32,512]{1,0:T(8,128)(2,1)}, u32[]{:S(2)}) copy-start(bf16[32,512]{1,0:T(8,128)(2,1)} %get-tuple-element.274.refs_11_) | copy-start | bytes 98308
  152.2 51.3 %copy-start.19 = (bf16[32,512]{1,0:T(8,128)(2,1)S(1)}, bf16[32,512]{1,0:T(8,128)(2,1)}, u32[]{:S(2)}) copy-start(bf16[32,512]{1,0:T(8,128)(2,1)} %get-tuple-element.275.refs_12_) | copy-start | bytes 98308
  152.2 51.3 %copy-start.20 = (bf16[32,512]{1,0:T(8,128)(2,1)S(1)}, bf16[32,512]{1,0:T(8,128)(2,1)}, u32[]{:S(2)}) copy-start(bf16[32,512]{1,0:T(8,128)(2,1)} %get-tuple-element.276.refs_13_) | copy-start | bytes 98308
  152.3 51.3 %copy-start.21 = (bf16[32,512]{1,0:T(8,128)(2,1)S(1)}, bf16[32,512]{1,0:T(8,128)(2,1)}, u32[]{:S(2)}) copy-start(bf16[32,512]{1,0:T(8,128)(2,1)} %get-tuple-element.277.refs_14_) | copy-start | bytes 98308
  152.3 51.3 %copy-start.22 = (bf16[32,512]{1,0:T(8,128)(2,1)S(1)}, bf16[32,512]{1,0:T(8,128)(2,1)}, u32[]{:S(2)}) copy-start(bf16[32,512]{1,0:T(8,128)(2,1)} %get-tuple-element.278.refs_15_) | copy-start | bytes 98308
  152.3 51.3 %copy-start.23 = (bf16[32,512]{1,0:T(8,128)(2,1)S(1)}, bf16[32,512]{1,0:T(8,128)(2,1)}, u32[]{:S(2)}) copy-start(bf16[32,512]{1,0:T(8,128)(2,1)} %get-tuple-element.279.refs_16_) | copy-start | bytes 98308
  152.3 51.3 %copy-start.24 = (bf16[32,512]{1,0:T(8,128)(2,1)S(1)}, bf16[32,512]{1,0:T(8,128)(2,1)}, u32[]{:S(2)}) copy-start(bf16[32,512]{1,0:T(8,128)(2,1)} %get-tuple-element.280.refs_17_) | copy-start | bytes 98308
  152.3 51.3 %copy-start.25 = (bf16[32,512]{1,0:T(8,128)(2,1)S(1)}, bf16[32,512]{1,0:T(8,128)(2,1)}, u32[]{:S(2)}) copy-start(bf16[32,512]{1,0:T(8,128)(2,1)} %get-tuple-element.281.refs_18_) | copy-start | bytes 98308
  152.3 51.3 %copy-start.26 = (bf16[32,512]{1,0:T(8,128)(2,1)S(1)}, bf16[32,512]{1,0:T(8,128)(2,1)}, u32[]{:S(2)}) copy-start(bf16[32,512]{1,0:T(8,128)(2,1)} %get-tuple-element.282.refs_19_) | copy-start | bytes 98308
  152.3 51.3 %copy-start.27 = (bf16[32,512]{1,0:T(8,128)(2,1)S(1)}, bf16[32,512]{1,0:T(8,128)(2,1)}, u32[]{:S(2)}) copy-start(bf16[32,512]{1,0:T(8,128)(2,1)} %get-tuple-element.283.refs_20_) | copy-start | bytes 98308
  152.3 51.3 %copy-start.28 = (bf16[32,512]{1,0:T(8,128)(2,1)S(1)}, bf16[32,512]{1,0:T(8,128)(2,1)}, u32[]{:S(2)}) copy-start(bf16[32,512]{1,0:T(8,128)(2,1)} %get-tuple-element.284.refs_21_) | copy-start | bytes 98308
  152.3 51.3 %copy-start.29 = (bf16[32,512]{1,0:T(8,128)(2,1)S(1)}, bf16[32,512]{1,0:T(8,128)(2,1)}, u32[]{:S(2)}) copy-start(bf16[32,512]{1,0:T(8,128)(2,1)} %get-tuple-element.285.refs_22_) | copy-start | bytes 98308
  152.3 51.3 %copy-start.30 = (bf16[32,512]{1,0:T(8,128)(2,1)S(1)}, bf16[32,512]{1,0:T(8,128)(2,1)}, u32[]{:S(2)}) copy-start(bf16[32,512]{1,0:T(8,128)(2,1)} %get-tuple-element.286.refs_23_) | copy-start | bytes 98308
  152.4 51.3 %copy-start.31 = (bf16[32,512]{1,0:T(8,128)(2,1)S(1)}, bf16[32,512]{1,0:T(8,128)(2,1)}, u32[]{:S(2)}) copy-start(bf16[32,512]{1,0:T(8,128)(2,1)} %get-tuple-element.287.refs_24_) | copy-start | bytes 98308
  152.4 51.3 %copy-start.32 = (bf16[32,512]{1,0:T(8,128)(2,1)S(1)}, bf16[32,512]{1,0:T(8,128)(2,1)}, u32[]{:S(2)}) copy-start(bf16[32,512]{1,0:T(8,128)(2,1)} %get-tuple-element.288.refs_25_) | copy-start | bytes 98308
  152.4 51.3 %copy-start.33 = (bf16[32,512]{1,0:T(8,128)(2,1)S(1)}, bf16[32,512]{1,0:T(8,128)(2,1)}, u32[]{:S(2)}) copy-start(bf16[32,512]{1,0:T(8,128)(2,1)} %get-tuple-element.289.refs_26_) | copy-start | bytes 98308
  152.4 51.3 %copy-start.34 = (bf16[32,512]{1,0:T(8,128)(2,1)S(1)}, bf16[32,512]{1,0:T(8,128)(2,1)}, u32[]{:S(2)}) copy-start(bf16[32,512]{1,0:T(8,128)(2,1)} %get-tuple-element.290.refs_27_) | copy-start | bytes 98308
  192.6 19.4 %collective-permute-start.1 = (bf16[16,64,448]{2,1,0:T(8,128)(2,1)S(1)}, bf16[16,64,448]{2,1,0:T(8,128)(2,1)S(1)}, u32[]{:S(2)}, u32[]{:S(2)}) collective-permute-start(bf16[16,64,448]{2,1,0:T(8,128)(2,1)S(1)} %get-tuple-element.207), channel_id=1, source_target_pairs={{0,16},{16,0},{32,48},{48,32},{64,80},{80,64},{96,112},{112,96},{1... | collective-permute-start | bytes 2752520 | tf_op jit(solution)/shard_map/ppermute | solution.py:224
  213.3 22.8 %all-to-all-start.1 = ((bf16[16,64,448]{2,1,0:T(8,128)(2,1)}), bf16[16,64,448]{2,1,0:T(8,128)(2,1)S(1)}, u32[]{:S(2)}, u32[]{:S(2)}) async-start(bf16[16,64,448]{2,1,0:T(8,128)(2,1)} %add_convert_fusion), calls=%async_computation.1 | async-start | bytes 2097152 | tf_op jit(solution)/shard_map/all_to_all | solution.py:176
  (182 other events, 2431.7 us)

commit v2 on v1

v2 whole, which is shorter than its diff:
```python
import functools

import jax
import jax.numpy as jnp
from jax import lax
from jax.experimental import pallas as pl
from jax.experimental.pallas import tpu as pltpu
from jax.sharding import PartitionSpec as P

BF = jnp.bfloat16
F32 = jnp.float32
VMEM_BYTES = 24 * 1024 * 1024


def dot_nn(a, b):
    return lax.dot_general(a, b, (((1,), (0,)), ((), ())), preferred_element_type=F32)


def dot_nt(a, b):
    return lax.dot_general(a, b, (((1,), (1,)), ((), ())), preferred_element_type=F32)


def dot_tn(a, b):
    return lax.dot_general(a, b, (((0,), (0,)), ((), ())), preferred_element_type=F32)


def params(**more):
    return pltpu.CompilerParams(vmem_limit_bytes=VMEM_BYTES, **more)


def cost(flops, moved):
    return pl.CostEstimate(flops=flops, bytes_accessed=moved, transcendentals=0)


def pickers(routes, experts, cap):
    top, ntok = routes.shape
    names = lax.broadcasted_iota(jnp.int32, (experts, ntok), 0)
    hits = [routes[k : k + 1, :] == names for k in range(top)]
    mask = sum(jnp.where(h, 1.0, 0.0) for h in hits)
    before = lax.broadcasted_iota(jnp.int32, (ntok, ntok), 0) < lax.broadcasted_iota(
        jnp.int32, (ntok, ntok), 1
    )
    slot = dot_nn(mask.astype(BF), jnp.where(before, 1.0, 0.0).astype(BF))
    want = lax.broadcasted_iota(jnp.int32, (experts, cap, ntok), 1).astype(F32)
    picks = []
    for h in hits:
        own = jnp.where(h, slot, -1.0)
        own = jnp.broadcast_to(own[:, None, :], (experts, cap, ntok))
        pick = jnp.where(own == want, 1.0, 0.0)
        picks.append(pick.reshape(experts * cap, ntok).astype(BF))
    return picks


def send_kernel(
    experts, cap, tok_hbm, cot_hbm, routes_hbm, weight_hbm, wg_hbm, wu_hbm, wd_hbm,
    out_ref, stack_hbm, tok_ref, cot_ref, routes_ref, weight_ref, sems,
):
    dsl, ntok = tok_ref.shape
    pairs = (
        (routes_hbm, routes_ref),
        (tok_hbm, tok_ref),
        (weight_hbm, weight_ref),
        (cot_hbm, cot_ref),
        (wg_hbm, stack_hbm.at[0]),
        (wu_hbm, stack_hbm.at[1]),
        (wd_hbm, stack_hbm.at[2]),
    )
    copies = [
        pltpu.make_async_copy(src, dst, sems.at[i])
        for i, (src, dst) in enumerate(pairs)
    ]
    for c in copies:
        c.start()
    copies[0].wait()
    picks = pickers(routes_ref[...], experts, cap)
    copies[1].wait()
    x = dot_nt(picks[0] + picks[1], tok_ref[...]).astype(BF)
    out_ref[:, :cap, :] = x.reshape(experts, cap, dsl)
    copies[2].wait()
    copies[3].wait()
    cot = cot_ref[...].astype(F32)
    weight = weight_ref[...]
    dy = sum(
        dot_nt(picks[k], (cot * weight[k : k + 1, :]).astype(BF)) for k in range(2)
    ).astype(BF)
    out_ref[:, cap:, :] = dy.reshape(experts, cap, dsl)
    for c in copies[4:]:
        c.wait()


def terms_kernel(cap, rows_ref, own_ref, other_ref, *rest):
    sources, _, dsl = rows_ref.shape
    outs, (held, sems) = rest[:-2], rest[-2:]
    half = own_ref.shape[2]
    step = 256 // cap
    copies = []
    for lo in range(0, sources, step):
        x = rows_ref[lo : lo + step, :cap, :].reshape(step * cap, dsl)
        dy = rows_ref[lo : lo + step, cap:, :].reshape(step * cap, dsl)
        at = slice(lo * cap, (lo + step) * cap)
        for q in range(6):
            j, h = divmod(q, 2)
            w = (own_ref, other_ref)[h][j]
            left = dy if j == 2 else x
            held[at, q * half : (q + 1) * half] = dot_nn(left, w).astype(BF)
            for i in range(lo, lo + step):
                k = 6 * i + q
                copies.append(
                    pltpu.make_async_copy(
                        held.at[pl.ds(i * cap, cap), pl.ds(q * half, half)],
                        outs[k],
                        sems.at[k],
                    )
                )
                copies[-1].start()
    for c in copies:
        c.wait()


def back_kernel(cap, n, *refs):
    pieces, (own_ref, other_ref, acts_ref, ret_ref, held, sems) = refs[:n], refs[n:]
    sources = n // 6
    dsl, half = own_ref.shape[1:]

    def copy(k):
        i, q = divmod(k, 6)
        return pltpu.make_async_copy(
            pieces[k],
            held.at[pl.ds(i * cap, cap), pl.ds(q * half, half)],
            sems.at[k],
        )

    for k in range(n):
        copy(k).start()
    step = 256 // cap
    for lo in range(0, sources, step):
        for k in range(6 * lo, 6 * (lo + step)):
            copy(k).wait()
        at = slice(lo * cap, (lo + step) * cap)
        out = back = None
        for h, w_ref in enumerate((own_ref, other_ref)):
            gate, up, down = (
                held[at, (2 * j + h) * half : (2 * j + h + 1) * half].astype(F32)
                for j in range(3)
            )
            sig = jax.nn.sigmoid(gate)
            active = gate * sig
            hid = (active * up).astype(BF)
            ggp = (down * up * sig * (1.0 + gate * (1.0 - sig))).astype(BF)
            gup = (down * active).astype(BF)
            for j, a in enumerate((ggp, gup, hid)):
                acts_ref[at, (3 * h + j) * half : (3 * h + j + 1) * half] = a
            part = dot_nt(hid, w_ref[2])
            out = part if out is None else out + part
            part = dot_nt(ggp, w_ref[0]) + dot_nt(gup, w_ref[1])
            back = part if back is None else back + part
        ret_ref[lo : lo + step, :cap, :] = out.astype(BF).reshape(step, cap, dsl)
        ret_ref[lo : lo + step, cap:, :] = back.astype(BF).reshape(step, cap, dsl)


def grad_of(cap, rows_ref, acts_ref, j):
    sources, _, dsl = rows_ref.shape
    half = acts_ref.shape[1] // 3
    first = cap if j == 2 else 0
    left = rows_ref[:, first : first + cap, :].reshape(sources * cap, dsl)
    return dot_tn(left, acts_ref[:, j * half : (j + 1) * half])


def other_grads_kernel(cap, rows_ref, acts_ref, out_ref):
    for j in range(3):
        out_ref[j] = grad_of(cap, rows_ref, acts_ref, j).astype(BF)


def own_grads_kernel(cap, rows_ref, acts_ref, theirs_ref, *outs):
    for j in range(3):
        part = grad_of(cap, rows_ref, acts_ref, j)
        outs[j][...] = (part + theirs_ref[j].astype(F32)).astype(BF)


def combine_kernel(experts, cap, ret_ref, routes_ref, weight_ref, out_ref, grad_ref):
    dsl = out_ref.shape[0]
    picks = pickers(routes_ref[...], experts, cap)
    weight = weight_ref[...]
    out = ret_ref[:, :cap, :].reshape(experts * cap, dsl)
    back = ret_ref[:, cap:, :].reshape(experts * cap, dsl)
    out_ref[...] = sum(
        dot_tn(out, picks[k]) * weight[k : k + 1, :] for k in range(2)
    ).astype(BF)
    grad_ref[...] = dot_tn(back, picks[0] + picks[1]).astype(BF)


def per_device(tokens, routes, route_weight, w_gate, w_up, w_down, cotangent):
    ntok, dsl = tokens.shape
    top = routes.shape[1]
    n_expert = lax.axis_size("expert")
    experts = n_expert // 2
    half = w_gate.shape[1]
    cap = 2 * max(1, ntok * top // experts)
    rows = experts * cap
    shape = jax.ShapeDtypeStruct
    hbm = pl.BlockSpec(memory_space=pltpu.HBM)
    vmem = pl.BlockSpec(memory_space=pltpu.VMEM)
    cores = [list(range(c, n_expert, 2)) for c in range(2)]
    swap = [(i, i ^ 1) for i in range(n_expert)]
    flops = 2 * rows * dsl * half

    def in_hbm(a):
        return pltpu.with_memory_space_constraint(a, pltpu.HBM)

    def exchange(a):
        return lax.all_to_all(a, "expert", 0, 0, axis_index_groups=cores, tiled=True)

    routes_t, weight_t = routes.T, route_weight.T
    block = shape((experts, 2 * cap, dsl), BF)
    stack = shape((3, dsl, half), BF)
    send, w_own = pl.pallas_call(
        functools.partial(send_kernel, experts, cap),
        out_shape=[block, stack],
        in_specs=[hbm] * 7,
        out_specs=[vmem, pl.BlockSpec(memory_space=pl.ANY)],
        scratch_shapes=[
            pltpu.VMEM((dsl, ntok), BF),
            pltpu.VMEM((dsl, ntok), BF),
            pltpu.VMEM((top, ntok), jnp.int32),
            pltpu.VMEM((top, ntok), F32),
            pltpu.SemaphoreType.DMA((7,)),
        ],
        compiler_params=params(),
        cost_estimate=cost(4 * rows * ntok * dsl, 2 * rows * dsl * 4),
    )(
        *(
            in_hbm(a)
            for a in (
                tokens.T, cotangent.T, routes_t, weight_t, w_gate, w_up, w_down.T
            )
        )
    )
    got = exchange(send)
    w_other = lax.ppermute(w_own, "expert", swap)

    n = 6 * experts
    pieces = pl.pallas_call(
        functools.partial(terms_kernel, cap),
        out_shape=[pltpu.HBM((cap, half), BF)] * n,
        in_specs=[vmem] * 3,
        out_specs=[hbm] * n,
        scratch_shapes=[
            pltpu.VMEM((rows, 6 * half), BF),
            pltpu.SemaphoreType.DMA((n,)),
        ],
        compiler_params=params(),
        cost_estimate=cost(6 * flops, 2 * rows * (dsl * 2 + 6 * half)),
    )(got, w_own, w_other)
    sums = [in_hbm(a) for a in lax.psum(list(pieces), "dp")]
    acts, ret = pl.pallas_call(
        functools.partial(back_kernel, cap, n),
        out_shape=[shape((rows, 6 * half), BF), block],
        in_specs=[hbm] * n + [vmem] * 2,
        out_specs=[vmem] * 2,
        scratch_shapes=[
            pltpu.VMEM((rows, 6 * half), BF),
            pltpu.SemaphoreType.DMA((n,)),
        ],
        compiler_params=params(),
        cost_estimate=cost(6 * flops, 2 * rows * (dsl * 2 + 12 * half)),
    )(*sums, w_own, w_other)
    ret = exchange(ret)

    whole = [
        pl.BlockSpec(block.shape, lambda i: (0, 0, 0)),
        pl.BlockSpec((rows, 3 * half), lambda i: (0, 1)),
    ]
    half_cost = cost(3 * flops, 2 * rows * (dsl * 2 + 3 * half))
    for_other = pl.pallas_call(
        functools.partial(other_grads_kernel, cap),
        grid=(1,),
        out_shape=stack,
        in_specs=whole,
        out_specs=pl.BlockSpec(stack.shape, lambda i: (0, 0, 0)),
        compiler_params=params(),
        cost_estimate=half_cost,
    )(got, acts)
    theirs = lax.ppermute(for_other, "expert", swap)
    whole[1] = pl.BlockSpec((rows, 3 * half), lambda i: (0, 0))
    grad_gate, grad_up, grad_down_t = pl.pallas_call(
        functools.partial(own_grads_kernel, cap),
        grid=(1,),
        out_shape=[shape((dsl, half), BF)] * 3,
        in_specs=whole + [pl.BlockSpec(stack.shape, lambda i: (0, 0, 0))],
        out_specs=[pl.BlockSpec((dsl, half), lambda i: (0, 0))] * 3,
        compiler_params=params(),
        cost_estimate=half_cost,
    )(got, acts, theirs)
    output_t, grad_tokens_t = pl.pallas_call(
        functools.partial(combine_kernel, experts, cap),
        out_shape=[shape((dsl, ntok), BF)] * 2,
        compiler_params=params(),
        cost_estimate=cost(6 * rows * ntok * dsl, 2 * rows * dsl * 4),
    )(ret, routes_t, weight_t)
    return output_t.T, grad_tokens_t.T, grad_gate, grad_up, grad_down_t.T


def solution(mesh):
    return jax.shard_map(
        per_device,
        mesh=mesh,
        in_specs=(
            P("expert", "dp"),
            P("expert", None),
            P("expert", None),
            P("dp", "expert"),
            P("dp", "expert"),
            P("expert", "dp"),
            P("expert", "dp"),
        ),
        out_specs=(
            P("expert", "dp"),
            P("expert", "dp"),
            P("dp", "expert"),
            P("dp", "expert"),
            P("expert", "dp"),
        ),
        check_vma=False,
    )
```

time: 242 us -> 153 us (0.63); the launches traced: 237 us -> 153 us
  local copies, waits for them, and re-layouts: 83.9 us -> 1.35 us
  blocking collectives: 102 us -> 117 us
  waiting for transfers between devices: 14 us -> 0.01 us
    unnamed x406 -> x8, local copies, waits for them, and re-layouts: 83.9 us -> 1.35 us
    all_to_all x1 -> x2, blocking collectives: 22.8 us -> 39.6 us  [exchange(): lax.all_to_all(a, 'expert', 0, 0, axis_index_groups=cores, tiled=True)]
    all_to_all x1 -> x0, waiting for transfers between devices: 14 us -> none  [exchange(): lax.all_to_all(a, 'expert', 0, 0, axis_index_groups=cores, tiled=True)]
    ppermute x2, starting transfers between devices: 15.7 us -> 20.2 us  [the longest x1 11.4 us: per_device(): theirs = lax.ppermute(for_other, 'expert', swap)]
    all_to_all x1 -> x0, starting transfers between devices: 3.65 us -> none  [exchange(): lax.all_to_all(a, 'expert', 0, 0, axis_index_groups=cores, tiled=True)]
    pallas_call x6 -> x5, Pallas kernels: 13.5 us -> 12.3 us  [the longest x1 4.6 us: per_device(): pl.pallas_call(functools.partial(back_kernel, cap, n), out_shape=[shape((...]
  transfers between devices with their start and end apart: 3 -> 2, of which waited for: 1 -> 0; matrix products, arithmetic and copies ran while one was open for 0% -> 0% of each run, Pallas kernels for 3% -> 1%
where the time goes in v2:
time: 153 us
  blocking collectives  117 us (76%)
  starting transfers between devices  20.2 us (13%)
  Pallas kernels  13.6 us (9%)
    psum x1, blocking collectives, per_device(): sums = [in_hbm(a) for a in lax.psum(list(pieces), 'dp')]  77.4 us
    all_to_all x2, blocking collectives, exchange(): lax.all_to_all(a, 'expert', 0, 0, axis_index_groups=cores, tiled=True)  39.6 us
    ppermute x1, starting transfers between devices, per_device(): theirs = lax.ppermute(for_other, 'expert', swap)  11.4 us
    ppermute x1, starting transfers between devices, per_device(): w_other = lax.ppermute(w_own, 'expert', swap)  8.79 us
    pallas_call x1, Pallas kernels, per_device(): pl.pallas_call(functools.partial(back_kernel, cap, n), out_shape=[shape((...  4.6 us
    pallas_call x1, Pallas kernels, per_device(): pl.pallas_call(functools.partial(terms_kernel, cap), out_shape=[pltpu.HBM...  3.32 us
  transfers between devices with their start and end apart: 2, of which 0 were waited for; matrix products, arithmetic and copies ran while one was open for 0% of the time, Pallas kernels for 1%

profile of v2, /device:TPU:1, one launch (start us, length us, event | category | flops | bytes accessed | tf_op | source)
XLA Modules:
  0.0 152.8 jit_solution(5403073896218428509)
XLA Ops:
  0.6 1.7 %shard_map.110 = (bf16[16,64,448]{2,1,0:T(8,128)(2,1)S(1)}, bf16[3,448,512]{2,1,0:T(8,128)(2,1)S(1)}) custom-call(bf16[448,128]{1,0:T(8,128)(2,1)} %bitcast.13, bf16[448,128]{1,0:T(8,128)(2,1)} %bitcast.14, s32[2,128]{1,0:T(2,128)} %bitcast.8, f32[2,128]{1,0:T(2,128)} %bitcast.10, bf16[448,512]{1,0:T(8,128)(2,1)} %wg_hbm.1, bf16[448,512]{1,0:T(8,128)(2,1)} %wu_hbm.1, ...), custom_call_target="tpu_custom_call" | custom-call | flops 117440512 | bytes 1835008 | tf_op jit(solution)/shard_map/pallas_call | solution.py:216
  2.4 8.8 %collective-permute-start = (bf16[3,448,512]{2,1,0:T(8,128)(2,1)S(1)}, bf16[3,448,512]{2,1,0:T(8,128)(2,1)S(1)}, u32[]{:S(2)}, u32[]{:S(2)}) collective-permute-start(bf16[3,448,512]{2,1,0:T(8,128)(2,1)S(1)} %get-tuple-element.111.own_ref.refs_96_), channel_id=1, source_target_pairs={{0,16},{16,0},{32,48},{48,32},{64,80},{80,64},{96,112},{112,96},{1... | collective-permute-start | bytes 4128776 | tf_op jit(solution)/shard_map/ppermute | solution.py:239
  11.2 19.7 %all_to_all.10.rows_ref = bf16[16,64,448]{2,1,0:T(8,128)(2,1)S(1)} all-to-all(bf16[16,64,448]{2,1,0:T(8,128)(2,1)S(1)} %get-tuple-element.110), channel_id=1, replica_groups={{0,32,64,96,128,160,192,224,256,288,320,352,384,416,448,480},{16,48,80,..., dimensions={0} | all-to-all | bytes 1835008 | tf_op jit(solution)/shard_map/all_to_all | solution.py:211
  30.9 0.0 collective-permute-done.other_ref.refs_97_
  30.9 0.0 copy-start
  30.9 3.3 %shard_map.111 = (bf16[32,512]{1,0:T(8,128)(2,1)}, bf16[32,512]{1,0:T(8,128)(2,1)}, bf16[32,512]{1,0:T(8,128)(2,1)}, bf16[32,512]{1,0:T(8,128)(2,1)}, bf16[32,51...) custom-call(bf16[16,64,448]{2,1,0:T(8,128)(2,1)S(1)} %all_to_all.10., ...), custom_call_target="tpu_custom_call" | custom-call | flops 1409286144 | bytes 4063232 | tf_op jit(solution)/shard_map/pallas_call | solution.py:242
  34.2 0.0 copy-done
  34.2 77.4 %all-reduce.2 = (bf16[32,512]{1,0:T(8,128)(2,1)}, bf16[32,512]{1,0:T(8,128)(2,1)}, bf16[32,512]{1,0:T(8,128)(2,1)}, bf16[32,512]{1,0:T(8,128)(2,1)}, bf16[32,512...) all-reduce(bf16[32,512]{1,0:T(8,128)(2,1)} %get-tuple-element.112, ...), channel_id=1, replica_groups=mesh['expert'=32,'dp'=16] {'dp'}, use_global_device_ids=true, to_apply=%region_0.0 | all-reduce | flops 1572864 | bytes 6291456 | tf_op jit(solution)/shard_map/psum | solution.py:254
  111.6 0.0 copy-start.1
  111.6 1.3 copy-done.1
  112.9 4.6 %shard_map.112 = (bf16[512,3072]{1,0:T(8,128)(2,1)S(1)}, bf16[16,64,448]{2,1,0:T(8,128)(2,1)S(1)}) custom-call(bf16[32,512]{1,0:T(8,128)(2,1)} %get-tuple-element.215.refs_0_, bf16[32,512]{1,0:T(8,128)(2,1)} %get-tuple-element.216.refs_1_, bf16[32,512]{1,0:T(8,128)(2,1)} %get-tuple-element.217.refs_2_, bf16[32,512]{1,0:T(8,128)(2,1)} %get-tuple-element.218.refs_3_, ...), custom_call_target="tpu_custom_call" | custom-call | flops 1409286144 | bytes 7208960 | tf_op jit(solution)/shard_map/pallas_call | solution.py:255
  117.5 0.9 shard_map.114
  118.4 0.0 copy-start.2
  118.4 0.0 copy-start.3
  118.4 11.4 %collective-permute-start.1 = (bf16[3,448,512]{2,1,0:T(8,128)(2,1)S(1)}, bf16[3,448,512]{2,1,0:T(8,128)(2,1)S(1)}, u32[]{:S(2)}, u32[]{:S(2)}) collective-permute-start(bf16[3,448,512]{2,1,0:T(8,128)(2,1)S(1)} %shard_map.114), channel_id=1, source_target_pairs={{0,16},{16,0},{32,48},{48,32},{64,80},{80,64},{96,112},{112,96},{1... | collective-permute-start | bytes 4128776 | tf_op jit(solution)/shard_map/ppermute | solution.py:283
  129.8 19.9 %all_to_all.11.ret_ref = bf16[16,64,448]{2,1,0:T(8,128)(2,1)S(1)} all-to-all(bf16[16,64,448]{2,1,0:T(8,128)(2,1)S(1)} %get-tuple-element.208), channel_id=1, replica_groups={{0,32,64,96,128,160,192,224,256,288,320,352,384,416,448,480},{16,48,80,..., dimensions={0} | all-to-all | bytes 1835008 | tf_op jit(solution)/shard_map/all_to_all | solution.py:211
  149.8 0.0 copy-done.2
  149.8 0.0 copy-done.3
  149.8 1.3 shard_map.113
  151.1 0.0 collective-permute-done.1.theirs_ref
  151.1 1.7 %shard_map.115 = (bf16[448,512]{1,0:T(8,128)(2,1)}, bf16[448,512]{1,0:T(8,128)(2,1)}, bf16[448,512]{1,0:T(8,128)(2,1)}) custom-call(bf16[16,64,448]{2,1,0:T(8,128)(2,1)S(1)} %all_to_all.10.rows_ref, bf16[512,3072]{1,0:T(8,128)(2,1)S(1)} %get-tuple-element.211.acts_ref, bf16[3,448,512]{2,1,0:T(8,128)(2,1)S(1)} %collective-permute-done.1.theirs_ref), custom_call_target="tpu_custom_call" | custom-call | flops 704643072 | bytes 2490368 | tf_op jit(solution)/shard_map/pallas_call | solution.py:285
Async XLA Ops:
  2.4 28.5 %collective-permute-start = (bf16[3,448,512]{2,1,0:T(8,128)(2,1)S(1)}, bf16[3,448,512]{2,1,0:T(8,128)(2,1)S(1)}, u32[]{:S(2)}, u32[]{:S(2)}) collective-permute-start(bf16[3,448,512]{2,1,0:T(8,128)(2,1)S(1)} %get-tuple-element.111.own_ref.refs_96_), channel_id=1, source_target_pairs={{0,16},{16,0},{32,48},{48,32},{64,80},{80,64},{96,112},{112,96},{1... | collective-permute-start | bytes 4128776 | tf_op jit(solution)/shard_map/ppermute | solution.py:239
  30.9 3.3 %copy-start = (bf16[3,448,512]{2,1,0:T(8,128)(2,1)}, bf16[3,448,512]{2,1,0:T(8,128)(2,1)S(1)}, u32[]{:S(2)}) copy-start(bf16[3,448,512]{2,1,0:T(8,128)(2,1)S(1)} %collective-permute-done.other_ref.refs_97_) | copy-start | bytes 4128772
  111.6 1.3 copy-start.1
  118.4 31.3 %copy-start.2 = (s32[128,2]{0,1:T(2,128)S(1)}, s32[128,2]{0,1:T(2,128)}, u32[]{:S(2)}) copy-start(s32[128,2]{0,1:T(2,128)} %param.8) | copy-start | bytes 3076
  118.4 31.3 %copy-start.3 = (f32[128,2]{0,1:T(2,128)S(1)}, f32[128,2]{0,1:T(2,128)}, u32[]{:S(2)}) copy-start(f32[128,2]{0,1:T(2,128)} %param.9) | copy-start | bytes 3076
  118.4 32.6 %collective-permute-start.1 = (bf16[3,448,512]{2,1,0:T(8,128)(2,1)S(1)}, bf16[3,448,512]{2,1,0:T(8,128)(2,1)S(1)}, u32[]{:S(2)}, u32[]{:S(2)}) collective-permute-start(bf16[3,448,512]{2,1,0:T(8,128)(2,1)S(1)} %shard_map.114), channel_id=1, source_target_pairs={{0,16},{16,0},{32,48},{48,32},{64,80},{80,64},{96,112},{112,96},{1... | collective-permute-start | bytes 4128776 | tf_op jit(solution)/shard_map/ppermute | solution.py:283

commit v3 on v2

--- a/solution.py
+++ b/solution.py
@@ -51,19 +51,50 @@
     return picks
 
 
+LANES = 128
+
+
+def tiles(ref, lo, hi, cap, which):
+    return jnp.concatenate(
+        [
+            ref[lo:hi, t * cap : (t + 1) * cap, :].reshape((hi - lo) * cap, LANES)
+            for t in which
+        ],
+        axis=1,
+    )
+
+
+def put_tile(ref, lo, hi, cap, t, value):
+    ref[lo:hi, t * cap : (t + 1) * cap, :] = value.reshape(hi - lo, cap, LANES)
+
+
+def layout(dsl):
+    full = dsl // LANES
+    assert 2 * (dsl - full * LANES) == LANES
+    first = [*range(full), 2 * full]
+    return full * LANES, first, [*range(full, 2 * full), 2 * full]
+
+
 def send_kernel(
     experts, cap, tok_hbm, cot_hbm, routes_hbm, weight_hbm, wg_hbm, wu_hbm, wd_hbm,
-    out_ref, stack_hbm, tok_ref, cot_ref, routes_ref, weight_ref, sems,
+    out_ref, stack_hbm, tok_ref, cot_ref, routes_ref, weight_ref, zeros, sems,
 ):
     dsl, ntok = tok_ref.shape
+    main, first, _ = layout(dsl)
+    tail = dsl - main
+    zeros[...] = jnp.zeros_like(zeros)
     pairs = (
         (routes_hbm, routes_ref),
         (tok_hbm, tok_ref),
         (weight_hbm, weight_ref),
         (cot_hbm, cot_ref),
-        (wg_hbm, stack_hbm.at[0]),
-        (wu_hbm, stack_hbm.at[1]),
-        (wd_hbm, stack_hbm.at[2]),
+        (wg_hbm, stack_hbm.at[0, pl.ds(0, dsl)]),
+        (wu_hbm, stack_hbm.at[1, pl.ds(0, dsl)]),
+        (wd_hbm.at[pl.ds(0, main)], stack_hbm.at[2, pl.ds(0, main)]),
+        (wd_hbm.at[pl.ds(main, tail)], stack_hbm.at[2, pl.ds(dsl, tail)]),
+        (zeros, stack_hbm.at[0, pl.ds(dsl, tail)]),
+        (zeros, stack_hbm.at[1, pl.ds(dsl, tail)]),
+        (zeros, stack_hbm.at[2, pl.ds(main, tail)]),
     )
     copies = [
         pltpu.make_async_copy(src, dst, sems.at[i])
@@ -73,30 +104,34 @@
         c.start()
     copies[0].wait()
     picks = pickers(routes_ref[...], experts, cap)
-    copies[1].wait()
-    x = dot_nt(picks[0] + picks[1], tok_ref[...]).astype(BF)
-    out_ref[:, :cap, :] = x.reshape(experts, cap, dsl)
-    copies[2].wait()
-    copies[3].wait()
+    for c in copies[1:4]:
+        c.wait()
+    tok = tok_ref[...]
     cot = cot_ref[...].astype(F32)
     weight = weight_ref[...]
-    dy = sum(
-        dot_nt(picks[k], (cot * weight[k : k + 1, :]).astype(BF)) for k in range(2)
-    ).astype(BF)
-    out_ref[:, cap:, :] = dy.reshape(experts, cap, dsl)
+    rows = None
+    for k, pick in enumerate(picks):
+        dy = (cot * weight[k : k + 1, :]).astype(BF)
+        right = jnp.concatenate([tok[:main], dy[:main], tok[main:], dy[main:]], axis=0)
+        part = dot_nt(pick, right)
+        rows = part if rows is None else rows + part
+    rows = rows.astype(BF)
+    for t in range(2 * len(first) - 1):
+        put_tile(out_ref, 0, experts, cap, t, rows[:, t * LANES : (t + 1) * LANES])
     for c in copies[4:]:
         c.wait()
 
 
-def terms_kernel(cap, rows_ref, own_ref, other_ref, *rest):
-    sources, _, dsl = rows_ref.shape
+def terms_kernel(dsl, cap, rows_ref, own_ref, other_ref, *rest):
+    sources = rows_ref.shape[0]
     outs, (held, sems) = rest[:-2], rest[-2:]
+    _, first, second = layout(dsl)
     half = own_ref.shape[2]
     step = 256 // cap
     copies = []
     for lo in range(0, sources, step):
-        x = rows_ref[lo : lo + step, :cap, :].reshape(step * cap, dsl)
-        dy = rows_ref[lo : lo + step, cap:, :].reshape(step * cap, dsl)
+        x = tiles(rows_ref, lo, lo + step, cap, first)
+        dy = tiles(rows_ref, lo, lo + step, cap, second)
         at = slice(lo * cap, (lo + step) * cap)
         for q in range(6):
             j, h = divmod(q, 2)
@@ -117,10 +152,15 @@
         c.wait()
 
 
-def back_kernel(cap, n, *refs):
-    pieces, (own_ref, other_ref, acts_ref, ret_ref, held, sems) = refs[:n], refs[n:]
+def back_kernel(dsl, cap, n, *refs):
+    pieces, (own_hbm, other_hbm, acts_ref, ret_hbm, held, own_ref, other_ref, ret_ref, sems) = (
+        refs[:n],
+        refs[n:],
+    )
     sources = n // 6
-    dsl, half = own_ref.shape[1:]
+    half = own_ref.shape[2]
+    main, first, _ = layout(dsl)
+    full = main // LANES
 
     def copy(k):
         i, q = divmod(k, 6)
@@ -130,9 +170,18 @@
             sems.at[k],
         )
 
-    for k in range(n):
+    weights = [
+        pltpu.make_async_copy(own_hbm, own_ref, sems.at[n]),
+        pltpu.make_async_copy(other_hbm, other_ref, sems.at[n + 1]),
+    ]
+    away = []
+    step = 256 // cap
+    for k in range(6 * step):
         copy(k).start()
-    step = 256 // cap
+    for c in weights:
+        c.start()
+    for k in range(6 * step, n):
+        copy(k).start()
     for lo in range(0, sources, step):
         for k in range(6 * lo, 6 * (lo + step)):
             copy(k).wait()
@@ -150,43 +199,69 @@
             gup = (down * active).astype(BF)
             for j, a in enumerate((ggp, gup, hid)):
                 acts_ref[at, (3 * h + j) * half : (3 * h + j + 1) * half] = a
+            if lo == 0:
+                weights[h].wait()
             part = dot_nt(hid, w_ref[2])
             out = part if out is None else out + part
             part = dot_nt(ggp, w_ref[0]) + dot_nt(gup, w_ref[1])
             back = part if back is None else back + part
-        ret_ref[lo : lo + step, :cap, :] = out.astype(BF).reshape(step, cap, dsl)
-        ret_ref[lo : lo + step, cap:, :] = back.astype(BF).reshape(step, cap, dsl)
-
-
-def grad_of(cap, rows_ref, acts_ref, j):
-    sources, _, dsl = rows_ref.shape
+        hi = lo + step
+        for t in range(full):
+            lanes = slice(t * LANES, (t + 1) * LANES)
+            put_tile(ret_ref, lo, hi, cap, t, back[:, lanes].astype(BF))
+            put_tile(ret_ref, lo, hi, cap, full + t, out[:, lanes].astype(BF))
+        last = back[:, main:] + out[:, main:]
+        put_tile(ret_ref, lo, hi, cap, 2 * full, last.astype(BF))
+        blocks = pl.ds(lo, step)
+        away.append(
+            pltpu.make_async_copy(
+                ret_ref.at[blocks], ret_hbm.at[blocks], sems.at[n + 2 + len(away)]
+            )
+        )
+        away[-1].start()
+    for c in away:
+        c.wait()
+
+
+def grad_of(dsl, cap, rows_ref, acts_ref, j):
+    sources = rows_ref.shape[0]
     half = acts_ref.shape[1] // 3
-    first = cap if j == 2 else 0
-    left = rows_ref[:, first : first + cap, :].reshape(sources * cap, dsl)
-    return dot_tn(left, acts_ref[:, j * half : (j + 1) * half])
-
-
-def other_grads_kernel(cap, rows_ref, acts_ref, out_ref):
+    main, first, second = layout(dsl)
+    left = tiles(rows_ref, 0, sources, cap, second if j == 2 else first)
+    grad = dot_tn(left, acts_ref[:, j * half : (j + 1) * half])
+    if j == 2:
+        return jnp.concatenate([grad[:main], grad[dsl:]], axis=0)
+    return grad[:dsl]
+
+
+def other_grads_kernel(dsl, cap, rows_ref, acts_ref, out_ref):
     for j in range(3):
-        out_ref[j] = grad_of(cap, rows_ref, acts_ref, j).astype(BF)
-
-
-def own_grads_kernel(cap, rows_ref, acts_ref, theirs_ref, *outs):
+        out_ref[j] = grad_of(dsl, cap, rows_ref, acts_ref, j).astype(BF)
+
+
+def own_grads_kernel(dsl, cap, rows_ref, acts_ref, theirs_ref, *outs):
     for j in range(3):
-        part = grad_of(cap, rows_ref, acts_ref, j)
+        part = grad_of(dsl, cap, rows_ref, acts_ref, j)
         outs[j][...] = (part + theirs_ref[j].astype(F32)).astype(BF)
 
 
-def combine_kernel(experts, cap, ret_ref, routes_ref, weight_ref, out_ref, grad_ref):
+def combine_kernel(experts, cap, ret_ref, routes_ref, weight_ref, _, out_ref, grad_ref):
     dsl = out_ref.shape[0]
+    main, first, _ = layout(dsl)
+    tail = dsl - main
     picks = pickers(routes_ref[...], experts, cap)
     weight = weight_ref[...]
-    out = ret_ref[:, :cap, :].reshape(experts * cap, dsl)
-    back = ret_ref[:, cap:, :].reshape(experts * cap, dsl)
-    out_ref[...] = sum(
-        dot_tn(out, picks[k]) * weight[k : k + 1, :] for k in range(2)
-    ).astype(BF)
-    grad_ref[...] = dot_tn(back, picks[0] + picks[1]).astype(BF)
+    rows = tiles(ret_ref, 0, experts, cap, range(2 * len(first) - 1))
+    out = back = None
+    for k, pick in enumerate(picks):
+        got = dot_tn(rows, pick)
+        b = jnp.concatenate([got[:main], got[2 * main : 2 * main + tail]], axis=0)
+        o = jnp.concatenate([got[main : 2 * main], got[2 * main + tail :]], axis=0)
+        o = o * weight[k : k + 1, :]
+        out = o if out is None else out + o
+        back = b if back is None else back + b
+    out_ref[...] = out.astype(BF)
+    grad_ref[...] = back.astype(BF)
 
 
 def per_device(tokens, routes, route_weight, w_gate, w_up, w_down, cotangent):
@@ -211,19 +286,22 @@
         return lax.all_to_all(a, "expert", 0, 0, axis_index_groups=cores, tiled=True)
 
     routes_t, weight_t = routes.T, route_weight.T
-    block = shape((experts, 2 * cap, dsl), BF)
+    main, first, _ = layout(dsl)
+    block = shape((experts, (2 * len(first) - 1) * cap, LANES), BF)
+    padded = (3, main + LANES, half)
     stack = shape((3, dsl, half), BF)
     send, w_own = pl.pallas_call(
         functools.partial(send_kernel, experts, cap),
-        out_shape=[block, stack],
+        out_shape=[block, pltpu.HBM(padded, BF)],
         in_specs=[hbm] * 7,
-        out_specs=[vmem, pl.BlockSpec(memory_space=pl.ANY)],
+        out_specs=[vmem, hbm],
         scratch_shapes=[
             pltpu.VMEM((dsl, ntok), BF),
             pltpu.VMEM((dsl, ntok), BF),
             pltpu.VMEM((top, ntok), jnp.int32),
             pltpu.VMEM((top, ntok), F32),
-            pltpu.SemaphoreType.DMA((7,)),
+            pltpu.VMEM((dsl - main, half), BF),
+            pltpu.SemaphoreType.DMA((11,)),
         ],
         compiler_params=params(),
         cost_estimate=cost(4 * rows * ntok * dsl, 2 * rows * dsl * 4),
@@ -240,7 +318,7 @@
 
     n = 6 * experts
     pieces = pl.pallas_call(
-        functools.partial(terms_kernel, cap),
+        functools.partial(terms_kernel, dsl, cap),
         out_shape=[pltpu.HBM((cap, half), BF)] * n,
         in_specs=[vmem] * 3,
         out_specs=[hbm] * n,
@@ -253,17 +331,20 @@
     )(got, w_own, w_other)
     sums = [in_hbm(a) for a in lax.psum(list(pieces), "dp")]
     acts, ret = pl.pallas_call(
-        functools.partial(back_kernel, cap, n),
-        out_shape=[shape((rows, 6 * half), BF), block],
-        in_specs=[hbm] * n + [vmem] * 2,
-        out_specs=[vmem] * 2,
+        functools.partial(back_kernel, dsl, cap, n),
+        out_shape=[shape((rows, 6 * half), BF), pltpu.HBM(block.shape, BF)],
+        in_specs=[hbm] * (n + 2),
+        out_specs=[vmem, hbm],
         scratch_shapes=[
             pltpu.VMEM((rows, 6 * half), BF),
-            pltpu.SemaphoreType.DMA((n,)),
+            pltpu.VMEM(padded, BF),
+            pltpu.VMEM(padded, BF),
+            pltpu.VMEM(block.shape, BF),
+            pltpu.SemaphoreType.DMA((n + 2 + rows // 256,)),
         ],
         compiler_params=params(),
         cost_estimate=cost(6 * flops, 2 * rows * (dsl * 2 + 12 * half)),
-    )(*sums, w_own, w_other)
+    )(*sums, in_hbm(w_own), in_hbm(w_other))
     ret = exchange(ret)
 
     whole = [
@@ -272,7 +353,7 @@
     ]
     half_cost = cost(3 * flops, 2 * rows * (dsl * 2 + 3 * half))
     for_other = pl.pallas_call(
-        functools.partial(other_grads_kernel, cap),
+        functools.partial(other_grads_kernel, dsl, cap),
         grid=(1,),
         out_shape=stack,
         in_specs=whole,
@@ -283,7 +364,7 @@
     theirs = lax.ppermute(for_other, "expert", swap)
     whole[1] = pl.BlockSpec((rows, 3 * half), lambda i: (0, 0))
     grad_gate, grad_up, grad_down_t = pl.pallas_call(
-        functools.partial(own_grads_kernel, cap),
+        functools.partial(own_grads_kernel, dsl, cap),
         grid=(1,),
         out_shape=[shape((dsl, half), BF)] * 3,
         in_specs=whole + [pl.BlockSpec(stack.shape, lambda i: (0, 0, 0))],
@@ -294,9 +375,11 @@
     output_t, grad_tokens_t = pl.pallas_call(
         functools.partial(combine_kernel, experts, cap),
         out_shape=[shape((dsl, ntok), BF)] * 2,
+        in_specs=[vmem] * 3 + [hbm],
+        out_specs=[vmem] * 2,
         compiler_params=params(),
         cost_estimate=cost(6 * rows * ntok * dsl, 2 * rows * dsl * 4),
-    )(ret, routes_t, weight_t)
+    )(ret, routes_t, weight_t, in_hbm(grad_gate))
     return output_t.T, grad_tokens_t.T, grad_gate, grad_up, grad_down_t.T
 
 

time: 153 us -> 196 us (1.28)
  Pallas kernels: 13.6 us -> 60.9 us
  blocking collectives: 117 us -> 95.7 us
  waiting for transfers between devices: 0.01 us -> 12.6 us
  starting transfers between devices: 20.2 us -> 24.1 us
    pallas_call x1, Pallas kernels: 1.74 us -> 42.9 us  [per_device(): pl.pallas_call(functools.partial(send_kernel, experts, cap), out_shape=[b...]
    all_to_all x2 -> x1, blocking collectives: 39.6 us -> 18.3 us  [exchange(): lax.all_to_all(a, 'expert', 0, 0, axis_index_groups=cores, tiled=True)]
    all_to_all x0 -> x1, waiting for transfers between devices: none -> 12.6 us  [exchange(): lax.all_to_all(a, 'expert', 0, 0, axis_index_groups=cores, tiled=True)]
    pallas_call x4, Pallas kernels: 10.6 us -> 15.3 us  [the longest x1 6.62 us: per_device(): pl.pallas_call(functools.partial(back_kernel, dsl, cap, n), out_shape=[sh...]
    all_to_all x0 -> x1, starting transfers between devices: none -> 4.32 us  [exchange(): lax.all_to_all(a, 'expert', 0, 0, axis_index_groups=cores, tiled=True)]
  transfers between devices with their start and end apart: 2 -> 3, of which waited for: 0 -> 1; matrix products, arithmetic and copies ran while one was open for 0% -> 0% of each run, Pallas kernels for 1% -> 2%
where the time goes in v3:
time: 196 us; the launch traced here: 195 us
  blocking collectives  95.7 us (49%)
  Pallas kernels  60.9 us (31%)
  starting transfers between devices  24.1 us (12%)
  waiting for transfers between devices  12.6 us (6%)
    psum x1, blocking collectives, per_device(): sums = [in_hbm(a) for a in lax.psum(list(pieces), 'dp')]  77.4 us
    pallas_call x1, Pallas kernels, per_device(): pl.pallas_call(functools.partial(send_kernel, experts, cap), out_shape=[b...  42.9 us
    all_to_all x1, blocking collectives, exchange(): lax.all_to_all(a, 'expert', 0, 0, axis_index_groups=cores, tiled=True)  18.3 us
    all_to_all x1, waiting for transfers between devices, exchange(): lax.all_to_all(a, 'expert', 0, 0, axis_index_groups=cores, tiled=True)  12.6 us
    ppermute x1, starting transfers between devices, per_device(): theirs = lax.ppermute(for_other, 'expert', swap)  10.9 us
    ppermute x1, starting transfers between devices, per_device(): w_other = lax.ppermute(w_own, 'expert', swap)  8.92 us
    pallas_call x1, Pallas kernels, per_device(): pl.pallas_call(functools.partial(back_kernel, dsl, cap, n), out_shape=[sh...  6.62 us
    all_to_all x1, starting transfers between devices, exchange(): lax.all_to_all(a, 'expert', 0, 0, axis_index_groups=cores, tiled=True)  4.32 us
  transfers between devices with their start and end apart: 3, of which 1 were waited for; matrix products, arithmetic and copies ran while one was open for 0% of the time, Pallas kernels for 2%

profile of v3, /device:TPU:1, one launch (start us, length us, event | category | flops | bytes accessed | tf_op | source)
XLA Modules:
  0.0 195.2 jit_solution(3869297560341416760)
XLA Ops:
  0.6 42.9 %shard_map.110 = (bf16[16,224,128]{2,1,0:T(8,128)(2,1)S(1)}, bf16[3,512,512]{2,1,0:T(8,128)(2,1)}) custom-call(bf16[448,128]{1,0:T(8,128)(2,1)} %bitcast.13, bf16[448,128]{1,0:T(8,128)(2,1)} %bitcast.14, s32[2,128]{1,0:T(2,128)} %bitcast.8, f32[2,128]{1,0:T(2,128)} %bitcast.10, bf16[448,512]{1,0:T(8,128)(2,1)} %wg_hbm.1, bf16[448,512]{1,0:T(8,128)(2,1)} %wu_hbm.1, ...), custom_call_target="tpu_custom_call" | custom-call | flops 117440512 | bytes 1835008 | tf_op jit(solution)/shard_map/pallas_call | solution.py:293
  43.5 0.0 copy-start.3
  43.6 8.9 %collective-permute-start = (bf16[3,512,512]{2,1,0:T(8,128)(2,1)}, bf16[3,512,512]{2,1,0:T(8,128)(2,1)S(1)}, u32[]{:S(2)}, u32[]{:S(2)}) collective-permute-start(bf16[3,512,512]{2,1,0:T(8,128)(2,1)} %get-tuple-element.111.own_ref.refs_96_), channel_id=1, source_target_pairs={{0,16},{16,0},{32,48},{48,32},{64,80},{80,64},{96,112},{112,96},{1... | collective-permute-start | bytes 4718600 | tf_op jit(solution)/shard_map/ppermute | solution.py:317
  52.5 18.3 %all_to_all.10.rows_ref = bf16[16,224,128]{2,1,0:T(8,128)(2,1)S(1)} all-to-all(bf16[16,224,128]{2,1,0:T(8,128)(2,1)S(1)} %get-tuple-element.110), channel_id=1, replica_groups={{0,32,64,96,128,160,192,224,256,288,320,352,384,416,448,480},{16,48,80,..., dimensions={0} | all-to-all | bytes 1835008 | tf_op jit(solution)/shard_map/all_to_all | solution.py:286
  70.7 0.0 collective-permute-done.other_ref.refs_97_
  70.8 0.0 copy-done.3
  70.8 0.0 copy-start.4
  70.8 3.4 %shard_map.111 = (bf16[32,512]{1,0:T(8,128)(2,1)}, bf16[32,512]{1,0:T(8,128)(2,1)}, bf16[32,512]{1,0:T(8,128)(2,1)}, bf16[32,512]{1,0:T(8,128)(2,1)}, bf16[32,51...) custom-call(bf16[16,224,128]{2,1,0:T(8,128)(2,1)S(1)} %all_to_all.10, ...), custom_call_target="tpu_custom_call" | custom-call | flops 1409286144 | bytes 4063232 | tf_op jit(solution)/shard_map/pallas_call | solution.py:320
  74.2 0.0 copy-done
  74.2 0.0 copy-done.4
  74.2 77.4 %all-reduce.2 = (bf16[32,512]{1,0:T(8,128)(2,1)}, bf16[32,512]{1,0:T(8,128)(2,1)}, bf16[32,512]{1,0:T(8,128)(2,1)}, bf16[32,512]{1,0:T(8,128)(2,1)}, bf16[32,512...) all-reduce(bf16[32,512]{1,0:T(8,128)(2,1)} %get-tuple-element.112, ...), channel_id=1, replica_groups=mesh['expert'=32,'dp'=16] {'dp'}, use_global_device_ids=true, to_apply=%region_0.0 | all-reduce | flops 1572864 | bytes 6291456 | tf_op jit(solution)/shard_map/psum | solution.py:332
  151.6 6.6 %shard_map.112 = (bf16[512,3072]{1,0:T(8,128)(2,1)S(1)}, bf16[16,224,128]{2,1,0:T(8,128)(2,1)}) custom-call(bf16[32,512]{1,0:T(8,128)(2,1)} %get-tuple-element.215.refs_0_, bf16[32,512]{1,0:T(8,128)(2,1)} %get-tuple-element.216.refs_1_, bf16[32,512]{1,0:T(8,128)(2,1)} %get-tuple-element.217.refs_2_, bf16[32,512]{1,0:T(8,128)(2,1)} %get-tuple-element.218.refs_3_, ...), custom_call_target="tpu_custom_call" | custom-call | flops 1409286144 | bytes 7208960 | tf_op jit(solution)/shard_map/pallas_call | solution.py:333
  158.3 0.0 copy-done.1
  158.3 2.1 %shard_map.113 = bf16[3,448,512]{2,1,0:T(8,128)(2,1)} custom-call(bf16[16,224,128]{2,1,0:T(8,128)(2,1)S(1)} %copy-done.1, bf16[512,3072]{1,0:T(8,128)(2,1)S(1)} %get-tuple-element.209.acts_ref), custom_call_target="tpu_custom_call" | custom-call | flops 704643072 | bytes 2490368 | tf_op jit(solution)/shard_map/pallas_call | solution.py:355
  160.4 10.9 %collective-permute-start.1 = (bf16[3,448,512]{2,1,0:T(8,128)(2,1)}, bf16[3,448,512]{2,1,0:T(8,128)(2,1)}, u32[]{:S(2)}, u32[]{:S(2)}) collective-permute-start(bf16[3,448,512]{2,1,0:T(8,128)(2,1)} %shard_map.113), channel_id=1, source_target_pairs={{0,16},{16,0},{32,48},{48,32},{64,80},{80,64},{96,112},{112,96},{1... | collective-permute-start | bytes 4128776 | tf_op jit(solution)/shard_map/ppermute | solution.py:364
  171.2 4.3 %all-to-all-start.1 = ((bf16[16,224,128]{2,1,0:T(8,128)(2,1)}), bf16[16,224,128]{2,1,0:T(8,128)(2,1)}, u32[]{:S(2)}, u32[]{:S(2)}) async-start(bf16[16,224,128]{2,1,0:T(8,128)(2,1)} %get-tuple-element.208), calls=%async_computation.1 | async-start | bytes 1835008 | tf_op jit(solution)/shard_map/all_to_all | solution.py:286
  175.6 0.0 collective-permute-done.1.theirs_ref
  175.6 0.0 copy-start.2
  175.6 1.2 copy-done.2
  176.8 3.2 %shard_map.114 = (bf16[448,512]{1,0:T(8,128)(2,1)}, bf16[448,512]{1,0:T(8,128)(2,1)}, bf16[448,512]{1,0:T(8,128)(2,1)}) custom-call(bf16[16,224,128]{2,1,0:T(8,128)(2,1)S(1)} %copy-done.2, bf16[512,3072]{1,0:T(8,128)(2,1)S(1)} %get-tuple-element.209.acts_ref, bf16[3,448,512]{2,1,0:T(8,128)(2,1)} %collective-permute-done.1.theirs_ref), custom_call_target="tpu_custom_call" | custom-call | flops 704643072 | bytes 2490368 | tf_op jit(solution)/shard_map/pallas_call | solution.py:366
  180.0 12.6 %all-to-all-done.1.ret_ref = bf16[16,224,128]{2,1,0:T(8,128)(2,1)} async-done(((bf16[16,224,128]{2,1,0:T(8,128)(2,1)}), bf16[16,224,128]{2,1,0:T(8,128)(2,1)}, u32[]{:S(2)}, u32[]{:S(2)}) %all-to-all-start.1) | async-done | bytes 917536 | tf_op jit(solution)/shard_map/all_to_all | solution.py:286
  192.6 0.0 copy-done.5
  192.6 0.0 copy-done.6
  192.6 2.6 %shard_map.115 = (bf16[448,128]{1,0:T(8,128)(2,1)}, bf16[448,128]{1,0:T(8,128)(2,1)}) custom-call(bf16[16,224,128]{2,1,0:T(8,128)(2,1)} %all-to-all-done.1.ret_ref, s32[2,128]{1,0:T(2,128)S(1)} %bitcast.9, f32[2,128]{1,0:T(2,128)S(1)} %bitcast.11, bf16[448,512]{1,0:T(8,128)(2,1)} %get-tuple-element.107._), custom_call_target="tpu_custom_call" | custom-call | flops 176160768 | bytes 1835008 | tf_op jit(solution)/shard_map/pallas_call | solution.py:375
  (4 shorter events, 0.0 us)
Async XLA Ops:
  43.5 27.2 %copy-start.3 = (bf16[3,512,512]{2,1,0:T(8,128)(2,1)S(1)}, bf16[3,512,512]{2,1,0:T(8,128)(2,1)}, u32[]{:S(2)}) copy-start(bf16[3,512,512]{2,1,0:T(8,128)(2,1)} %get-tuple-element.111.own_ref.refs_96_) | copy-start | bytes 4718596
  43.6 27.2 %collective-permute-start = (bf16[3,512,512]{2,1,0:T(8,128)(2,1)}, bf16[3,512,512]{2,1,0:T(8,128)(2,1)S(1)}, u32[]{:S(2)}, u32[]{:S(2)}) collective-permute-start(bf16[3,512,512]{2,1,0:T(8,128)(2,1)} %get-tuple-element.111.own_ref.refs_96_), channel_id=1, source_target_pairs={{0,16},{16,0},{32,48},{48,32},{64,80},{80,64},{96,112},{112,96},{1... | collective-permute-start | bytes 4718600 | tf_op jit(solution)/shard_map/ppermute | solution.py:317
  70.7 3.4 %copy-start = (bf16[16,224,128]{2,1,0:T(8,128)(2,1)}, bf16[16,224,128]{2,1,0:T(8,128)(2,1)S(1)}, u32[]{:S(2)}) copy-start(bf16[16,224,128]{2,1,0:T(8,128)(2,1)S(1)} %all_to_all.10.rows_ref) | copy-start | bytes 2752516
  70.8 3.4 %copy-start.4 = (bf16[3,512,512]{2,1,0:T(8,128)(2,1)}, bf16[3,512,512]{2,1,0:T(8,128)(2,1)S(1)}, u32[]{:S(2)}) copy-start(bf16[3,512,512]{2,1,0:T(8,128)(2,1)S(1)} %collective-permute-done.other_ref.refs_97_) | copy-start | bytes 4718596
  151.6 6.6 %copy-start.1 = (bf16[16,224,128]{2,1,0:T(8,128)(2,1)S(1)}, bf16[16,224,128]{2,1,0:T(8,128)(2,1)}, u32[]{:S(2)}) copy-start(bf16[16,224,128]{2,1,0:T(8,128)(2,1)} %copy-done) | copy-start | bytes 2752516
  160.4 15.2 %collective-permute-start.1 = (bf16[3,448,512]{2,1,0:T(8,128)(2,1)}, bf16[3,448,512]{2,1,0:T(8,128)(2,1)}, u32[]{:S(2)}, u32[]{:S(2)}) collective-permute-start(bf16[3,448,512]{2,1,0:T(8,128)(2,1)} %shard_map.113), channel_id=1, source_target_pairs={{0,16},{16,0},{32,48},{48,32},{64,80},{80,64},{96,112},{112,96},{1... | collective-permute-start | bytes 4128776 | tf_op jit(solution)/shard_map/ppermute | solution.py:364
  171.2 21.3 %all-to-all-start.1 = ((bf16[16,224,128]{2,1,0:T(8,128)(2,1)}), bf16[16,224,128]{2,1,0:T(8,128)(2,1)}, u32[]{:S(2)}, u32[]{:S(2)}) async-start(bf16[16,224,128]{2,1,0:T(8,128)(2,1)} %get-tuple-element.208), calls=%async_computation.1 | async-start | bytes 1835008 | tf_op jit(solution)/shard_map/all_to_all | solution.py:286
  175.6 1.2 copy-start.2
  176.8 15.8 %copy-start.5 = (s32[128,2]{0,1:T(2,128)S(1)}, s32[128,2]{0,1:T(2,128)}, u32[]{:S(2)}) copy-start(s32[128,2]{0,1:T(2,128)} %param.8) | copy-start | bytes 3076
  176.8 15.8 %copy-start.6 = (f32[128,2]{0,1:T(2,128)S(1)}, f32[128,2]{0,1:T(2,128)}, u32[]{:S(2)}) copy-start(f32[128,2]{0,1:T(2,128)} %param.9) | copy-start | bytes 3076

commit v4 on v2

--- a/solution.py
+++ b/solution.py
@@ -118,9 +118,14 @@
 
 
 def back_kernel(cap, n, *refs):
-    pieces, (own_ref, other_ref, acts_ref, ret_ref, held, sems) = refs[:n], refs[n:]
+    pieces = refs[:n]
+    own_hbm, other_ref, acts_ref, ret_ref, held, own_ref, sems = refs[n:]
     sources = n // 6
     dsl, half = own_ref.shape[1:]
+    weights = [
+        pltpu.make_async_copy(own_hbm.at[j], own_ref.at[j], sems.at[n + j])
+        for j in range(3)
+    ]
 
     def copy(k):
         i, q = divmod(k, 6)
@@ -130,15 +135,19 @@
             sems.at[k],
         )
 
-    for k in range(n):
+    step = 256 // cap
+    for k in range(6 * step):
         copy(k).start()
-    step = 256 // cap
+    for c in weights:
+        c.start()
+    for k in range(6 * step, n):
+        copy(k).start()
     for lo in range(0, sources, step):
         for k in range(6 * lo, 6 * (lo + step)):
             copy(k).wait()
         at = slice(lo * cap, (lo + step) * cap)
         out = back = None
-        for h, w_ref in enumerate((own_ref, other_ref)):
+        for h, w_ref in ((1, other_ref), (0, own_ref)):
             gate, up, down = (
                 held[at, (2 * j + h) * half : (2 * j + h + 1) * half].astype(F32)
                 for j in range(3)
@@ -150,6 +159,9 @@
             gup = (down * active).astype(BF)
             for j, a in enumerate((ggp, gup, hid)):
                 acts_ref[at, (3 * h + j) * half : (3 * h + j + 1) * half] = a
+            if lo == 0 and h == 0:
+                for c in weights:
+                    c.wait()
             part = dot_nt(hid, w_ref[2])
             out = part if out is None else out + part
             part = dot_nt(ggp, w_ref[0]) + dot_nt(gup, w_ref[1])
@@ -166,15 +178,15 @@
     return dot_tn(left, acts_ref[:, j * half : (j + 1) * half])
 
 
-def other_grads_kernel(cap, rows_ref, acts_ref, out_ref):
+def grads_kernel(cap, rows_ref, acts_ref, *rest):
+    out_ref = rest[-1]
     for j in range(3):
-        out_ref[j] = grad_of(cap, rows_ref, acts_ref, j).astype(BF)
-
-
-def own_grads_kernel(cap, rows_ref, acts_ref, theirs_ref, *outs):
-    for j in range(3):
-        part = grad_of(cap, rows_ref, acts_ref, j)
-        outs[j][...] = (part + theirs_ref[j].astype(F32)).astype(BF)
+        out_ref[j] = grad_of(cap, rows_ref, acts_ref, j).astype(out_ref.dtype)
+
+
+def add_kernel(own_ref, theirs_ref, *outs):
+    for j, out_ref in enumerate(outs):
+        out_ref[...] = (own_ref[j] + theirs_ref[j].astype(F32)).astype(BF)
 
 
 def combine_kernel(experts, cap, ret_ref, routes_ref, weight_ref, out_ref, grad_ref):
@@ -255,48 +267,47 @@
     acts, ret = pl.pallas_call(
         functools.partial(back_kernel, cap, n),
         out_shape=[shape((rows, 6 * half), BF), block],
-        in_specs=[hbm] * n + [vmem] * 2,
+        in_specs=[hbm] * (n + 1) + [vmem],
         out_specs=[vmem] * 2,
         scratch_shapes=[
             pltpu.VMEM((rows, 6 * half), BF),
-            pltpu.SemaphoreType.DMA((n,)),
+            pltpu.VMEM(stack.shape, BF),
+            pltpu.SemaphoreType.DMA((n + 3,)),
         ],
         compiler_params=params(),
         cost_estimate=cost(6 * flops, 2 * rows * (dsl * 2 + 12 * half)),
-    )(*sums, w_own, w_other)
+    )(*sums, in_hbm(w_own), w_other)
     ret = exchange(ret)
 
-    whole = [
-        pl.BlockSpec(block.shape, lambda i: (0, 0, 0)),
-        pl.BlockSpec((rows, 3 * half), lambda i: (0, 1)),
-    ]
-    half_cost = cost(3 * flops, 2 * rows * (dsl * 2 + 3 * half))
-    for_other = pl.pallas_call(
-        functools.partial(other_grads_kernel, cap),
-        grid=(1,),
-        out_shape=stack,
-        in_specs=whole,
-        out_specs=pl.BlockSpec(stack.shape, lambda i: (0, 0, 0)),
-        compiler_params=params(),
-        cost_estimate=half_cost,
-    )(got, acts)
-    theirs = lax.ppermute(for_other, "expert", swap)
-    whole[1] = pl.BlockSpec((rows, 3 * half), lambda i: (0, 0))
-    grad_gate, grad_up, grad_down_t = pl.pallas_call(
-        functools.partial(own_grads_kernel, cap),
-        grid=(1,),
-        out_shape=[shape((dsl, half), BF)] * 3,
-        in_specs=whole + [pl.BlockSpec(stack.shape, lambda i: (0, 0, 0))],
-        out_specs=[pl.BlockSpec((dsl, half), lambda i: (0, 0))] * 3,
-        compiler_params=params(),
-        cost_estimate=half_cost,
-    )(got, acts, theirs)
+    def grads(part, dtype, *after):
+        return pl.pallas_call(
+            functools.partial(grads_kernel, cap),
+            grid=(1,),
+            out_shape=shape(stack.shape, dtype),
+            in_specs=[
+                pl.BlockSpec(block.shape, lambda i: (0, 0, 0)),
+                pl.BlockSpec((rows, 3 * half), lambda i: (0, part)),
+            ]
+            + [hbm] * len(after),
+            out_specs=pl.BlockSpec(stack.shape, lambda i: (0, 0, 0)),
+            compiler_params=params(),
+            cost_estimate=cost(3 * flops, 2 * rows * (dsl * 2 + 3 * half)),
+        )(got, acts, *after)
+
+    theirs = lax.ppermute(grads(1, BF, in_hbm(ret)), "expert", swap)
+    own = grads(0, F32)
     output_t, grad_tokens_t = pl.pallas_call(
         functools.partial(combine_kernel, experts, cap),
         out_shape=[shape((dsl, ntok), BF)] * 2,
         compiler_params=params(),
         cost_estimate=cost(6 * rows * ntok * dsl, 2 * rows * dsl * 4),
     )(ret, routes_t, weight_t)
+    grad_gate, grad_up, grad_down_t = pl.pallas_call(
+        add_kernel,
+        out_shape=[shape((dsl, half), BF)] * 3,
+        compiler_params=params(),
+        cost_estimate=cost(3 * dsl * half, 24 * dsl * half),
+    )(own, theirs)
     return output_t.T, grad_tokens_t.T, grad_gate, grad_up, grad_down_t.T
 
 

time: 153 us -> 150 us (0.980)
  blocking collectives: 117 us -> 112 us
  starting transfers between devices: 20.2 us -> 21.8 us
    all_to_all x2, blocking collectives: 39.6 us -> 34.9 us  [exchange(): lax.all_to_all(a, 'expert', 0, 0, axis_index_groups=cores, tiled=True)]
    ppermute x1, starting transfers between devices: 11.4 us -> 13 us  [per_device(): theirs = lax.ppermute(grads(1, BF, in_hbm(ret)), 'expert', swap)]
    pallas_call x2 -> x3, Pallas kernels: 2.65 us -> 3.07 us  [the longest x2 1.82 us: grads(): pl.pallas_call(functools.partial(grads_kernel, cap), grid=(1,), out_shape...]
  transfers between devices with their start and end apart: 2 -> 2, of which waited for: 0 -> 1; matrix products, arithmetic and copies ran while one was open for 0% -> 0% of each run, Pallas kernels for 1% -> 1%
where the time goes in v4:
time: 150 us
  blocking collectives  112 us (75%)
  starting transfers between devices  21.8 us (15%)
  Pallas kernels  14.8 us (10%)
    psum x1, blocking collectives, per_device(): sums = [in_hbm(a) for a in lax.psum(list(pieces), 'dp')]  77.3 us
    all_to_all x2, blocking collectives, exchange(): lax.all_to_all(a, 'expert', 0, 0, axis_index_groups=cores, tiled=True)  34.9 us
    ppermute x1, starting transfers between devices, per_device(): theirs = lax.ppermute(grads(1, BF, in_hbm(ret)), 'expert', swap)  13 us
    ppermute x1, starting transfers between devices, per_device(): w_other = lax.ppermute(w_own, 'expert', swap)  8.79 us
    pallas_call x1, Pallas kernels, per_device(): pl.pallas_call(functools.partial(back_kernel, cap, n), out_shape=[shape((...  5.31 us
    pallas_call x1, Pallas kernels, per_device(): pl.pallas_call(functools.partial(terms_kernel, cap), out_shape=[pltpu.HBM...  3.32 us
  transfers between devices with their start and end apart: 2, of which 1 were waited for; matrix products, arithmetic and copies ran while one was open for 0% of the time, Pallas kernels for 1%

profile of v4, /device:TPU:1, one launch (start us, length us, event | category | flops | bytes accessed | tf_op | source)
XLA Modules:
  0.0 149.9 jit_solution(8371400573997784260)
XLA Ops:
  0.6 1.7 %shard_map.110 = (bf16[16,64,448]{2,1,0:T(8,128)(2,1)S(1)}, bf16[3,448,512]{2,1,0:T(8,128)(2,1)S(1)}) custom-call(bf16[448,128]{1,0:T(8,128)(2,1)} %bitcast.13, bf16[448,128]{1,0:T(8,128)(2,1)} %bitcast.14, s32[2,128]{1,0:T(2,128)} %bitcast.8, f32[2,128]{1,0:T(2,128)} %bitcast.10, bf16[448,512]{1,0:T(8,128)(2,1)} %wg_hbm.1, bf16[448,512]{1,0:T(8,128)(2,1)} %wu_hbm.1, ...), custom_call_target="tpu_custom_call" | custom-call | flops 117440512 | bytes 1835008 | tf_op jit(solution)/shard_map/pallas_call | solution.py:228
  2.4 0.0 copy-start.1
  2.4 8.8 %collective-permute-start = (bf16[3,448,512]{2,1,0:T(8,128)(2,1)S(1)}, bf16[3,448,512]{2,1,0:T(8,128)(2,1)S(1)}, u32[]{:S(2)}, u32[]{:S(2)}) collective-permute-start(bf16[3,448,512]{2,1,0:T(8,128)(2,1)S(1)} %get-tuple-element.111.own_ref.refs_96_), channel_id=1, source_target_pairs={{0,16},{16,0},{32,48},{48,32},{64,80},{80,64},{96,112},{112,96},{1... | collective-permute-start | bytes 4128776 | tf_op jit(solution)/shard_map/ppermute | solution.py:251
  11.2 19.7 %all_to_all.10.rows_ref = bf16[16,64,448]{2,1,0:T(8,128)(2,1)S(1)} all-to-all(bf16[16,64,448]{2,1,0:T(8,128)(2,1)S(1)} %get-tuple-element.110), channel_id=1, replica_groups={{0,32,64,96,128,160,192,224,256,288,320,352,384,416,448,480},{16,48,80,..., dimensions={0} | all-to-all | bytes 1835008 | tf_op jit(solution)/shard_map/all_to_all | solution.py:223
  30.9 0.0 collective-permute-done.other_ref.refs_97_
  30.9 3.3 %shard_map.111 = (bf16[32,512]{1,0:T(8,128)(2,1)}, bf16[32,512]{1,0:T(8,128)(2,1)}, bf16[32,512]{1,0:T(8,128)(2,1)}, bf16[32,512]{1,0:T(8,128)(2,1)}, bf16[32,51...) custom-call(bf16[16,64,448]{2,1,0:T(8,128)(2,1)S(1)} %all_to_all.10., ...), custom_call_target="tpu_custom_call" | custom-call | flops 1409286144 | bytes 4063232 | tf_op jit(solution)/shard_map/pallas_call | solution.py:254
  34.2 0.0 copy-done.1
  34.2 0.0 copy-done.2
  34.2 0.0 copy-start.3
  34.2 77.3 %all-reduce.2 = (bf16[32,512]{1,0:T(8,128)(2,1)}, bf16[32,512]{1,0:T(8,128)(2,1)}, bf16[32,512]{1,0:T(8,128)(2,1)}, bf16[32,512]{1,0:T(8,128)(2,1)}, bf16[32,512...) all-reduce(bf16[32,512]{1,0:T(8,128)(2,1)} %get-tuple-element.112, ...), channel_id=1, replica_groups=mesh['expert'=32,'dp'=16] {'dp'}, use_global_device_ids=true, to_apply=%region_0.0 | all-reduce | flops 1572864 | bytes 6291456 | tf_op jit(solution)/shard_map/psum | solution.py:266
  111.5 0.0 copy-done.3
  111.5 5.3 %shard_map.112 = (bf16[512,3072]{1,0:T(8,128)(2,1)S(1)}, bf16[16,64,448]{2,1,0:T(8,128)(2,1)S(1)}) custom-call(bf16[32,512]{1,0:T(8,128)(2,1)} %get-tuple-element.215.refs_0_, bf16[32,512]{1,0:T(8,128)(2,1)} %get-tuple-element.216.refs_1_, bf16[32,512]{1,0:T(8,128)(2,1)} %get-tuple-element.217.refs_2_, bf16[32,512]{1,0:T(8,128)(2,1)} %get-tuple-element.218.refs_3_, ...), custom_call_target="tpu_custom_call" | custom-call | flops 1409286144 | bytes 7208960 | tf_op jit(solution)/shard_map/pallas_call | solution.py:267
  116.8 15.2 %all_to_all.11.ret_ref.rest_0_ = bf16[16,64,448]{2,1,0:T(8,128)(2,1)} all-to-all(bf16[16,64,448]{2,1,0:T(8,128)(2,1)S(1)} %get-tuple-element.208), channel_id=1, replica_groups={{0,32,64,96,128,160,192,224,256,288,320,352,384,416,448,480},{16,48,80,..., dimensions={0} | all-to-all | bytes 1835008 | tf_op jit(solution)/shard_map/all_to_all | solution.py:223
  132.0 0.9 shard_map.115
  132.9 0.0 copy-start
  132.9 0.0 copy-start.4
  133.0 0.0 copy-start.5
  133.0 13.0 %collective-permute-start.1 = (bf16[3,448,512]{2,1,0:T(8,128)(2,1)S(1)}, bf16[3,448,512]{2,1,0:T(8,128)(2,1)S(1)}, u32[]{:S(2)}, u32[]{:S(2)}) collective-permute-start(bf16[3,448,512]{2,1,0:T(8,128)(2,1)S(1)} %shard_map.115), channel_id=1, source_target_pairs={{0,16},{16,0},{32,48},{48,32},{64,80},{80,64},{96,112},{112,96},{1... | collective-permute-start | bytes 4128776 | tf_op jit(solution)/shard_map/ppermute | solution.py:297
  145.9 0.9 shard_map.114.own_ref
  146.9 0.0 copy-done
  146.9 0.0 copy-done.4
  146.9 1.3 shard_map.113
  148.2 0.5 collective-permute-done.1.theirs_ref
  148.7 1.2 shard_map.116
  (2 shorter events, 0.0 us)
Async XLA Ops:
  2.4 31.8 %copy-start.1 = (bf16[3,448,512]{2,1,0:T(8,128)(2,1)}, bf16[3,448,512]{2,1,0:T(8,128)(2,1)S(1)}, u32[]{:S(2)}) copy-start(bf16[3,448,512]{2,1,0:T(8,128)(2,1)S(1)} %get-tuple-element.111.own_ref.refs_96_) | copy-start | bytes 4128772
  2.4 28.5 %collective-permute-start = (bf16[3,448,512]{2,1,0:T(8,128)(2,1)S(1)}, bf16[3,448,512]{2,1,0:T(8,128)(2,1)S(1)}, u32[]{:S(2)}, u32[]{:S(2)}) collective-permute-start(bf16[3,448,512]{2,1,0:T(8,128)(2,1)S(1)} %get-tuple-element.111.own_ref.refs_96_), channel_id=1, source_target_pairs={{0,16},{16,0},{32,48},{48,32},{64,80},{80,64},{96,112},{112,96},{1... | collective-permute-start | bytes 4128776 | tf_op jit(solution)/shard_map/ppermute | solution.py:251
  30.9 3.3 %copy-start.2 = (bf16[3,448,512]{2,1,0:T(8,128)(2,1)}, bf16[3,448,512]{2,1,0:T(8,128)(2,1)S(1)}, u32[]{:S(2)}) copy-start(bf16[3,448,512]{2,1,0:T(8,128)(2,1)S(1)} %collective-permute-done.other_ref.refs_97_) | copy-start | bytes 4128772
  34.2 77.3 %copy-start.3 = (bf16[3,448,512]{2,1,0:T(8,128)(2,1)S(1)}, bf16[3,448,512]{2,1,0:T(8,128)(2,1)}, u32[]{:S(2)}) copy-start(bf16[3,448,512]{2,1,0:T(8,128)(2,1)} %copy-done.2) | copy-start | bytes 4128772
  132.9 13.9 %copy-start = (bf16[16,64,448]{2,1,0:T(8,128)(2,1)S(1)}, bf16[16,64,448]{2,1,0:T(8,128)(2,1)}, u32[]{:S(2)}) copy-start(bf16[16,64,448]{2,1,0:T(8,128)(2,1)} %all_to_all.11.ret_ref.rest_0_) | copy-start | bytes 2752516
  132.9 13.9 %copy-start.4 = (s32[128,2]{0,1:T(2,128)S(1)}, s32[128,2]{0,1:T(2,128)}, u32[]{:S(2)}) copy-start(s32[128,2]{0,1:T(2,128)} %param.8) | copy-start | bytes 3076
  133.0 13.9 %copy-start.5 = (f32[128,2]{0,1:T(2,128)S(1)}, f32[128,2]{0,1:T(2,128)}, u32[]{:S(2)}) copy-start(f32[128,2]{0,1:T(2,128)} %param.9) | copy-start | bytes 3076
  133.0 15.7 %collective-permute-start.1 = (bf16[3,448,512]{2,1,0:T(8,128)(2,1)S(1)}, bf16[3,448,512]{2,1,0:T(8,128)(2,1)S(1)}, u32[]{:S(2)}, u32[]{:S(2)}) collective-permute-start(bf16[3,448,512]{2,1,0:T(8,128)(2,1)S(1)} %shard_map.115), channel_id=1, source_target_pairs={{0,16},{16,0},{32,48},{48,32},{64,80},{80,64},{96,112},{112,96},{1... | collective-permute-start | bytes 4128776 | tf_op jit(solution)/shard_map/ppermute | solution.py:297

commit v5 on v3

--- a/solution.py
+++ b/solution.py
@@ -153,74 +153,63 @@
 
 
 def back_kernel(dsl, cap, n, *refs):
-    pieces, (own_hbm, other_hbm, acts_ref, ret_hbm, held, own_ref, other_ref, ret_ref, sems) = (
-        refs[:n],
-        refs[n:],
-    )
+    pieces = refs[:n]
+    own_ref, other_hbm, acts_ref, ret_ref, held, other_ref, sems = refs[n:]
     sources = n // 6
+    weights = [
+        pltpu.make_async_copy(other_hbm.at[j], other_ref.at[j], sems.at[n + j])
+        for j in range(3)
+    ]
     half = own_ref.shape[2]
-    main, first, _ = layout(dsl)
+    main, _, _ = layout(dsl)
     full = main // LANES
-
-    def copy(k):
-        i, q = divmod(k, 6)
-        return pltpu.make_async_copy(
-            pieces[k],
-            held.at[pl.ds(i * cap, cap), pl.ds(q * half, half)],
-            sems.at[k],
+    step = 256 // cap
+
+    def copies(lo, h):
+        for i in range(lo, lo + step):
+            for q in range(h, 6, 2):
+                k = 6 * i + q
+                yield pltpu.make_async_copy(pieces[k], held.at[q, i], sems.at[k])
+
+    order = [(lo, h) for lo in range(0, sources, step) for h in range(2)]
+    for lo, h in order:
+        for c in copies(lo, h):
+            c.start()
+        if lo == 0 and h == 1:
+            for c in weights:
+                c.start()
+    for lo, h in order:
+        for c in copies(lo, h):
+            c.wait()
+        hi = lo + step
+        at = slice(lo * cap, hi * cap)
+        gate, up, down = (
+            held[2 * j + h, lo:hi].reshape(step * cap, half).astype(F32)
+            for j in range(3)
         )
-
-    weights = [
-        pltpu.make_async_copy(own_hbm, own_ref, sems.at[n]),
-        pltpu.make_async_copy(other_hbm, other_ref, sems.at[n + 1]),
-    ]
-    away = []
-    step = 256 // cap
-    for k in range(6 * step):
-        copy(k).start()
-    for c in weights:
-        c.start()
-    for k in range(6 * step, n):
-        copy(k).start()
-    for lo in range(0, sources, step):
-        for k in range(6 * lo, 6 * (lo + step)):
-            copy(k).wait()
-        at = slice(lo * cap, (lo + step) * cap)
-        out = back = None
-        for h, w_ref in enumerate((own_ref, other_ref)):
-            gate, up, down = (
-                held[at, (2 * j + h) * half : (2 * j + h + 1) * half].astype(F32)
-                for j in range(3)
-            )
-            sig = jax.nn.sigmoid(gate)
-            active = gate * sig
-            hid = (active * up).astype(BF)
-            ggp = (down * up * sig * (1.0 + gate * (1.0 - sig))).astype(BF)
-            gup = (down * active).astype(BF)
-            for j, a in enumerate((ggp, gup, hid)):
-                acts_ref[at, (3 * h + j) * half : (3 * h + j + 1) * half] = a
-            if lo == 0:
-                weights[h].wait()
-            part = dot_nt(hid, w_ref[2])
-            out = part if out is None else out + part
-            part = dot_nt(ggp, w_ref[0]) + dot_nt(gup, w_ref[1])
-            back = part if back is None else back + part
-        hi = lo + step
+        sig = jax.nn.sigmoid(gate)
+        active = gate * sig
+        hid = (active * up).astype(BF)
+        ggp = (down * up * sig * (1.0 + gate * (1.0 - sig))).astype(BF)
+        gup = (down * active).astype(BF)
+        for j, a in enumerate((ggp, gup, hid)):
+            acts_ref[at, (3 * h + j) * half : (3 * h + j + 1) * half] = a
+        if lo == 0 and h == 1:
+            for c in weights:
+                c.wait()
+        w_ref = (own_ref, other_ref)[h]
+        part_out = dot_nt(hid, w_ref[2])
+        part_back = dot_nt(ggp, w_ref[0]) + dot_nt(gup, w_ref[1])
+        if h == 0:
+            out, back = part_out, part_back
+            continue
+        out, back = out + part_out, back + part_back
         for t in range(full):
             lanes = slice(t * LANES, (t + 1) * LANES)
             put_tile(ret_ref, lo, hi, cap, t, back[:, lanes].astype(BF))
             put_tile(ret_ref, lo, hi, cap, full + t, out[:, lanes].astype(BF))
         last = back[:, main:] + out[:, main:]
         put_tile(ret_ref, lo, hi, cap, 2 * full, last.astype(BF))
-        blocks = pl.ds(lo, step)
-        away.append(
-            pltpu.make_async_copy(
-                ret_ref.at[blocks], ret_hbm.at[blocks], sems.at[n + 2 + len(away)]
-            )
-        )
-        away[-1].start()
-    for c in away:
-        c.wait()
 
 
 def grad_of(dsl, cap, rows_ref, acts_ref, j):
@@ -234,18 +223,18 @@
     return grad[:dsl]
 
 
-def other_grads_kernel(dsl, cap, rows_ref, acts_ref, out_ref):
+def grads_kernel(dsl, cap, rows_ref, acts_ref, *rest):
+    out_ref = rest[-1]
     for j in range(3):
-        out_ref[j] = grad_of(dsl, cap, rows_ref, acts_ref, j).astype(BF)
-
-
-def own_grads_kernel(dsl, cap, rows_ref, acts_ref, theirs_ref, *outs):
-    for j in range(3):
-        part = grad_of(dsl, cap, rows_ref, acts_ref, j)
-        outs[j][...] = (part + theirs_ref[j].astype(F32)).astype(BF)
-
-
-def combine_kernel(experts, cap, ret_ref, routes_ref, weight_ref, _, out_ref, grad_ref):
+        out_ref[j] = grad_of(dsl, cap, rows_ref, acts_ref, j).astype(out_ref.dtype)
+
+
+def add_kernel(own_ref, theirs_ref, *outs):
+    for j, out_ref in enumerate(outs):
+        out_ref[...] = (own_ref[j] + theirs_ref[j].astype(F32)).astype(BF)
+
+
+def combine_kernel(experts, cap, ret_ref, routes_ref, weight_ref, out_ref, grad_ref):
     dsl = out_ref.shape[0]
     main, first, _ = layout(dsl)
     tail = dsl - main
@@ -288,13 +277,13 @@
     routes_t, weight_t = routes.T, route_weight.T
     main, first, _ = layout(dsl)
     block = shape((experts, (2 * len(first) - 1) * cap, LANES), BF)
-    padded = (3, main + LANES, half)
+    padded = shape((3, main + LANES, half), BF)
     stack = shape((3, dsl, half), BF)
     send, w_own = pl.pallas_call(
         functools.partial(send_kernel, experts, cap),
-        out_shape=[block, pltpu.HBM(padded, BF)],
+        out_shape=[block, padded],
         in_specs=[hbm] * 7,
-        out_specs=[vmem, hbm],
+        out_specs=[vmem, pl.BlockSpec(memory_space=pl.ANY)],
         scratch_shapes=[
             pltpu.VMEM((dsl, ntok), BF),
             pltpu.VMEM((dsl, ntok), BF),
@@ -332,54 +321,50 @@
     sums = [in_hbm(a) for a in lax.psum(list(pieces), "dp")]
     acts, ret = pl.pallas_call(
         functools.partial(back_kernel, dsl, cap, n),
-        out_shape=[shape((rows, 6 * half), BF), pltpu.HBM(block.shape, BF)],
-        in_specs=[hbm] * (n + 2),
-        out_specs=[vmem, hbm],
+        out_shape=[shape((rows, 6 * half), BF), block],
+        in_specs=[hbm] * n + [vmem, hbm],
+        out_specs=[vmem] * 2,
         scratch_shapes=[
-            pltpu.VMEM((rows, 6 * half), BF),
-            pltpu.VMEM(padded, BF),
-            pltpu.VMEM(padded, BF),
-            pltpu.VMEM(block.shape, BF),
-            pltpu.SemaphoreType.DMA((n + 2 + rows // 256,)),
+            pltpu.VMEM((6, experts, cap, half), BF),
+            pltpu.VMEM(padded.shape, BF),
+            pltpu.SemaphoreType.DMA((n + 3,)),
         ],
         compiler_params=params(),
         cost_estimate=cost(6 * flops, 2 * rows * (dsl * 2 + 12 * half)),
-    )(*sums, in_hbm(w_own), in_hbm(w_other))
+    )(*sums, w_own, in_hbm(w_other))
     ret = exchange(ret)
 
-    whole = [
-        pl.BlockSpec(block.shape, lambda i: (0, 0, 0)),
-        pl.BlockSpec((rows, 3 * half), lambda i: (0, 1)),
-    ]
-    half_cost = cost(3 * flops, 2 * rows * (dsl * 2 + 3 * half))
-    for_other = pl.pallas_call(
-        functools.partial(other_grads_kernel, dsl, cap),
-        grid=(1,),
-        out_shape=stack,
-        in_specs=whole,
-        out_specs=pl.BlockSpec(stack.shape, lambda i: (0, 0, 0)),
-        compiler_params=params(),
-        cost_estimate=half_cost,
-    )(got, acts)
-    theirs = lax.ppermute(for_other, "expert", swap)
-    whole[1] = pl.BlockSpec((rows, 3 * half), lambda i: (0, 0))
-    grad_gate, grad_up, grad_down_t = pl.pallas_call(
-        functools.partial(own_grads_kernel, dsl, cap),
-        grid=(1,),
-        out_shape=[shape((dsl, half), BF)] * 3,
-        in_specs=whole + [pl.BlockSpec(stack.shape, lambda i: (0, 0, 0))],
-        out_specs=[pl.BlockSpec((dsl, half), lambda i: (0, 0))] * 3,
-        compiler_params=params(),
-        cost_estimate=half_cost,
-    )(got, acts, theirs)
+    parked = in_hbm(got)
+
+    def grads(part, dtype, *after):
+        return pl.pallas_call(
+            functools.partial(grads_kernel, dsl, cap),
+            grid=(1,),
+            out_shape=shape(stack.shape, dtype),
+            in_specs=[
+                pl.BlockSpec(block.shape, lambda i: (0, 0, 0)),
+                pl.BlockSpec((rows, 3 * half), lambda i: (0, part)),
+            ]
+            + [hbm] * len(after),
+            out_specs=pl.BlockSpec(stack.shape, lambda i: (0, 0, 0)),
+            compiler_params=params(),
+            cost_estimate=cost(3 * flops, 2 * rows * (dsl * 2 + 3 * half)),
+        )(parked, acts, *after)
+
+    theirs = lax.ppermute(grads(1, BF, in_hbm(ret)), "expert", swap)
+    own = grads(0, F32)
     output_t, grad_tokens_t = pl.pallas_call(
         functools.partial(combine_kernel, experts, cap),
         out_shape=[shape((dsl, ntok), BF)] * 2,
-        in_specs=[vmem] * 3 + [hbm],
-        out_specs=[vmem] * 2,
         compiler_params=params(),
         cost_estimate=cost(6 * rows * ntok * dsl, 2 * rows * dsl * 4),
-    )(ret, routes_t, weight_t, in_hbm(grad_gate))
+    )(ret, routes_t, weight_t)
+    grad_gate, grad_up, grad_down_t = pl.pallas_call(
+        add_kernel,
+        out_shape=[shape((dsl, half), BF)] * 3,
+        compiler_params=params(),
+        cost_estimate=cost(3 * dsl * half, 24 * dsl * half),
+    )(own, theirs)
     return output_t.T, grad_tokens_t.T, grad_gate, grad_up, grad_down_t.T
 
 

time: 196 us -> 150 us (0.77)
  Pallas kernels: 60.9 us -> 17.2 us
  blocking collectives: 95.7 us -> 110 us
  waiting for transfers between devices: 12.6 us -> 0.01 us
  starting transfers between devices: 24.1 us -> 21.6 us
    pallas_call x1, Pallas kernels: 42.9 us -> 1.75 us  [per_device(): pl.pallas_call(functools.partial(send_kernel, experts, cap), out_shape=[b...]
    all_to_all x1 -> x2, blocking collectives: 18.3 us -> 32.7 us  [exchange(): lax.all_to_all(a, 'expert', 0, 0, axis_index_groups=cores, tiled=True)]
    all_to_all x1 -> x0, waiting for transfers between devices: 12.6 us -> none  [exchange(): lax.all_to_all(a, 'expert', 0, 0, axis_index_groups=cores, tiled=True)]
    all_to_all x1 -> x0, starting transfers between devices: 4.32 us -> none  [exchange(): lax.all_to_all(a, 'expert', 0, 0, axis_index_groups=cores, tiled=True)]
    pallas_call x2 -> x3, Pallas kernels: 5.31 us -> 5.63 us  [the longest x2 4.38 us: grads(): pl.pallas_call(functools.partial(grads_kernel, dsl, cap), grid=(1,), out_...]
  transfers between devices with their start and end apart: 3 -> 2, of which waited for: 1 -> 0; matrix products, arithmetic and copies ran while one was open for 0% -> 0% of each run, Pallas kernels for 2% -> 2%
where the time goes in v5:
time: 150 us
  blocking collectives  110 us (73%)
  starting transfers between devices  21.6 us (14%)
  Pallas kernels  17.2 us (11%)
    psum x1, blocking collectives, per_device(): sums = [in_hbm(a) for a in lax.psum(list(pieces), 'dp')]  77.4 us
    all_to_all x2, blocking collectives, exchange(): lax.all_to_all(a, 'expert', 0, 0, axis_index_groups=cores, tiled=True)  32.7 us
    ppermute x1, starting transfers between devices, per_device(): theirs = lax.ppermute(grads(1, BF, in_hbm(ret)), 'expert', swap)  12.8 us
    ppermute x1, starting transfers between devices, per_device(): w_other = lax.ppermute(w_own, 'expert', swap)  8.79 us
    pallas_call x1, Pallas kernels, per_device(): pl.pallas_call(functools.partial(back_kernel, dsl, cap, n), out_shape=[sh...  4.97 us
    pallas_call x2, Pallas kernels, grads(): pl.pallas_call(functools.partial(grads_kernel, dsl, cap), grid=(1,), out_...  4.38 us
    pallas_call x1, Pallas kernels, per_device(): pl.pallas_call(functools.partial(terms_kernel, dsl, cap), out_shape=[pltp...  3.39 us
  transfers between devices with their start and end apart: 2, of which 0 were waited for; matrix products, arithmetic and copies ran while one was open for 0% of the time, Pallas kernels for 2%

profile of v5, /device:TPU:1, one launch (start us, length us, event | category | flops | bytes accessed | tf_op | source)
XLA Modules:
  0.0 149.7 jit_solution(14896406150156044386)
XLA Ops:
  0.6 1.7 %shard_map.110 = (bf16[16,224,128]{2,1,0:T(8,128)(2,1)S(1)}, bf16[3,512,512]{2,1,0:T(8,128)(2,1)S(1)}) custom-call(bf16[448,128]{1,0:T(8,128)(2,1)} %bitcast.13, bf16[448,128]{1,0:T(8,128)(2,1)} %bitcast.14, s32[2,128]{1,0:T(2,128)} %bitcast.8, f32[2,128]{1,0:T(2,128)} %bitcast.10, bf16[448,512]{1,0:T(8,128)(2,1)} %wg_hbm.1, bf16[448,512]{1,0:T(8,128)(2,1)} %wu_hbm.1, ...), custom_call_target="tpu_custom_call" | custom-call | flops 117440512 | bytes 1835008 | tf_op jit(solution)/shard_map/pallas_call | solution.py:282
  2.4 8.8 %collective-permute-start = (bf16[3,512,512]{2,1,0:T(8,128)(2,1)S(1)}, bf16[3,512,512]{2,1,0:T(8,128)(2,1)S(1)}, u32[]{:S(2)}, u32[]{:S(2)}) collective-permute-start(bf16[3,512,512]{2,1,0:T(8,128)(2,1)S(1)} %get-tuple-element.111.own_ref.refs_96_), channel_id=1, source_target_pairs={{0,16},{16,0},{32,48},{48,32},{64,80},{80,64},{96,112},{112,96},{1... | collective-permute-start | bytes 4718600 | tf_op jit(solution)/shard_map/ppermute | solution.py:306
  11.2 18.3 %all_to_all.10.rows_ref = bf16[16,224,128]{2,1,0:T(8,128)(2,1)S(1)} all-to-all(bf16[16,224,128]{2,1,0:T(8,128)(2,1)S(1)} %get-tuple-element.110), channel_id=1, replica_groups={{0,32,64,96,128,160,192,224,256,288,320,352,384,416,448,480},{16,48,80,..., dimensions={0} | all-to-all | bytes 1835008 | tf_op jit(solution)/shard_map/all_to_all | solution.py:275
  29.5 0.0 copy-start.1
  29.5 0.0 collective-permute-done.other_ref.refs_97_
  29.5 0.0 copy-start.2
  29.5 3.4 %shard_map.111 = (bf16[32,512]{1,0:T(8,128)(2,1)}, bf16[32,512]{1,0:T(8,128)(2,1)}, bf16[32,512]{1,0:T(8,128)(2,1)}, bf16[32,512]{1,0:T(8,128)(2,1)}, bf16[32,51...) custom-call(bf16[16,224,128]{2,1,0:T(8,128)(2,1)S(1)} %all_to_all.10, ...), custom_call_target="tpu_custom_call" | custom-call | flops 1409286144 | bytes 4063232 | tf_op jit(solution)/shard_map/pallas_call | solution.py:309
  32.9 0.0 copy-done.1
  32.9 0.0 copy-done.2
  32.9 77.4 %all-reduce.2 = (bf16[32,512]{1,0:T(8,128)(2,1)}, bf16[32,512]{1,0:T(8,128)(2,1)}, bf16[32,512]{1,0:T(8,128)(2,1)}, bf16[32,512]{1,0:T(8,128)(2,1)}, bf16[32,512...) all-reduce(bf16[32,512]{1,0:T(8,128)(2,1)} %get-tuple-element.112, ...), channel_id=1, replica_groups=mesh['expert'=32,'dp'=16] {'dp'}, use_global_device_ids=true, to_apply=%region_0.0 | all-reduce | flops 1572864 | bytes 6291456 | tf_op jit(solution)/shard_map/psum | solution.py:321
  110.3 5.0 %shard_map.112 = (bf16[512,3072]{1,0:T(8,128)(2,1)S(1)}, bf16[16,224,128]{2,1,0:T(8,128)(2,1)S(1)}) custom-call(bf16[32,512]{1,0:T(8,128)(2,1)} %get-tuple-element.215.refs_0_, bf16[32,512]{1,0:T(8,128)(2,1)} %get-tuple-element.216.refs_1_, bf16[32,512]{1,0:T(8,128)(2,1)} %get-tuple-element.217.refs_2_, bf16[32,512]{1,0:T(8,128)(2,1)} %get-tuple-element.218.refs_3_, ...), custom_call_target="tpu_custom_call" | custom-call | flops 1409286144 | bytes 7208960 | tf_op jit(solution)/shard_map/pallas_call | solution.py:322
  115.3 14.4 %all_to_all.11.ret_ref.rest_0_ = bf16[16,224,128]{2,1,0:T(8,128)(2,1)} all-to-all(bf16[16,224,128]{2,1,0:T(8,128)(2,1)S(1)} %get-tuple-element.208), channel_id=1, replica_groups={{0,32,64,96,128,160,192,224,256,288,320,352,384,416,448,480},{16,48,80,..., dimensions={0} | all-to-all | bytes 1835008 | tf_op jit(solution)/shard_map/all_to_all | solution.py:275
  129.7 2.2 %shard_map.115 = bf16[3,448,512]{2,1,0:T(8,128)(2,1)S(1)} custom-call(bf16[16,224,128]{2,1,0:T(8,128)(2,1)} %copy-done.1, bf16[512,3072]{1,0:T(8,128)(2,1)S(1)} %get-tuple-element.211.acts_ref, bf16[16,224,128]{2,1,0:T(8,128)(2,1)} %all_to_all.11.ret_ref.rest_0_), custom_call_target="tpu_custom_call" | custom-call | flops 704643072 | bytes 2490368 | tf_op jit(solution)/shard_map/pallas_call | solution.py:340
  131.9 0.0 copy-start
  131.9 0.0 copy-start.3
  131.9 0.0 copy-start.4
  131.9 12.8 %collective-permute-start.1 = (bf16[3,448,512]{2,1,0:T(8,128)(2,1)S(1)}, bf16[3,448,512]{2,1,0:T(8,128)(2,1)S(1)}, u32[]{:S(2)}, u32[]{:S(2)}) collective-permute-start(bf16[3,448,512]{2,1,0:T(8,128)(2,1)S(1)} %shard_map.115), channel_id=1, source_target_pairs={{0,16},{16,0},{32,48},{48,32},{64,80},{80,64},{96,112},{112,96},{1... | collective-permute-start | bytes 4128776 | tf_op jit(solution)/shard_map/ppermute | solution.py:354
  144.8 2.2 %shard_map.114.own_ref = f32[3,448,512]{2,1,0:T(8,128)S(1)} custom-call(bf16[16,224,128]{2,1,0:T(8,128)(2,1)} %copy-done.1, bf16[512,3072]{1,0:T(8,128)(2,1)S(1)} %get-tuple-element.211.acts_ref), custom_call_target="tpu_custom_call" | custom-call | flops 704643072 | bytes 2490368 | tf_op jit(solution)/shard_map/pallas_call | solution.py:340
  147.0 0.0 copy-done
  147.0 0.0 copy-done.3
  147.0 0.0 copy-done.4
  147.0 1.5 shard_map.113
  148.5 0.0 collective-permute-done.1.theirs_ref
  148.5 1.2 shard_map.116
Async XLA Ops:
  2.4 27.1 %collective-permute-start = (bf16[3,512,512]{2,1,0:T(8,128)(2,1)S(1)}, bf16[3,512,512]{2,1,0:T(8,128)(2,1)S(1)}, u32[]{:S(2)}, u32[]{:S(2)}) collective-permute-start(bf16[3,512,512]{2,1,0:T(8,128)(2,1)S(1)} %get-tuple-element.111.own_ref.refs_96_), channel_id=1, source_target_pairs={{0,16},{16,0},{32,48},{48,32},{64,80},{80,64},{96,112},{112,96},{1... | collective-permute-start | bytes 4718600 | tf_op jit(solution)/shard_map/ppermute | solution.py:306
  29.5 3.4 %copy-start.1 = (bf16[16,224,128]{2,1,0:T(8,128)(2,1)}, bf16[16,224,128]{2,1,0:T(8,128)(2,1)S(1)}, u32[]{:S(2)}) copy-start(bf16[16,224,128]{2,1,0:T(8,128)(2,1)S(1)} %all_to_all.10.rows_ref) | copy-start | bytes 2752516
  29.5 3.4 %copy-start.2 = (bf16[3,512,512]{2,1,0:T(8,128)(2,1)}, bf16[3,512,512]{2,1,0:T(8,128)(2,1)S(1)}, u32[]{:S(2)}) copy-start(bf16[3,512,512]{2,1,0:T(8,128)(2,1)S(1)} %collective-permute-done.other_ref.refs_97_) | copy-start | bytes 4718596
  131.9 15.1 %copy-start = (bf16[16,224,128]{2,1,0:T(8,128)(2,1)S(1)}, bf16[16,224,128]{2,1,0:T(8,128)(2,1)}, u32[]{:S(2)}) copy-start(bf16[16,224,128]{2,1,0:T(8,128)(2,1)} %all_to_all.11.ret_ref.rest_0_) | copy-start | bytes 2752516
  131.9 15.1 %copy-start.3 = (s32[128,2]{0,1:T(2,128)S(1)}, s32[128,2]{0,1:T(2,128)}, u32[]{:S(2)}) copy-start(s32[128,2]{0,1:T(2,128)} %param.8) | copy-start | bytes 3076
  131.9 15.1 %copy-start.4 = (f32[128,2]{0,1:T(2,128)S(1)}, f32[128,2]{0,1:T(2,128)}, u32[]{:S(2)}) copy-start(f32[128,2]{0,1:T(2,128)} %param.9) | copy-start | bytes 3076
  131.9 16.5 %collective-permute-start.1 = (bf16[3,448,512]{2,1,0:T(8,128)(2,1)S(1)}, bf16[3,448,512]{2,1,0:T(8,128)(2,1)S(1)}, u32[]{:S(2)}, u32[]{:S(2)}) collective-permute-start(bf16[3,448,512]{2,1,0:T(8,128)(2,1)S(1)} %shard_map.115), channel_id=1, source_target_pairs={{0,16},{16,0},{32,48},{48,32},{64,80},{80,64},{96,112},{112,96},{1... | collective-permute-start | bytes 4128776 | tf_op jit(solution)/shard_map/ppermute | solution.py:354

commit v6 on v5

--- a/solution.py
+++ b/solution.py
@@ -154,11 +154,14 @@
 
 def back_kernel(dsl, cap, n, *refs):
     pieces = refs[:n]
-    own_ref, other_hbm, acts_ref, ret_ref, held, other_ref, sems = refs[n:]
+    own_hbm, other_hbm, acts_ref, ret_hbm, held, own_ref, other_ref, ret_ref, sems = refs[n:]
     sources = n // 6
     weights = [
-        pltpu.make_async_copy(other_hbm.at[j], other_ref.at[j], sems.at[n + j])
-        for j in range(3)
+        [
+            pltpu.make_async_copy(src.at[j], dst.at[j], sems.at[n + 3 * h + j])
+            for j in range(3)
+        ]
+        for h, (src, dst) in enumerate(((own_hbm, own_ref), (other_hbm, other_ref)))
     ]
     half = own_ref.shape[2]
     main, _, _ = layout(dsl)
@@ -171,12 +174,13 @@
                 k = 6 * i + q
                 yield pltpu.make_async_copy(pieces[k], held.at[q, i], sems.at[k])
 
+    away = []
     order = [(lo, h) for lo in range(0, sources, step) for h in range(2)]
     for lo, h in order:
         for c in copies(lo, h):
             c.start()
-        if lo == 0 and h == 1:
-            for c in weights:
+        if lo == 0:
+            for c in weights[h]:
                 c.start()
     for lo, h in order:
         for c in copies(lo, h):
@@ -194,8 +198,8 @@
         gup = (down * active).astype(BF)
         for j, a in enumerate((ggp, gup, hid)):
             acts_ref[at, (3 * h + j) * half : (3 * h + j + 1) * half] = a
-        if lo == 0 and h == 1:
-            for c in weights:
+        if lo == 0:
+            for c in weights[h]:
                 c.wait()
         w_ref = (own_ref, other_ref)[h]
         part_out = dot_nt(hid, w_ref[2])
@@ -210,6 +214,15 @@
             put_tile(ret_ref, lo, hi, cap, full + t, out[:, lanes].astype(BF))
         last = back[:, main:] + out[:, main:]
         put_tile(ret_ref, lo, hi, cap, 2 * full, last.astype(BF))
+        blocks = pl.ds(lo, step)
+        away.append(
+            pltpu.make_async_copy(
+                ret_ref.at[blocks], ret_hbm.at[blocks], sems.at[n + 6 + len(away)]
+            )
+        )
+        away[-1].start()
+    for c in away:
+        c.wait()
 
 
 def grad_of(dsl, cap, rows_ref, acts_ref, j):
@@ -223,15 +236,15 @@
     return grad[:dsl]
 
 
-def grads_kernel(dsl, cap, rows_ref, acts_ref, *rest):
-    out_ref = rest[-1]
+def other_grads_kernel(dsl, cap, rows_ref, acts_ref, *outs):
+    for j, out_ref in enumerate(outs):
+        out_ref[...] = grad_of(dsl, cap, rows_ref, acts_ref, j).astype(BF)
+
+
+def own_grads_kernel(dsl, cap, rows_ref, acts_ref, *rest):
     for j in range(3):
-        out_ref[j] = grad_of(dsl, cap, rows_ref, acts_ref, j).astype(out_ref.dtype)
-
-
-def add_kernel(own_ref, theirs_ref, *outs):
-    for j, out_ref in enumerate(outs):
-        out_ref[...] = (own_ref[j] + theirs_ref[j].astype(F32)).astype(BF)
+        part = grad_of(dsl, cap, rows_ref, acts_ref, j)
+        rest[3 + j][...] = (part + rest[j][...].astype(F32)).astype(BF)
 
 
 def combine_kernel(experts, cap, ret_ref, routes_ref, weight_ref, out_ref, grad_ref):
@@ -321,50 +334,47 @@
     sums = [in_hbm(a) for a in lax.psum(list(pieces), "dp")]
     acts, ret = pl.pallas_call(
         functools.partial(back_kernel, dsl, cap, n),
-        out_shape=[shape((rows, 6 * half), BF), block],
-        in_specs=[hbm] * n + [vmem, hbm],
-        out_specs=[vmem] * 2,
+        out_shape=[shape((rows, 6 * half), BF), pltpu.HBM(block.shape, BF)],
+        in_specs=[hbm] * (n + 2),
+        out_specs=[vmem, hbm],
         scratch_shapes=[
             pltpu.VMEM((6, experts, cap, half), BF),
             pltpu.VMEM(padded.shape, BF),
-            pltpu.SemaphoreType.DMA((n + 3,)),
+            pltpu.VMEM(padded.shape, BF),
+            pltpu.VMEM(block.shape, BF),
+            pltpu.SemaphoreType.DMA((n + 6 + rows // 256,)),
         ],
         compiler_params=params(),
         cost_estimate=cost(6 * flops, 2 * rows * (dsl * 2 + 12 * half)),
-    )(*sums, w_own, in_hbm(w_other))
+    )(*sums, in_hbm(w_own), in_hbm(w_other))
     ret = exchange(ret)
 
-    parked = in_hbm(got)
-
-    def grads(part, dtype, *after):
+    def grads(kernel, part, *more):
+        whole = pl.BlockSpec((dsl, half), lambda i: (0, 0))
         return pl.pallas_call(
-            functools.partial(grads_kernel, dsl, cap),
+            functools.partial(kernel, dsl, cap),
             grid=(1,),
-            out_shape=shape(stack.shape, dtype),
+            out_shape=[shape((dsl, half), BF)] * 3,
             in_specs=[
                 pl.BlockSpec(block.shape, lambda i: (0, 0, 0)),
                 pl.BlockSpec((rows, 3 * half), lambda i: (0, part)),
             ]
-            + [hbm] * len(after),
-            out_specs=pl.BlockSpec(stack.shape, lambda i: (0, 0, 0)),
+            + [whole] * len(more),
+            out_specs=[whole] * 3,
             compiler_params=params(),
             cost_estimate=cost(3 * flops, 2 * rows * (dsl * 2 + 3 * half)),
-        )(parked, acts, *after)
-
-    theirs = lax.ppermute(grads(1, BF, in_hbm(ret)), "expert", swap)
-    own = grads(0, F32)
+        )(got, acts, *more)
+
+    theirs = [
+        lax.ppermute(g, "expert", swap) for g in grads(other_grads_kernel, 1)
+    ]
+    grad_gate, grad_up, grad_down_t = grads(own_grads_kernel, 0, *theirs)
     output_t, grad_tokens_t = pl.pallas_call(
         functools.partial(combine_kernel, experts, cap),
         out_shape=[shape((dsl, ntok), BF)] * 2,
         compiler_params=params(),
         cost_estimate=cost(6 * rows * ntok * dsl, 2 * rows * dsl * 4),
     )(ret, routes_t, weight_t)
-    grad_gate, grad_up, grad_down_t = pl.pallas_call(
-        add_kernel,
-        out_shape=[shape((dsl, half), BF)] * 3,
-        compiler_params=params(),
-        cost_estimate=cost(3 * dsl * half, 24 * dsl * half),
-    )(own, theirs)
     return output_t.T, grad_tokens_t.T, grad_gate, grad_up, grad_down_t.T
 
 

time: 150 us -> 145 us (0.967)
  blocking collectives: 110 us -> 95.4 us
  starting transfers between devices: 21.6 us -> 29 us
    all_to_all x2 -> x1, blocking collectives: 32.7 us -> 18.3 us  [exchange(): lax.all_to_all(a, 'expert', 0, 0, axis_index_groups=cores, tiled=True)]
    all_to_all x0 -> x1, starting transfers between devices: none -> 4.32 us  [exchange(): lax.all_to_all(a, 'expert', 0, 0, axis_index_groups=cores, tiled=True)]
    ppermute x1 -> x3, starting transfers between devices: 12.8 us -> 15.9 us  [per_device(): lax.ppermute(g, 'expert', swap)]
    pallas_call x3 -> x2, Pallas kernels: 5.63 us -> 2.79 us  [grads(): pl.pallas_call(functools.partial(kernel, dsl, cap), grid=(1,), out_shape=...]
  transfers between devices with their start and end apart: 2 -> 5, of which waited for: 0 -> 1; matrix products, arithmetic and copies ran while one was open for 0% -> 0% of each run, Pallas kernels for 2% -> 2%
where the time goes in v6:
time: 145 us
  blocking collectives  95.4 us (66%)
  starting transfers between devices  29 us (20%)
  Pallas kernels  16.9 us (12%)
    psum x1, blocking collectives, per_device(): sums = [in_hbm(a) for a in lax.psum(list(pieces), 'dp')]  77.2 us
    all_to_all x1, blocking collectives, exchange(): lax.all_to_all(a, 'expert', 0, 0, axis_index_groups=cores, tiled=True)  18.3 us
    ppermute x3, starting transfers between devices, per_device(): lax.ppermute(g, 'expert', swap)  15.9 us
    ppermute x1, starting transfers between devices, per_device(): w_other = lax.ppermute(w_own, 'expert', swap)  8.79 us
    pallas_call x1, Pallas kernels, per_device(): pl.pallas_call(functools.partial(back_kernel, dsl, cap, n), out_shape=[sh...  6.33 us
    all_to_all x1, starting transfers between devices, exchange(): lax.all_to_all(a, 'expert', 0, 0, axis_index_groups=cores, tiled=True)  4.32 us
    pallas_call x1, Pallas kernels, per_device(): pl.pallas_call(functools.partial(terms_kernel, dsl, cap), out_shape=[pltp...  3.39 us
  transfers between devices with their start and end apart: 5, of which 1 were waited for; matrix products, arithmetic and copies ran while one was open for 0% of the time, Pallas kernels for 2%

profile of v6, /device:TPU:1, one launch (start us, length us, event | category | flops | bytes accessed | tf_op | source)
XLA Modules:
  0.0 144.7 jit_solution(13119558597525944177)
XLA Ops:
  0.6 1.7 %shard_map.110 = (bf16[16,224,128]{2,1,0:T(8,128)(2,1)S(1)}, bf16[3,512,512]{2,1,0:T(8,128)(2,1)S(1)}) custom-call(bf16[448,128]{1,0:T(8,128)(2,1)} %bitcast.13, bf16[448,128]{1,0:T(8,128)(2,1)} %bitcast.14, s32[2,128]{1,0:T(2,128)} %bitcast.8, f32[2,128]{1,0:T(2,128)} %bitcast.10, bf16[448,512]{1,0:T(8,128)(2,1)} %wg_hbm.1, bf16[448,512]{1,0:T(8,128)(2,1)} %wu_hbm.1, ...), custom_call_target="tpu_custom_call" | custom-call | flops 117440512 | bytes 1835008 | tf_op jit(solution)/shard_map/pallas_call | solution.py:295
  2.4 0.0 copy-start.2
  2.4 8.8 %collective-permute-start = (bf16[3,512,512]{2,1,0:T(8,128)(2,1)S(1)}, bf16[3,512,512]{2,1,0:T(8,128)(2,1)S(1)}, u32[]{:S(2)}, u32[]{:S(2)}) collective-permute-start(bf16[3,512,512]{2,1,0:T(8,128)(2,1)S(1)} %get-tuple-element.114.own_ref.refs_96_), channel_id=1, source_target_pairs={{0,16},{16,0},{32,48},{48,32},{64,80},{80,64},{96,112},{112,96},{1... | collective-permute-start | bytes 4718600 | tf_op jit(solution)/shard_map/ppermute | solution.py:319
  11.2 18.3 %all_to_all.10.rows_ref = bf16[16,224,128]{2,1,0:T(8,128)(2,1)S(1)} all-to-all(bf16[16,224,128]{2,1,0:T(8,128)(2,1)S(1)} %get-tuple-element.113), channel_id=1, replica_groups={{0,32,64,96,128,160,192,224,256,288,320,352,384,416,448,480},{16,48,80,..., dimensions={0} | all-to-all | bytes 1835008 | tf_op jit(solution)/shard_map/all_to_all | solution.py:288
  29.5 0.0 collective-permute-done.other_ref.refs_97_
  29.5 3.4 %shard_map.111 = (bf16[32,512]{1,0:T(8,128)(2,1)}, bf16[32,512]{1,0:T(8,128)(2,1)}, bf16[32,512]{1,0:T(8,128)(2,1)}, bf16[32,512]{1,0:T(8,128)(2,1)}, bf16[32,51...) custom-call(bf16[16,224,128]{2,1,0:T(8,128)(2,1)S(1)} %all_to_all.10, ...), custom_call_target="tpu_custom_call" | custom-call | flops 1409286144 | bytes 4063232 | tf_op jit(solution)/shard_map/pallas_call | solution.py:322
  32.9 77.2 %all-reduce.2 = (bf16[32,512]{1,0:T(8,128)(2,1)}, bf16[32,512]{1,0:T(8,128)(2,1)}, bf16[32,512]{1,0:T(8,128)(2,1)}, bf16[32,512]{1,0:T(8,128)(2,1)}, bf16[32,512...) all-reduce(bf16[32,512]{1,0:T(8,128)(2,1)} %get-tuple-element.115, ...), channel_id=1, replica_groups=mesh['expert'=32,'dp'=16] {'dp'}, use_global_device_ids=true, to_apply=%region_0.0 | all-reduce | flops 1572864 | bytes 6291456 | tf_op jit(solution)/shard_map/psum | solution.py:334
  110.1 6.3 %shard_map.112 = (bf16[512,3072]{1,0:T(8,128)(2,1)S(1)}, bf16[16,224,128]{2,1,0:T(8,128)(2,1)}) custom-call(bf16[32,512]{1,0:T(8,128)(2,1)} %get-tuple-element.221.refs_0_, bf16[32,512]{1,0:T(8,128)(2,1)} %get-tuple-element.222.refs_1_, bf16[32,512]{1,0:T(8,128)(2,1)} %get-tuple-element.223.refs_2_, bf16[32,512]{1,0:T(8,128)(2,1)} %get-tuple-element.224.refs_3_, ...), custom_call_target="tpu_custom_call" | custom-call | flops 1409286144 | bytes 7208960 | tf_op jit(solution)/shard_map/pallas_call | solution.py:335
  116.4 4.3 %all-to-all-start.1 = ((bf16[16,224,128]{2,1,0:T(8,128)(2,1)}), bf16[16,224,128]{2,1,0:T(8,128)(2,1)}, u32[]{:S(2)}, u32[]{:S(2)}) async-start(bf16[16,224,128]{2,1,0:T(8,128)(2,1)} %get-tuple-element.211), calls=%async_computation.1 | async-start | bytes 1835008 | tf_op jit(solution)/shard_map/all_to_all | solution.py:288
  120.7 0.0 copy-start.1
  120.7 1.2 copy-done.1
  121.9 1.0 shard_map.114
  122.9 11.6 %collective-permute-start.1 = (bf16[448,512]{1,0:T(8,128)(2,1)S(1)}, bf16[448,512]{1,0:T(8,128)(2,1)S(1)}, u32[]{:S(2)}, u32[]{:S(2)}) collective-permute-start(bf16[448,512]{1,0:T(8,128)(2,1)S(1)} %get-tuple-element.215), channel_id=1, source_target_pairs={{0,16},{16,0},{32,48},{48,32},{64,80},{80,64},{96,112},{112,96},{1... | collective-permute-start | bytes 1376264 | tf_op jit(solution)/shard_map/ppermute | solution.py:369
  134.5 1.9 %collective-permute-start.2 = (bf16[448,512]{1,0:T(8,128)(2,1)S(1)}, bf16[448,512]{1,0:T(8,128)(2,1)S(1)}, u32[]{:S(2)}, u32[]{:S(2)}) collective-permute-start(bf16[448,512]{1,0:T(8,128)(2,1)S(1)} %get-tuple-element.216), channel_id=1, source_target_pairs={{0,16},{16,0},{32,48},{48,32},{64,80},{80,64},{96,112},{112,96},{1... | collective-permute-start | bytes 1376264 | tf_op jit(solution)/shard_map/ppermute | solution.py:369
  136.4 0.0 copy-start.4
  136.4 0.0 copy-start.5
  136.4 2.4 %collective-permute-start.3 = (bf16[448,512]{1,0:T(8,128)(2,1)S(1)}, bf16[448,512]{1,0:T(8,128)(2,1)S(1)}, u32[]{:S(2)}, u32[]{:S(2)}) collective-permute-start(bf16[448,512]{1,0:T(8,128)(2,1)S(1)} %get-tuple-element.217), channel_id=1, source_target_pairs={{0,16},{16,0},{32,48},{48,32},{64,80},{80,64},{96,112},{112,96},{1... | collective-permute-start | bytes 1376264 | tf_op jit(solution)/shard_map/ppermute | solution.py:369
  138.9 0.0 collective-permute-done.1.rest_0_
  138.9 0.0 collective-permute-done.2.rest_1_
  138.9 1.4 collective-permute-done.3.rest_2_
  140.3 1.8 %shard_map.115 = (bf16[448,512]{1,0:T(8,128)(2,1)}, bf16[448,512]{1,0:T(8,128)(2,1)}, bf16[448,512]{1,0:T(8,128)(2,1)}) custom-call(bf16[16,224,128]{2,1,0:T(8,128)(2,1)S(1)} %copy-done.1, bf16[512,3072]{1,0:T(8,128)(2,1)S(1)} %get-tuple-element.214.acts_ref, bf16[448,512]{1,0:T(8,128)(2,1)S(1)} %collective-permute-done.1.rest_0_, ...), custom_call_target="tpu_custom_call" | custom-call | flops 704643072 | bytes 2490368 | tf_op jit(solution)/shard_map/pallas_call | solution.py:354
  142.1 0.0 all-to-all-done.1.ret_ref
  142.1 0.0 copy-done.4
  142.1 2.6 %shard_map.113 = (bf16[448,128]{1,0:T(8,128)(2,1)}, bf16[448,128]{1,0:T(8,128)(2,1)}) custom-call(bf16[16,224,128]{2,1,0:T(8,128)(2,1)} %all-to-all-done.1.ret_ref, s32[2,128]{1,0:T(2,128)S(1)} %bitcast.9, f32[2,128]{1,0:T(2,128)S(1)} %bitcast.11), custom_call_target="tpu_custom_call" | custom-call | flops 176160768 | bytes 1835008 | tf_op jit(solution)/shard_map/pallas_call | solution.py:372
  (6 shorter events, 0.0 us)
Async XLA Ops:
  2.4 30.5 %copy-start.2 = (bf16[3,512,512]{2,1,0:T(8,128)(2,1)}, bf16[3,512,512]{2,1,0:T(8,128)(2,1)S(1)}, u32[]{:S(2)}) copy-start(bf16[3,512,512]{2,1,0:T(8,128)(2,1)S(1)} %get-tuple-element.114.own_ref.refs_96_) | copy-start | bytes 4718596
  2.4 27.1 %collective-permute-start = (bf16[3,512,512]{2,1,0:T(8,128)(2,1)S(1)}, bf16[3,512,512]{2,1,0:T(8,128)(2,1)S(1)}, u32[]{:S(2)}, u32[]{:S(2)}) collective-permute-start(bf16[3,512,512]{2,1,0:T(8,128)(2,1)S(1)} %get-tuple-element.114.own_ref.refs_96_), channel_id=1, source_target_pairs={{0,16},{16,0},{32,48},{48,32},{64,80},{80,64},{96,112},{112,96},{1... | collective-permute-start | bytes 4718600 | tf_op jit(solution)/shard_map/ppermute | solution.py:319
  29.5 3.4 %copy-start = (bf16[16,224,128]{2,1,0:T(8,128)(2,1)}, bf16[16,224,128]{2,1,0:T(8,128)(2,1)S(1)}, u32[]{:S(2)}) copy-start(bf16[16,224,128]{2,1,0:T(8,128)(2,1)S(1)} %all_to_all.10.rows_ref) | copy-start | bytes 2752516
  29.5 3.4 %copy-start.3 = (bf16[3,512,512]{2,1,0:T(8,128)(2,1)}, bf16[3,512,512]{2,1,0:T(8,128)(2,1)S(1)}, u32[]{:S(2)}) copy-start(bf16[3,512,512]{2,1,0:T(8,128)(2,1)S(1)} %collective-permute-done.other_ref.refs_97_) | copy-start | bytes 4718596
  116.4 25.7 %all-to-all-start.1 = ((bf16[16,224,128]{2,1,0:T(8,128)(2,1)}), bf16[16,224,128]{2,1,0:T(8,128)(2,1)}, u32[]{:S(2)}, u32[]{:S(2)}) async-start(bf16[16,224,128]{2,1,0:T(8,128)(2,1)} %get-tuple-element.211), calls=%async_computation.1 | async-start | bytes 1835008 | tf_op jit(solution)/shard_map/all_to_all | solution.py:288
  120.7 1.2 copy-start.1
  122.9 15.9 %collective-permute-start.1 = (bf16[448,512]{1,0:T(8,128)(2,1)S(1)}, bf16[448,512]{1,0:T(8,128)(2,1)S(1)}, u32[]{:S(2)}, u32[]{:S(2)}) collective-permute-start(bf16[448,512]{1,0:T(8,128)(2,1)S(1)} %get-tuple-element.215), channel_id=1, source_target_pairs={{0,16},{16,0},{32,48},{48,32},{64,80},{80,64},{96,112},{112,96},{1... | collective-permute-start | bytes 1376264 | tf_op jit(solution)/shard_map/ppermute | solution.py:369
  134.5 4.4 %collective-permute-start.2 = (bf16[448,512]{1,0:T(8,128)(2,1)S(1)}, bf16[448,512]{1,0:T(8,128)(2,1)S(1)}, u32[]{:S(2)}, u32[]{:S(2)}) collective-permute-start(bf16[448,512]{1,0:T(8,128)(2,1)S(1)} %get-tuple-element.216), channel_id=1, source_target_pairs={{0,16},{16,0},{32,48},{48,32},{64,80},{80,64},{96,112},{112,96},{1... | collective-permute-start | bytes 1376264 | tf_op jit(solution)/shard_map/ppermute | solution.py:369
  136.4 5.6 %copy-start.4 = (s32[128,2]{0,1:T(2,128)S(1)}, s32[128,2]{0,1:T(2,128)}, u32[]{:S(2)}) copy-start(s32[128,2]{0,1:T(2,128)} %param.8) | copy-start | bytes 3076
  136.4 5.6 %copy-start.5 = (f32[128,2]{0,1:T(2,128)S(1)}, f32[128,2]{0,1:T(2,128)}, u32[]{:S(2)}) copy-start(f32[128,2]{0,1:T(2,128)} %param.9) | copy-start | bytes 3076
  136.4 3.8 %collective-permute-start.3 = (bf16[448,512]{1,0:T(8,128)(2,1)S(1)}, bf16[448,512]{1,0:T(8,128)(2,1)S(1)}, u32[]{:S(2)}, u32[]{:S(2)}) collective-permute-start(bf16[448,512]{1,0:T(8,128)(2,1)S(1)} %get-tuple-element.217), channel_id=1, source_target_pairs={{0,16},{16,0},{32,48},{48,32},{64,80},{80,64},{96,112},{112,96},{1... | collective-permute-start | bytes 1376264 | tf_op jit(solution)/shard_map/ppermute | solution.py:369

commit v7 on v6

--- a/solution.py
+++ b/solution.py
@@ -76,25 +76,16 @@
 
 
 def send_kernel(
-    experts, cap, tok_hbm, cot_hbm, routes_hbm, weight_hbm, wg_hbm, wu_hbm, wd_hbm,
-    out_ref, stack_hbm, tok_ref, cot_ref, routes_ref, weight_ref, zeros, sems,
+    experts, cap, tok_hbm, cot_hbm, routes_hbm, weight_hbm,
+    out_ref, tok_ref, cot_ref, routes_ref, weight_ref, sems,
 ):
     dsl, ntok = tok_ref.shape
     main, first, _ = layout(dsl)
-    tail = dsl - main
-    zeros[...] = jnp.zeros_like(zeros)
     pairs = (
         (routes_hbm, routes_ref),
         (tok_hbm, tok_ref),
         (weight_hbm, weight_ref),
         (cot_hbm, cot_ref),
-        (wg_hbm, stack_hbm.at[0, pl.ds(0, dsl)]),
-        (wu_hbm, stack_hbm.at[1, pl.ds(0, dsl)]),
-        (wd_hbm.at[pl.ds(0, main)], stack_hbm.at[2, pl.ds(0, main)]),
-        (wd_hbm.at[pl.ds(main, tail)], stack_hbm.at[2, pl.ds(dsl, tail)]),
-        (zeros, stack_hbm.at[0, pl.ds(dsl, tail)]),
-        (zeros, stack_hbm.at[1, pl.ds(dsl, tail)]),
-        (zeros, stack_hbm.at[2, pl.ds(main, tail)]),
     )
     copies = [
         pltpu.make_async_copy(src, dst, sems.at[i])
@@ -104,7 +95,7 @@
         c.start()
     copies[0].wait()
     picks = pickers(routes_ref[...], experts, cap)
-    for c in copies[1:4]:
+    for c in copies[1:]:
         c.wait()
     tok = tok_ref[...]
     cot = cot_ref[...].astype(F32)
@@ -118,25 +109,39 @@
     rows = rows.astype(BF)
     for t in range(2 * len(first) - 1):
         put_tile(out_ref, 0, experts, cap, t, rows[:, t * LANES : (t + 1) * LANES])
-    for c in copies[4:]:
-        c.wait()
-
-
-def terms_kernel(dsl, cap, rows_ref, own_ref, other_ref, *rest):
+
+
+def terms_kernel(cap, rows_ref, *rest):
     sources = rows_ref.shape[0]
-    outs, (held, sems) = rest[:-2], rest[-2:]
-    _, first, second = layout(dsl)
-    half = own_ref.shape[2]
+    own_hbm, others, outs, (held, own_ref, sems) = (
+        rest[:3],
+        rest[3:6],
+        rest[6:-3],
+        rest[-3:],
+    )
+    dsl, half = others[0].shape
+    fetches = [
+        pltpu.make_async_copy(own_hbm[j], own_ref.at[j], sems.at[len(outs) + j])
+        for j in range(3)
+    ]
+    for c in fetches:
+        c.start()
+    main, first, second = layout(dsl)
+    gap = jnp.zeros((dsl - main, half), BF)
     step = 256 // cap
     copies = []
     for lo in range(0, sources, step):
         x = tiles(rows_ref, lo, lo + step, cap, first)
         dy = tiles(rows_ref, lo, lo + step, cap, second)
         at = slice(lo * cap, (lo + step) * cap)
-        for q in range(6):
+        for q in (1, 3, 5, 0, 2, 4):
             j, h = divmod(q, 2)
-            w = (own_ref, other_ref)[h][j]
-            left = dy if j == 2 else x
+            if lo == 0 and h == 0:
+                fetches[j].wait()
+            w = others[j][...] if h else own_ref[j]
+            if j == 2:
+                w = jnp.concatenate([w[:main], gap, w[main:]], axis=0)
+            left = dy if j == 2 else x[:, :dsl]
             held[at, q * half : (q + 1) * half] = dot_nn(left, w).astype(BF)
             for i in range(lo, lo + step):
                 k = 6 * i + q
@@ -154,19 +159,31 @@
 
 def back_kernel(dsl, cap, n, *refs):
     pieces = refs[:n]
-    own_hbm, other_hbm, acts_ref, ret_hbm, held, own_ref, other_ref, ret_ref, sems = refs[n:]
+    acts_ref, ret_hbm, held, own_ref, other_ref, ret_ref, sems = refs[n + 6 :]
     sources = n // 6
-    weights = [
-        [
-            pltpu.make_async_copy(src.at[j], dst.at[j], sems.at[n + 3 * h + j])
-            for j in range(3)
-        ]
-        for h, (src, dst) in enumerate(((own_hbm, own_ref), (other_hbm, other_ref)))
-    ]
     half = own_ref.shape[2]
     main, _, _ = layout(dsl)
     full = main // LANES
+    tail = dsl - main
     step = 256 // cap
+    weights = []
+    for h, w_ref in enumerate((own_ref, other_ref)):
+        gate, up, down = refs[n + 3 * h : n + 3 * h + 3]
+        parts = (
+            (gate, w_ref.at[0, pl.ds(0, dsl)]),
+            (up, w_ref.at[1, pl.ds(0, dsl)]),
+            (down.at[pl.ds(0, main)], w_ref.at[2, pl.ds(0, main)]),
+            (down.at[pl.ds(main, tail)], w_ref.at[2, pl.ds(dsl, tail)]),
+        )
+        weights.append(
+            [
+                pltpu.make_async_copy(src, dst, sems.at[n + 4 * h + i])
+                for i, (src, dst) in enumerate(parts)
+            ]
+        )
+        for j in range(3):
+            lo = main if j == 2 else dsl
+            w_ref[j, lo : lo + tail] = jnp.zeros((tail, half), BF)
 
     def copies(lo, h):
         for i in range(lo, lo + step):
@@ -217,7 +234,7 @@
         blocks = pl.ds(lo, step)
         away.append(
             pltpu.make_async_copy(
-                ret_ref.at[blocks], ret_hbm.at[blocks], sems.at[n + 6 + len(away)]
+                ret_ref.at[blocks], ret_hbm.at[blocks], sems.at[n + 8 + len(away)]
             )
         )
         away[-1].start()
@@ -247,12 +264,17 @@
         rest[3 + j][...] = (part + rest[j][...].astype(F32)).astype(BF)
 
 
-def combine_kernel(experts, cap, ret_ref, routes_ref, weight_ref, out_ref, grad_ref):
+def combine_kernel(
+    experts, cap, ret_hbm, routes_ref, weight_ref, out_ref, grad_ref, ret_ref, sem
+):
+    fetch = pltpu.make_async_copy(ret_hbm, ret_ref, sem)
+    fetch.start()
     dsl = out_ref.shape[0]
     main, first, _ = layout(dsl)
     tail = dsl - main
     picks = pickers(routes_ref[...], experts, cap)
     weight = weight_ref[...]
+    fetch.wait()
     rows = tiles(ret_ref, 0, experts, cap, range(2 * len(first) - 1))
     out = back = None
     for k, pick in enumerate(picks):
@@ -291,62 +313,56 @@
     main, first, _ = layout(dsl)
     block = shape((experts, (2 * len(first) - 1) * cap, LANES), BF)
     padded = shape((3, main + LANES, half), BF)
+    w_own = [w_gate, w_up, w_down.T]
     stack = shape((3, dsl, half), BF)
-    send, w_own = pl.pallas_call(
+    send = pl.pallas_call(
         functools.partial(send_kernel, experts, cap),
-        out_shape=[block, padded],
-        in_specs=[hbm] * 7,
-        out_specs=[vmem, pl.BlockSpec(memory_space=pl.ANY)],
+        out_shape=block,
+        in_specs=[hbm] * 4,
+        out_specs=vmem,
         scratch_shapes=[
             pltpu.VMEM((dsl, ntok), BF),
             pltpu.VMEM((dsl, ntok), BF),
             pltpu.VMEM((top, ntok), jnp.int32),
             pltpu.VMEM((top, ntok), F32),
-            pltpu.VMEM((dsl - main, half), BF),
-            pltpu.SemaphoreType.DMA((11,)),
+            pltpu.SemaphoreType.DMA((4,)),
         ],
         compiler_params=params(),
         cost_estimate=cost(4 * rows * ntok * dsl, 2 * rows * dsl * 4),
-    )(
-        *(
-            in_hbm(a)
-            for a in (
-                tokens.T, cotangent.T, routes_t, weight_t, w_gate, w_up, w_down.T
-            )
-        )
-    )
+    )(*(in_hbm(a) for a in (tokens.T, cotangent.T, routes_t, weight_t)))
     got = exchange(send)
-    w_other = lax.ppermute(w_own, "expert", swap)
+    w_other = [lax.ppermute(w, "expert", swap) for w in w_own]
 
     n = 6 * experts
     pieces = pl.pallas_call(
-        functools.partial(terms_kernel, dsl, cap),
+        functools.partial(terms_kernel, cap),
         out_shape=[pltpu.HBM((cap, half), BF)] * n,
-        in_specs=[vmem] * 3,
+        in_specs=[vmem] + [hbm] * 3 + [vmem] * 3,
         out_specs=[hbm] * n,
         scratch_shapes=[
             pltpu.VMEM((rows, 6 * half), BF),
-            pltpu.SemaphoreType.DMA((n,)),
+            pltpu.VMEM(stack.shape, BF),
+            pltpu.SemaphoreType.DMA((n + 3,)),
         ],
         compiler_params=params(),
         cost_estimate=cost(6 * flops, 2 * rows * (dsl * 2 + 6 * half)),
-    )(got, w_own, w_other)
+    )(got, *(in_hbm(w) for w in w_own), *w_other)
     sums = [in_hbm(a) for a in lax.psum(list(pieces), "dp")]
     acts, ret = pl.pallas_call(
         functools.partial(back_kernel, dsl, cap, n),
         out_shape=[shape((rows, 6 * half), BF), pltpu.HBM(block.shape, BF)],
-        in_specs=[hbm] * (n + 2),
+        in_specs=[hbm] * (n + 6),
         out_specs=[vmem, hbm],
         scratch_shapes=[
             pltpu.VMEM((6, experts, cap, half), BF),
             pltpu.VMEM(padded.shape, BF),
             pltpu.VMEM(padded.shape, BF),
             pltpu.VMEM(block.shape, BF),
-            pltpu.SemaphoreType.DMA((n + 6 + rows // 256,)),
+            pltpu.SemaphoreType.DMA((n + 8 + rows // 256,)),
         ],
         compiler_params=params(),
         cost_estimate=cost(6 * flops, 2 * rows * (dsl * 2 + 12 * half)),
-    )(*sums, in_hbm(w_own), in_hbm(w_other))
+    )(*sums, *(in_hbm(w) for w in w_own + w_other))
     ret = exchange(ret)
 
     def grads(kernel, part, *more):
@@ -372,9 +388,12 @@
     output_t, grad_tokens_t = pl.pallas_call(
         functools.partial(combine_kernel, experts, cap),
         out_shape=[shape((dsl, ntok), BF)] * 2,
+        in_specs=[hbm, vmem, vmem],
+        out_specs=[vmem] * 2,
+        scratch_shapes=[pltpu.VMEM(block.shape, BF), pltpu.SemaphoreType.DMA(())],
         compiler_params=params(),
         cost_estimate=cost(6 * rows * ntok * dsl, 2 * rows * dsl * 4),
-    )(ret, routes_t, weight_t)
+    )(in_hbm(ret), routes_t, weight_t)
     return output_t.T, grad_tokens_t.T, grad_gate, grad_up, grad_down_t.T
 
 

time: 145 us -> 145 us (level)
  blocking collectives: 95.4 us -> 81.2 us
  starting transfers between devices: 29 us -> 36.4 us
  waiting for transfers between devices: 1.41 us -> 5.15 us
  Pallas kernels: 16.9 us -> 19.1 us
    all_to_all x1 -> x0, blocking collectives: 18.3 us -> none  [exchange(): lax.all_to_all(a, 'expert', 0, 0, axis_index_groups=cores, tiled=True)]
    all_to_all x1 -> x2, starting transfers between devices: 4.32 us -> 11.9 us  [exchange(): lax.all_to_all(a, 'expert', 0, 0, axis_index_groups=cores, tiled=True)]
    psum x1, blocking collectives: 77.2 us -> 81.2 us  [per_device(): sums = [in_hbm(a) for a in lax.psum(list(pieces), 'dp')]]
    pallas_call x2, Pallas kernels: 5.13 us -> 7.48 us  [the longest x1 4.88 us: per_device(): pl.pallas_call(functools.partial(terms_kernel, cap), out_shape=[pltpu.HBM...]
    all_to_all x1 -> x2, waiting for transfers between devices: 0.01 us -> 2.15 us  [exchange(): lax.all_to_all(a, 'expert', 0, 0, axis_index_groups=cores, tiled=True)]
    ppermute x1 -> x3, waiting for transfers between devices: 0.01 us -> 1.59 us  [per_device(): w_other = [lax.ppermute(w, 'expert', swap) for w in w_own]]
    ppermute x1 -> x3, starting transfers between devices: 8.79 us -> 9.17 us  [per_device(): w_other = [lax.ppermute(w, 'expert', swap) for w in w_own]]
  transfers between devices with their start and end apart: 5 -> 8, of which waited for: 1 -> 3; matrix products, arithmetic and copies ran while one was open for 0% -> 0% of each run, Pallas kernels for 2% -> 2%
where the time goes in v7:
time: 145 us; the launch traced here: 144 us
  blocking collectives  81.2 us (56%)
  starting transfers between devices  36.4 us (25%)
  Pallas kernels  19.1 us (13%)
  waiting for transfers between devices  5.15 us (4%)
    psum x1, blocking collectives, per_device(): sums = [in_hbm(a) for a in lax.psum(list(pieces), 'dp')]  81.2 us
    ppermute x3, starting transfers between devices, per_device(): lax.ppermute(g, 'expert', swap)  15.3 us
    all_to_all x2, starting transfers between devices, exchange(): lax.all_to_all(a, 'expert', 0, 0, axis_index_groups=cores, tiled=True)  11.9 us
    ppermute x3, starting transfers between devices, per_device(): w_other = [lax.ppermute(w, 'expert', swap) for w in w_own]  9.17 us
    pallas_call x1, Pallas kernels, per_device(): pl.pallas_call(functools.partial(back_kernel, dsl, cap, n), out_shape=[sh...  6.3 us
    pallas_call x1, Pallas kernels, per_device(): pl.pallas_call(functools.partial(terms_kernel, cap), out_shape=[pltpu.HBM...  4.88 us
  transfers between devices with their start and end apart: 8, of which 3 were waited for; matrix products, arithmetic and copies ran while one was open for 0% of the time, Pallas kernels for 2%

profile of v7, /device:TPU:1, one launch (start us, length us, event | category | flops | bytes accessed | tf_op | source)
XLA Modules:
  0.0 143.9 jit_solution(16834467477190250751)
XLA Ops:
  0.6 2.6 %shard_map.110 = bf16[16,224,128]{2,1,0:T(8,128)(2,1)} custom-call(bf16[448,128]{1,0:T(8,128)(2,1)} %bitcast.15, bf16[448,128]{1,0:T(8,128)(2,1)} %bitcast.16, s32[2,128]{1,0:T(2,128)} %bitcast.8, f32[2,128]{1,0:T(2,128)} %bitcast.10), custom_call_target="tpu_custom_call" | custom-call | flops 117440512 | bytes 1835008 | tf_op jit(solution)/shard_map/pallas_call | solution.py:318
  3.2 7.6 %all-to-all-start = ((bf16[16,224,128]{2,1,0:T(8,128)(2,1)}), bf16[16,224,128]{2,1,0:T(8,128)(2,1)S(1)}, u32[]{:S(2)}, u32[]{:S(2)}) async-start(bf16[16,224,128]{2,1,0:T(8,128)(2,1)} %shard_map.110), calls=%async_computation | async-start | bytes 1835008 | tf_op jit(solution)/shard_map/all_to_all | solution.py:310
  10.8 4.8 %collective-permute-start.2 = (bf16[448,512]{1,0:T(8,128)(2,1)}, bf16[448,512]{1,0:T(8,128)(2,1)S(1)}, u32[]{:S(2)}, u32[]{:S(2)}) collective-permute-start(bf16[448,512]{1,0:T(8,128)(2,1)} %bitcast.12), channel_id=1, source_target_pairs={{0,16},{16,0},{32,48},{48,32},{64,80},{80,64},{96,112},{112,96},{1... | collective-permute-start | bytes 1376264 | tf_op jit(solution)/shard_map/ppermute | solution.py:334
  15.7 1.9 %collective-permute-start = (bf16[448,512]{1,0:T(8,128)(2,1)}, bf16[448,512]{1,0:T(8,128)(2,1)S(1)}, u32[]{:S(2)}, u32[]{:S(2)}) collective-permute-start(bf16[448,512]{1,0:T(8,128)(2,1)} %refs_96_.1), channel_id=1, source_target_pairs={{0,16},{16,0},{32,48},{48,32},{64,80},{80,64},{96,112},{112,96},{1... | collective-permute-start | bytes 1376264 | tf_op jit(solution)/shard_map/ppermute | solution.py:334
  17.6 2.4 %collective-permute-start.1 = (bf16[448,512]{1,0:T(8,128)(2,1)}, bf16[448,512]{1,0:T(8,128)(2,1)S(1)}, u32[]{:S(2)}, u32[]{:S(2)}) collective-permute-start(bf16[448,512]{1,0:T(8,128)(2,1)} %refs_97_.1), channel_id=1, source_target_pairs={{0,16},{16,0},{32,48},{48,32},{64,80},{80,64},{96,112},{112,96},{1... | collective-permute-start | bytes 1376264 | tf_op jit(solution)/shard_map/ppermute | solution.py:334
  20.1 0.0 copy-start.2
  20.1 0.0 collective-permute-done.rest_3_.refs_99_
  20.1 0.0 copy-start.3
  20.1 1.6 %collective-permute-done.1.rest_4_.refs_100_ = bf16[448,512]{1,0:T(8,128)(2,1)S(1)} collective-permute-done((bf16[448,512]{1,0:T(8,128)(2,1)}, bf16[448,512]{1,0:T(8,128)(2,1)S(1)}, u32[]{:S(2)}, u32[]{:S(2)}) %collective-permute-start.1) | collective-permute-done | bytes 458784 | tf_op jit(solution)/shard_map/ppermute | solution.py:334
  21.7 2.2 %all-to-all-done.rows_ref = bf16[16,224,128]{2,1,0:T(8,128)(2,1)S(1)} async-done(((bf16[16,224,128]{2,1,0:T(8,128)(2,1)}), bf16[16,224,128]{2,1,0:T(8,128)(2,1)S(1)}, u32[]{:S(2)}, u32[]{:S(2)}) %all-to-all-start) | async-done | bytes 917536 | tf_op jit(solution)/shard_map/all_to_all | solution.py:310
  23.8 4.9 %shard_map.111 = (bf16[32,512]{1,0:T(8,128)(2,1)}, bf16[32,512]{1,0:T(8,128)(2,1)}, bf16[32,512]{1,0:T(8,128)(2,1)}, bf16[32,512]{1,0:T(8,128)(2,1)}, bf16[32,51...) custom-call(bf16[16,224,128]{2,1,0:T(8,128)(2,1)S(1)} %all-to-all-do, ...), custom_call_target="tpu_custom_call" | custom-call | flops 1409286144 | bytes 4063232 | tf_op jit(solution)/shard_map/pallas_call | solution.py:337
  28.7 81.2 %all-reduce.2 = (bf16[32,512]{1,0:T(8,128)(2,1)}, bf16[32,512]{1,0:T(8,128)(2,1)}, bf16[32,512]{1,0:T(8,128)(2,1)}, bf16[32,512]{1,0:T(8,128)(2,1)}, bf16[32,512...) all-reduce(bf16[32,512]{1,0:T(8,128)(2,1)} %get-tuple-element.111, ...), channel_id=1, replica_groups=mesh['expert'=32,'dp'=16] {'dp'}, use_global_device_ids=true, to_apply=%region_0.0 | all-reduce | flops 1572864 | bytes 6291456 | tf_op jit(solution)/shard_map/psum | solution.py:350
  109.9 6.3 %shard_map.112 = (bf16[512,3072]{1,0:T(8,128)(2,1)S(1)}, bf16[16,224,128]{2,1,0:T(8,128)(2,1)}) custom-call(bf16[32,512]{1,0:T(8,128)(2,1)} %get-tuple-element.217.refs_0_, bf16[32,512]{1,0:T(8,128)(2,1)} %get-tuple-element.218.refs_1_, bf16[32,512]{1,0:T(8,128)(2,1)} %get-tuple-element.219.refs_2_, bf16[32,512]{1,0:T(8,128)(2,1)} %get-tuple-element.220.refs_3_, ...), custom_call_target="tpu_custom_call" | custom-call | flops 1409286144 | bytes 7208960 | tf_op jit(solution)/shard_map/pallas_call | solution.py:351
  116.2 4.3 %all-to-all-start.1 = ((bf16[16,224,128]{2,1,0:T(8,128)(2,1)}), bf16[16,224,128]{2,1,0:T(8,128)(2,1)}, u32[]{:S(2)}, u32[]{:S(2)}) async-start(bf16[16,224,128]{2,1,0:T(8,128)(2,1)} %get-tuple-element.207), calls=%async_computation.1 | async-start | bytes 1835008 | tf_op jit(solution)/shard_map/all_to_all | solution.py:310
  120.6 1.2 copy-done.1
  121.8 1.0 shard_map.114
  122.8 0.0 copy-start.5
  122.8 0.0 copy-start.6
  122.8 11.0 %collective-permute-start.3 = (bf16[448,512]{1,0:T(8,128)(2,1)S(1)}, bf16[448,512]{1,0:T(8,128)(2,1)S(1)}, u32[]{:S(2)}, u32[]{:S(2)}) collective-permute-start(bf16[448,512]{1,0:T(8,128)(2,1)S(1)} %get-tuple-element.211), channel_id=1, source_target_pairs={{0,16},{16,0},{32,48},{48,32},{64,80},{80,64},{96,112},{112,96},{1... | collective-permute-start | bytes 1376264 | tf_op jit(solution)/shard_map/ppermute | solution.py:385
  133.8 1.9 %collective-permute-start.4 = (bf16[448,512]{1,0:T(8,128)(2,1)S(1)}, bf16[448,512]{1,0:T(8,128)(2,1)S(1)}, u32[]{:S(2)}, u32[]{:S(2)}) collective-permute-start(bf16[448,512]{1,0:T(8,128)(2,1)S(1)} %get-tuple-element.212), channel_id=1, source_target_pairs={{0,16},{16,0},{32,48},{48,32},{64,80},{80,64},{96,112},{112,96},{1... | collective-permute-start | bytes 1376264 | tf_op jit(solution)/shard_map/ppermute | solution.py:385
  135.7 2.4 %collective-permute-start.5 = (bf16[448,512]{1,0:T(8,128)(2,1)S(1)}, bf16[448,512]{1,0:T(8,128)(2,1)S(1)}, u32[]{:S(2)}, u32[]{:S(2)}) collective-permute-start(bf16[448,512]{1,0:T(8,128)(2,1)S(1)} %get-tuple-element.213), channel_id=1, source_target_pairs={{0,16},{16,0},{32,48},{48,32},{64,80},{80,64},{96,112},{112,96},{1... | collective-permute-start | bytes 1376264 | tf_op jit(solution)/shard_map/ppermute | solution.py:385
  138.1 1.4 collective-permute-done.5.rest_2_
  139.5 1.8 %shard_map.115 = (bf16[448,512]{1,0:T(8,128)(2,1)}, bf16[448,512]{1,0:T(8,128)(2,1)}, bf16[448,512]{1,0:T(8,128)(2,1)}) custom-call(bf16[16,224,128]{2,1,0:T(8,128)(2,1)S(1)} %copy-done.1, bf16[512,3072]{1,0:T(8,128)(2,1)S(1)} %get-tuple-element.210.acts_ref, bf16[448,512]{1,0:T(8,128)(2,1)S(1)} %collective-permute-done.3.rest_0_, ...), custom_call_target="tpu_custom_call" | custom-call | flops 704643072 | bytes 2490368 | tf_op jit(solution)/shard_map/pallas_call | solution.py:370
  141.3 2.5 %shard_map.113 = (bf16[448,128]{1,0:T(8,128)(2,1)}, bf16[448,128]{1,0:T(8,128)(2,1)}) custom-call(bf16[16,224,128]{2,1,0:T(8,128)(2,1)} %all-to-all-done.1.ret_hbm, s32[2,128]{1,0:T(2,128)S(1)} %bitcast.9, f32[2,128]{1,0:T(2,128)S(1)} %bitcast.11), custom_call_target="tpu_custom_call" | custom-call | flops 176160768 | bytes 1835008 | tf_op jit(solution)/shard_map/pallas_call | solution.py:388
  (13 shorter events, 0.0 us)
Async XLA Ops:
  3.2 20.6 %all-to-all-start = ((bf16[16,224,128]{2,1,0:T(8,128)(2,1)}), bf16[16,224,128]{2,1,0:T(8,128)(2,1)S(1)}, u32[]{:S(2)}, u32[]{:S(2)}) async-start(bf16[16,224,128]{2,1,0:T(8,128)(2,1)} %shard_map.110), calls=%async_computation | async-start | bytes 1835008 | tf_op jit(solution)/shard_map/all_to_all | solution.py:310
  10.8 9.2 %collective-permute-start.2 = (bf16[448,512]{1,0:T(8,128)(2,1)}, bf16[448,512]{1,0:T(8,128)(2,1)S(1)}, u32[]{:S(2)}, u32[]{:S(2)}) collective-permute-start(bf16[448,512]{1,0:T(8,128)(2,1)} %bitcast.12), channel_id=1, source_target_pairs={{0,16},{16,0},{32,48},{48,32},{64,80},{80,64},{96,112},{112,96},{1... | collective-permute-start | bytes 1376264 | tf_op jit(solution)/shard_map/ppermute | solution.py:334
  15.7 4.4 %collective-permute-start = (bf16[448,512]{1,0:T(8,128)(2,1)}, bf16[448,512]{1,0:T(8,128)(2,1)S(1)}, u32[]{:S(2)}, u32[]{:S(2)}) collective-permute-start(bf16[448,512]{1,0:T(8,128)(2,1)} %refs_96_.1), channel_id=1, source_target_pairs={{0,16},{16,0},{32,48},{48,32},{64,80},{80,64},{96,112},{112,96},{1... | collective-permute-start | bytes 1376264 | tf_op jit(solution)/shard_map/ppermute | solution.py:334
  17.6 4.0 %collective-permute-start.1 = (bf16[448,512]{1,0:T(8,128)(2,1)}, bf16[448,512]{1,0:T(8,128)(2,1)S(1)}, u32[]{:S(2)}, u32[]{:S(2)}) collective-permute-start(bf16[448,512]{1,0:T(8,128)(2,1)} %refs_97_.1), channel_id=1, source_target_pairs={{0,16},{16,0},{32,48},{48,32},{64,80},{80,64},{96,112},{112,96},{1... | collective-permute-start | bytes 1376264 | tf_op jit(solution)/shard_map/ppermute | solution.py:334
  20.1 89.9 %copy-start.2 = (bf16[448,512]{1,0:T(8,128)(2,1)}, bf16[448,512]{1,0:T(8,128)(2,1)S(1)}, u32[]{:S(2)}) copy-start(bf16[448,512]{1,0:T(8,128)(2,1)S(1)} %collective-permute-done.2.rest_5_.refs_101_) | copy-start | bytes 1376260
  20.1 89.8 %copy-start.3 = (bf16[448,512]{1,0:T(8,128)(2,1)}, bf16[448,512]{1,0:T(8,128)(2,1)S(1)}, u32[]{:S(2)}) copy-start(bf16[448,512]{1,0:T(8,128)(2,1)S(1)} %collective-permute-done.rest_3_.refs_99_) | copy-start | bytes 1376260
  21.7 88.2 %copy-start.4 = (bf16[448,512]{1,0:T(8,128)(2,1)}, bf16[448,512]{1,0:T(8,128)(2,1)S(1)}, u32[]{:S(2)}) copy-start(bf16[448,512]{1,0:T(8,128)(2,1)S(1)} %collective-permute-done.1.rest_4_.refs_100_) | copy-start | bytes 1376260
  23.8 86.1 %copy-start = (bf16[16,224,128]{2,1,0:T(8,128)(2,1)}, bf16[16,224,128]{2,1,0:T(8,128)(2,1)S(1)}, u32[]{:S(2)}) copy-start(bf16[16,224,128]{2,1,0:T(8,128)(2,1)S(1)} %all-to-all-done.rows_ref) | copy-start | bytes 2752516
  116.2 25.1 %all-to-all-start.1 = ((bf16[16,224,128]{2,1,0:T(8,128)(2,1)}), bf16[16,224,128]{2,1,0:T(8,128)(2,1)}, u32[]{:S(2)}, u32[]{:S(2)}) async-start(bf16[16,224,128]{2,1,0:T(8,128)(2,1)} %get-tuple-element.207), calls=%async_computation.1 | async-start | bytes 1835008 | tf_op jit(solution)/shard_map/all_to_all | solution.py:310
  120.6 1.2 copy-start.1
  122.8 18.6 %copy-start.5 = (s32[128,2]{0,1:T(2,128)S(1)}, s32[128,2]{0,1:T(2,128)}, u32[]{:S(2)}) copy-start(s32[128,2]{0,1:T(2,128)} %param.8) | copy-start | bytes 3076
  122.8 18.6 %copy-start.6 = (f32[128,2]{0,1:T(2,128)S(1)}, f32[128,2]{0,1:T(2,128)}, u32[]{:S(2)}) copy-start(f32[128,2]{0,1:T(2,128)} %param.9) | copy-start | bytes 3076
  122.8 15.3 %collective-permute-start.3 = (bf16[448,512]{1,0:T(8,128)(2,1)S(1)}, bf16[448,512]{1,0:T(8,128)(2,1)S(1)}, u32[]{:S(2)}, u32[]{:S(2)}) collective-permute-start(bf16[448,512]{1,0:T(8,128)(2,1)S(1)} %get-tuple-element.211), channel_id=1, source_target_pairs={{0,16},{16,0},{32,48},{48,32},{64,80},{80,64},{96,112},{112,96},{1... | collective-permute-start | bytes 1376264 | tf_op jit(solution)/shard_map/ppermute | solution.py:385
  133.8 4.4 %collective-permute-start.4 = (bf16[448,512]{1,0:T(8,128)(2,1)S(1)}, bf16[448,512]{1,0:T(8,128)(2,1)S(1)}, u32[]{:S(2)}, u32[]{:S(2)}) collective-permute-start(bf16[448,512]{1,0:T(8,128)(2,1)S(1)} %get-tuple-element.212), channel_id=1, source_target_pairs={{0,16},{16,0},{32,48},{48,32},{64,80},{80,64},{96,112},{112,96},{1... | collective-permute-start | bytes 1376264 | tf_op jit(solution)/shard_map/ppermute | solution.py:385
  135.7 3.8 %collective-permute-start.5 = (bf16[448,512]{1,0:T(8,128)(2,1)S(1)}, bf16[448,512]{1,0:T(8,128)(2,1)S(1)}, u32[]{:S(2)}, u32[]{:S(2)}) collective-permute-start(bf16[448,512]{1,0:T(8,128)(2,1)S(1)} %get-tuple-element.213), channel_id=1, source_target_pairs={{0,16},{16,0},{32,48},{48,32},{64,80},{80,64},{96,112},{112,96},{1... | collective-permute-start | bytes 1376264 | tf_op jit(solution)/shard_map/ppermute | solution.py:385

commit v8 on v7

--- a/solution.py
+++ b/solution.py
@@ -77,7 +77,7 @@
 
 def send_kernel(
     experts, cap, tok_hbm, cot_hbm, routes_hbm, weight_hbm,
-    out_ref, tok_ref, cot_ref, routes_ref, weight_ref, sems,
+    out_hbm, tok_ref, cot_ref, routes_ref, weight_ref, out_ref, sems,
 ):
     dsl, ntok = tok_ref.shape
     main, first, _ = layout(dsl)
@@ -100,32 +100,50 @@
     tok = tok_ref[...]
     cot = cot_ref[...].astype(F32)
     weight = weight_ref[...]
-    rows = None
-    for k, pick in enumerate(picks):
+    rights = []
+    for k in range(2):
         dy = (cot * weight[k : k + 1, :]).astype(BF)
-        right = jnp.concatenate([tok[:main], dy[:main], tok[main:], dy[main:]], axis=0)
-        part = dot_nt(pick, right)
-        rows = part if rows is None else rows + part
-    rows = rows.astype(BF)
-    for t in range(2 * len(first) - 1):
-        put_tile(out_ref, 0, experts, cap, t, rows[:, t * LANES : (t + 1) * LANES])
-
-
-def terms_kernel(cap, rows_ref, *rest):
+        rights.append(
+            jnp.concatenate([tok[:main], dy[:main], tok[main:], dy[main:]], axis=0)
+        )
+    away = []
+    step = experts // 2
+    for lo in range(0, experts, step):
+        hi = lo + step
+        at = slice(lo * cap, hi * cap)
+        rows = dot_nt(picks[0][at], rights[0]) + dot_nt(picks[1][at], rights[1])
+        rows = rows.astype(BF)
+        for t in range(2 * len(first) - 1):
+            put_tile(out_ref, lo, hi, cap, t, rows[:, t * LANES : (t + 1) * LANES])
+        blocks = pl.ds(lo, step)
+        away.append(
+            pltpu.make_async_copy(
+                out_ref.at[blocks], out_hbm.at[blocks], sems.at[4 + len(away)]
+            )
+        )
+        away[-1].start()
+    for c in away:
+        c.wait()
+
+
+def fetch_kernel(*refs):
+    out_ref, sems = refs[-2:]
+    copies = [
+        pltpu.make_async_copy(src, out_ref.at[i], sems.at[i])
+        for i, src in enumerate(refs[:-2])
+    ]
+    for c in copies:
+        c.start()
+    for c in copies:
+        c.wait()
+
+
+def terms_kernel(cap, rows_ref, near_ref, down_hbm, *rest):
     sources = rows_ref.shape[0]
-    own_hbm, others, outs, (held, own_ref, sems) = (
-        rest[:3],
-        rest[3:6],
-        rest[6:-3],
-        rest[-3:],
-    )
-    dsl, half = others[0].shape
-    fetches = [
-        pltpu.make_async_copy(own_hbm[j], own_ref.at[j], sems.at[len(outs) + j])
-        for j in range(3)
-    ]
-    for c in fetches:
-        c.start()
+    others, outs, (held, down_ref, sems) = rest[:3], rest[3:-3], rest[-3:]
+    _, dsl, half = near_ref.shape
+    fetch = pltpu.make_async_copy(down_hbm, down_ref, sems.at[len(outs)])
+    fetch.start()
     main, first, second = layout(dsl)
     gap = jnp.zeros((dsl - main, half), BF)
     step = 256 // cap
@@ -134,11 +152,11 @@
         x = tiles(rows_ref, lo, lo + step, cap, first)
         dy = tiles(rows_ref, lo, lo + step, cap, second)
         at = slice(lo * cap, (lo + step) * cap)
-        for q in (1, 3, 5, 0, 2, 4):
+        for q in (0, 1, 2, 3, 5, 4):
             j, h = divmod(q, 2)
-            if lo == 0 and h == 0:
-                fetches[j].wait()
-            w = others[j][...] if h else own_ref[j]
+            if lo == 0 and q == 4:
+                fetch.wait()
+            w = others[j][...] if h else down_ref[...] if j == 2 else near_ref[j]
             if j == 2:
                 w = jnp.concatenate([w[:main], gap, w[main:]], axis=0)
             left = dy if j == 2 else x[:, :dsl]
@@ -314,39 +332,48 @@
     block = shape((experts, (2 * len(first) - 1) * cap, LANES), BF)
     padded = shape((3, main + LANES, half), BF)
     w_own = [w_gate, w_up, w_down.T]
-    stack = shape((3, dsl, half), BF)
     send = pl.pallas_call(
         functools.partial(send_kernel, experts, cap),
-        out_shape=block,
+        out_shape=pltpu.HBM(block.shape, BF),
         in_specs=[hbm] * 4,
-        out_specs=vmem,
+        out_specs=hbm,
         scratch_shapes=[
             pltpu.VMEM((dsl, ntok), BF),
             pltpu.VMEM((dsl, ntok), BF),
             pltpu.VMEM((top, ntok), jnp.int32),
             pltpu.VMEM((top, ntok), F32),
-            pltpu.SemaphoreType.DMA((4,)),
+            pltpu.VMEM(block.shape, BF),
+            pltpu.SemaphoreType.DMA((6,)),
         ],
         compiler_params=params(),
         cost_estimate=cost(4 * rows * ntok * dsl, 2 * rows * dsl * 4),
     )(*(in_hbm(a) for a in (tokens.T, cotangent.T, routes_t, weight_t)))
     got = exchange(send)
     w_other = [lax.ppermute(w, "expert", swap) for w in w_own]
+    near = pl.pallas_call(
+        fetch_kernel,
+        out_shape=shape((2, dsl, half), BF),
+        in_specs=[hbm] * 2,
+        out_specs=vmem,
+        scratch_shapes=[pltpu.SemaphoreType.DMA((2,))],
+        compiler_params=params(),
+        cost_estimate=cost(0, 8 * dsl * half),
+    )(in_hbm(w_gate), in_hbm(w_up))
 
     n = 6 * experts
     pieces = pl.pallas_call(
         functools.partial(terms_kernel, cap),
         out_shape=[pltpu.HBM((cap, half), BF)] * n,
-        in_specs=[vmem] + [hbm] * 3 + [vmem] * 3,
+        in_specs=[vmem] * 2 + [hbm] + [vmem] * 3,
         out_specs=[hbm] * n,
         scratch_shapes=[
             pltpu.VMEM((rows, 6 * half), BF),
-            pltpu.VMEM(stack.shape, BF),
-            pltpu.SemaphoreType.DMA((n + 3,)),
+            pltpu.VMEM((dsl, half), BF),
+            pltpu.SemaphoreType.DMA((n + 1,)),
         ],
         compiler_params=params(),
         cost_estimate=cost(6 * flops, 2 * rows * (dsl * 2 + 6 * half)),
-    )(got, *(in_hbm(w) for w in w_own), *w_other)
+    )(got, near, in_hbm(w_own[2]), *w_other)
     sums = [in_hbm(a) for a in lax.psum(list(pieces), "dp")]
     acts, ret = pl.pallas_call(
         functools.partial(back_kernel, dsl, cap, n),

time: 145 us -> 144 us (level)
    pallas_call x1 -> x2, Pallas kernels: 2.61 us -> 3.64 us  [the longest x1 2.46 us: per_device(): pl.pallas_call(functools.partial(send_kernel, experts, cap), out_shape=pl...]
  transfers between devices with their start and end apart: 8 -> 8, of which waited for: 3 -> 3; matrix products, arithmetic and copies ran while one was open for 0% -> 0% of each run, Pallas kernels for 2% -> 3%
where the time goes in v8:
time: 144 us; the launch traced here: 143 us
  blocking collectives  81.2 us (56%)
  starting transfers between devices  36.5 us (25%)
  Pallas kernels  19.4 us (13%)
  waiting for transfers between devices  3.96 us (3%)
    psum x1, blocking collectives, per_device(): sums = [in_hbm(a) for a in lax.psum(list(pieces), 'dp')]  81.2 us
    ppermute x3, starting transfers between devices, per_device(): lax.ppermute(g, 'expert', swap)  15.4 us
    all_to_all x2, starting transfers between devices, exchange(): lax.all_to_all(a, 'expert', 0, 0, axis_index_groups=cores, tiled=True)  11.9 us
    ppermute x3, starting transfers between devices, per_device(): w_other = [lax.ppermute(w, 'expert', swap) for w in w_own]  9.17 us
    pallas_call x1, Pallas kernels, per_device(): pl.pallas_call(functools.partial(back_kernel, dsl, cap, n), out_shape=[sh...  6.3 us
    pallas_call x1, Pallas kernels, per_device(): pl.pallas_call(functools.partial(terms_kernel, cap), out_shape=[pltpu.HBM...  4.17 us
  transfers between devices with their start and end apart: 8, of which 3 were waited for; matrix products, arithmetic and copies ran while one was open for 0% of the time, Pallas kernels for 3%

profile of v8, /device:TPU:1, one launch (start us, length us, event | category | flops | bytes accessed | tf_op | source)
XLA Modules:
  0.0 143.1 jit_solution(12656253234660044803)
XLA Ops:
  0.6 2.5 %shard_map.110 = bf16[16,224,128]{2,1,0:T(8,128)(2,1)} custom-call(bf16[448,128]{1,0:T(8,128)(2,1)} %bitcast.15, bf16[448,128]{1,0:T(8,128)(2,1)} %bitcast.16, s32[2,128]{1,0:T(2,128)} %bitcast.8, f32[2,128]{1,0:T(2,128)} %bitcast.10), custom_call_target="tpu_custom_call" | custom-call | flops 117440512 | bytes 1835008 | tf_op jit(solution)/shard_map/pallas_call | solution.py:335
  3.1 7.6 %all-to-all-start = ((bf16[16,224,128]{2,1,0:T(8,128)(2,1)}), bf16[16,224,128]{2,1,0:T(8,128)(2,1)S(1)}, u32[]{:S(2)}, u32[]{:S(2)}) async-start(bf16[16,224,128]{2,1,0:T(8,128)(2,1)} %shard_map.110), calls=%async_computation | async-start | bytes 1835008 | tf_op jit(solution)/shard_map/all_to_all | solution.py:328
  10.7 4.8 %collective-permute-start.2 = (bf16[448,512]{1,0:T(8,128)(2,1)}, bf16[448,512]{1,0:T(8,128)(2,1)S(1)}, u32[]{:S(2)}, u32[]{:S(2)}) collective-permute-start(bf16[448,512]{1,0:T(8,128)(2,1)} %bitcast.12), channel_id=1, source_target_pairs={{0,16},{16,0},{32,48},{48,32},{64,80},{80,64},{96,112},{112,96},{1... | collective-permute-start | bytes 1376264 | tf_op jit(solution)/shard_map/ppermute | solution.py:352
  15.6 1.9 %collective-permute-start = (bf16[448,512]{1,0:T(8,128)(2,1)}, bf16[448,512]{1,0:T(8,128)(2,1)S(1)}, u32[]{:S(2)}, u32[]{:S(2)}) collective-permute-start(bf16[448,512]{1,0:T(8,128)(2,1)} %refs_96_.1), channel_id=1, source_target_pairs={{0,16},{16,0},{32,48},{48,32},{64,80},{80,64},{96,112},{112,96},{1... | collective-permute-start | bytes 1376264 | tf_op jit(solution)/shard_map/ppermute | solution.py:352
  17.5 2.4 %collective-permute-start.1 = (bf16[448,512]{1,0:T(8,128)(2,1)}, bf16[448,512]{1,0:T(8,128)(2,1)S(1)}, u32[]{:S(2)}, u32[]{:S(2)}) collective-permute-start(bf16[448,512]{1,0:T(8,128)(2,1)} %refs_97_.1), channel_id=1, source_target_pairs={{0,16},{16,0},{32,48},{48,32},{64,80},{80,64},{96,112},{112,96},{1... | collective-permute-start | bytes 1376264 | tf_op jit(solution)/shard_map/ppermute | solution.py:352
  19.9 1.2 shard_map.111.near_ref
  21.1 0.0 copy-start.2
  21.1 0.0 copy-start.3
  21.1 0.4 collective-permute-done.1.rest_1_.refs_100_
  21.5 2.1 %all-to-all-done.rows_ref = bf16[16,224,128]{2,1,0:T(8,128)(2,1)S(1)} async-done(((bf16[16,224,128]{2,1,0:T(8,128)(2,1)}), bf16[16,224,128]{2,1,0:T(8,128)(2,1)S(1)}, u32[]{:S(2)}, u32[]{:S(2)}) %all-to-all-start) | async-done | bytes 917536 | tf_op jit(solution)/shard_map/all_to_all | solution.py:328
  23.7 4.2 %shard_map.112 = (bf16[32,512]{1,0:T(8,128)(2,1)}, bf16[32,512]{1,0:T(8,128)(2,1)}, bf16[32,512]{1,0:T(8,128)(2,1)}, bf16[32,512]{1,0:T(8,128)(2,1)}, bf16[32,51...) custom-call(bf16[16,224,128]{2,1,0:T(8,128)(2,1)S(1)} %all-to-all-do, ...), custom_call_target="tpu_custom_call" | custom-call | flops 1409286144 | bytes 4063232 | tf_op jit(solution)/shard_map/pallas_call | solution.py:364
  27.9 81.2 %all-reduce.2 = (bf16[32,512]{1,0:T(8,128)(2,1)}, bf16[32,512]{1,0:T(8,128)(2,1)}, bf16[32,512]{1,0:T(8,128)(2,1)}, bf16[32,512]{1,0:T(8,128)(2,1)}, bf16[32,512...) all-reduce(bf16[32,512]{1,0:T(8,128)(2,1)} %get-tuple-element.111, ...), channel_id=1, replica_groups=mesh['expert'=32,'dp'=16] {'dp'}, use_global_device_ids=true, to_apply=%region_0.0 | all-reduce | flops 1572864 | bytes 6291456 | tf_op jit(solution)/shard_map/psum | solution.py:377
  109.1 6.3 %shard_map.113 = (bf16[512,3072]{1,0:T(8,128)(2,1)S(1)}, bf16[16,224,128]{2,1,0:T(8,128)(2,1)}) custom-call(bf16[32,512]{1,0:T(8,128)(2,1)} %get-tuple-element.217.refs_0_, bf16[32,512]{1,0:T(8,128)(2,1)} %get-tuple-element.218.refs_1_, bf16[32,512]{1,0:T(8,128)(2,1)} %get-tuple-element.219.refs_2_, bf16[32,512]{1,0:T(8,128)(2,1)} %get-tuple-element.220.refs_3_, ...), custom_call_target="tpu_custom_call" | custom-call | flops 1409286144 | bytes 7208960 | tf_op jit(solution)/shard_map/pallas_call | solution.py:378
  115.4 4.3 %all-to-all-start.1 = ((bf16[16,224,128]{2,1,0:T(8,128)(2,1)}), bf16[16,224,128]{2,1,0:T(8,128)(2,1)}, u32[]{:S(2)}, u32[]{:S(2)}) async-start(bf16[16,224,128]{2,1,0:T(8,128)(2,1)} %get-tuple-element.207), calls=%async_computation.1 | async-start | bytes 1835008 | tf_op jit(solution)/shard_map/all_to_all | solution.py:328
  119.7 1.2 copy-done.1
  120.9 1.0 shard_map.115
  121.9 0.0 copy-start.5
  121.9 0.0 copy-start.6
  121.9 11.0 %collective-permute-start.3 = (bf16[448,512]{1,0:T(8,128)(2,1)S(1)}, bf16[448,512]{1,0:T(8,128)(2,1)S(1)}, u32[]{:S(2)}, u32[]{:S(2)}) collective-permute-start(bf16[448,512]{1,0:T(8,128)(2,1)S(1)} %get-tuple-element.211), channel_id=1, source_target_pairs={{0,16},{16,0},{32,48},{48,32},{64,80},{80,64},{96,112},{112,96},{1... | collective-permute-start | bytes 1376264 | tf_op jit(solution)/shard_map/ppermute | solution.py:412
  133.0 1.9 %collective-permute-start.4 = (bf16[448,512]{1,0:T(8,128)(2,1)S(1)}, bf16[448,512]{1,0:T(8,128)(2,1)S(1)}, u32[]{:S(2)}, u32[]{:S(2)}) collective-permute-start(bf16[448,512]{1,0:T(8,128)(2,1)S(1)} %get-tuple-element.212), channel_id=1, source_target_pairs={{0,16},{16,0},{32,48},{48,32},{64,80},{80,64},{96,112},{112,96},{1... | collective-permute-start | bytes 1376264 | tf_op jit(solution)/shard_map/ppermute | solution.py:412
  134.9 2.4 %collective-permute-start.5 = (bf16[448,512]{1,0:T(8,128)(2,1)S(1)}, bf16[448,512]{1,0:T(8,128)(2,1)S(1)}, u32[]{:S(2)}, u32[]{:S(2)}) collective-permute-start(bf16[448,512]{1,0:T(8,128)(2,1)S(1)} %get-tuple-element.213), channel_id=1, source_target_pairs={{0,16},{16,0},{32,48},{48,32},{64,80},{80,64},{96,112},{112,96},{1... | collective-permute-start | bytes 1376264 | tf_op jit(solution)/shard_map/ppermute | solution.py:412
  137.3 1.4 collective-permute-done.5.rest_2_
  138.7 1.8 %shard_map.116 = (bf16[448,512]{1,0:T(8,128)(2,1)}, bf16[448,512]{1,0:T(8,128)(2,1)}, bf16[448,512]{1,0:T(8,128)(2,1)}) custom-call(bf16[16,224,128]{2,1,0:T(8,128)(2,1)S(1)} %copy-done.1, bf16[512,3072]{1,0:T(8,128)(2,1)S(1)} %get-tuple-element.210.acts_ref, bf16[448,512]{1,0:T(8,128)(2,1)S(1)} %collective-permute-done.3.rest_0_, ...), custom_call_target="tpu_custom_call" | custom-call | flops 704643072 | bytes 2490368 | tf_op jit(solution)/shard_map/pallas_call | solution.py:397
  140.5 2.5 %shard_map.114 = (bf16[448,128]{1,0:T(8,128)(2,1)}, bf16[448,128]{1,0:T(8,128)(2,1)}) custom-call(bf16[16,224,128]{2,1,0:T(8,128)(2,1)} %all-to-all-done.1.ret_hbm, s32[2,128]{1,0:T(2,128)S(1)} %bitcast.9, f32[2,128]{1,0:T(2,128)S(1)} %bitcast.11), custom_call_target="tpu_custom_call" | custom-call | flops 176160768 | bytes 1835008 | tf_op jit(solution)/shard_map/pallas_call | solution.py:415
  (14 shorter events, 0.0 us)
Async XLA Ops:
  3.1 20.6 %all-to-all-start = ((bf16[16,224,128]{2,1,0:T(8,128)(2,1)}), bf16[16,224,128]{2,1,0:T(8,128)(2,1)S(1)}, u32[]{:S(2)}, u32[]{:S(2)}) async-start(bf16[16,224,128]{2,1,0:T(8,128)(2,1)} %shard_map.110), calls=%async_computation | async-start | bytes 1835008 | tf_op jit(solution)/shard_map/all_to_all | solution.py:328
  10.7 10.4 %collective-permute-start.2 = (bf16[448,512]{1,0:T(8,128)(2,1)}, bf16[448,512]{1,0:T(8,128)(2,1)S(1)}, u32[]{:S(2)}, u32[]{:S(2)}) collective-permute-start(bf16[448,512]{1,0:T(8,128)(2,1)} %bitcast.12), channel_id=1, source_target_pairs={{0,16},{16,0},{32,48},{48,32},{64,80},{80,64},{96,112},{112,96},{1... | collective-permute-start | bytes 1376264 | tf_op jit(solution)/shard_map/ppermute | solution.py:352
  15.6 5.6 %collective-permute-start = (bf16[448,512]{1,0:T(8,128)(2,1)}, bf16[448,512]{1,0:T(8,128)(2,1)S(1)}, u32[]{:S(2)}, u32[]{:S(2)}) collective-permute-start(bf16[448,512]{1,0:T(8,128)(2,1)} %refs_96_.1), channel_id=1, source_target_pairs={{0,16},{16,0},{32,48},{48,32},{64,80},{80,64},{96,112},{112,96},{1... | collective-permute-start | bytes 1376264 | tf_op jit(solution)/shard_map/ppermute | solution.py:352
  17.5 4.0 %collective-permute-start.1 = (bf16[448,512]{1,0:T(8,128)(2,1)}, bf16[448,512]{1,0:T(8,128)(2,1)S(1)}, u32[]{:S(2)}, u32[]{:S(2)}) collective-permute-start(bf16[448,512]{1,0:T(8,128)(2,1)} %refs_97_.1), channel_id=1, source_target_pairs={{0,16},{16,0},{32,48},{48,32},{64,80},{80,64},{96,112},{112,96},{1... | collective-permute-start | bytes 1376264 | tf_op jit(solution)/shard_map/ppermute | solution.py:352
  21.1 88.0 %copy-start.2 = (bf16[448,512]{1,0:T(8,128)(2,1)}, bf16[448,512]{1,0:T(8,128)(2,1)S(1)}, u32[]{:S(2)}) copy-start(bf16[448,512]{1,0:T(8,128)(2,1)S(1)} %collective-permute-done.2.rest_2_.refs_101_) | copy-start | bytes 1376260
  21.1 88.0 %copy-start.3 = (bf16[448,512]{1,0:T(8,128)(2,1)}, bf16[448,512]{1,0:T(8,128)(2,1)S(1)}, u32[]{:S(2)}) copy-start(bf16[448,512]{1,0:T(8,128)(2,1)S(1)} %collective-permute-done.rest_0_.refs_99_) | copy-start | bytes 1376260
  21.5 87.5 %copy-start.4 = (bf16[448,512]{1,0:T(8,128)(2,1)}, bf16[448,512]{1,0:T(8,128)(2,1)S(1)}, u32[]{:S(2)}) copy-start(bf16[448,512]{1,0:T(8,128)(2,1)S(1)} %collective-permute-done.1.rest_1_.refs_100_) | copy-start | bytes 1376260
  23.7 85.4 %copy-start = (bf16[16,224,128]{2,1,0:T(8,128)(2,1)}, bf16[16,224,128]{2,1,0:T(8,128)(2,1)S(1)}, u32[]{:S(2)}) copy-start(bf16[16,224,128]{2,1,0:T(8,128)(2,1)S(1)} %all-to-all-done.rows_ref) | copy-start | bytes 2752516
  115.4 25.1 %all-to-all-start.1 = ((bf16[16,224,128]{2,1,0:T(8,128)(2,1)}), bf16[16,224,128]{2,1,0:T(8,128)(2,1)}, u32[]{:S(2)}, u32[]{:S(2)}) async-start(bf16[16,224,128]{2,1,0:T(8,128)(2,1)} %get-tuple-element.207), calls=%async_computation.1 | async-start | bytes 1835008 | tf_op jit(solution)/shard_map/all_to_all | solution.py:328
  119.7 1.2 copy-start.1
  121.9 18.6 %copy-start.5 = (s32[128,2]{0,1:T(2,128)S(1)}, s32[128,2]{0,1:T(2,128)}, u32[]{:S(2)}) copy-start(s32[128,2]{0,1:T(2,128)} %param.8) | copy-start | bytes 3076
  121.9 18.6 %copy-start.6 = (f32[128,2]{0,1:T(2,128)S(1)}, f32[128,2]{0,1:T(2,128)}, u32[]{:S(2)}) copy-start(f32[128,2]{0,1:T(2,128)} %param.9) | copy-start | bytes 3076
  121.9 15.4 %collective-permute-start.3 = (bf16[448,512]{1,0:T(8,128)(2,1)S(1)}, bf16[448,512]{1,0:T(8,128)(2,1)S(1)}, u32[]{:S(2)}, u32[]{:S(2)}) collective-permute-start(bf16[448,512]{1,0:T(8,128)(2,1)S(1)} %get-tuple-element.211), channel_id=1, source_target_pairs={{0,16},{16,0},{32,48},{48,32},{64,80},{80,64},{96,112},{112,96},{1... | collective-permute-start | bytes 1376264 | tf_op jit(solution)/shard_map/ppermute | solution.py:412
  133.0 4.4 %collective-permute-start.4 = (bf16[448,512]{1,0:T(8,128)(2,1)S(1)}, bf16[448,512]{1,0:T(8,128)(2,1)S(1)}, u32[]{:S(2)}, u32[]{:S(2)}) collective-permute-start(bf16[448,512]{1,0:T(8,128)(2,1)S(1)} %get-tuple-element.212), channel_id=1, source_target_pairs={{0,16},{16,0},{32,48},{48,32},{64,80},{80,64},{96,112},{112,96},{1... | collective-permute-start | bytes 1376264 | tf_op jit(solution)/shard_map/ppermute | solution.py:412
  134.9 3.8 %collective-permute-start.5 = (bf16[448,512]{1,0:T(8,128)(2,1)S(1)}, bf16[448,512]{1,0:T(8,128)(2,1)S(1)}, u32[]{:S(2)}, u32[]{:S(2)}) collective-permute-start(bf16[448,512]{1,0:T(8,128)(2,1)S(1)} %get-tuple-element.213), channel_id=1, source_target_pairs={{0,16},{16,0},{32,48},{48,32},{64,80},{80,64},{96,112},{112,96},{1... | collective-permute-start | bytes 1376264 | tf_op jit(solution)/shard_map/ppermute | solution.py:412

commit v9 on v8

--- a/solution.py
+++ b/solution.py
@@ -271,28 +271,37 @@
     return grad[:dsl]
 
 
-def other_grads_kernel(dsl, cap, rows_ref, acts_ref, *outs):
+def grads_kernel(dsl, cap, rows_ref, acts_ref, *outs):
     for j, out_ref in enumerate(outs):
-        out_ref[...] = grad_of(dsl, cap, rows_ref, acts_ref, j).astype(BF)
-
-
-def own_grads_kernel(dsl, cap, rows_ref, acts_ref, *rest):
+        out_ref[...] = grad_of(dsl, cap, rows_ref, acts_ref, j).astype(out_ref.dtype)
+
+
+def add_kernel(*refs):
     for j in range(3):
-        part = grad_of(dsl, cap, rows_ref, acts_ref, j)
-        rest[3 + j][...] = (part + rest[j][...].astype(F32)).astype(BF)
+        refs[6 + j][...] = (refs[j][...] + refs[3 + j][...].astype(F32)).astype(BF)
 
 
 def combine_kernel(
     experts, cap, ret_hbm, routes_ref, weight_ref, out_ref, grad_ref, ret_ref, sem
 ):
-    fetch = pltpu.make_async_copy(ret_hbm, ret_ref, sem)
-    fetch.start()
+    step = experts // 4
+    fetches = [
+        pltpu.make_async_copy(
+            ret_hbm.at[pl.ds(i * step, step)],
+            ret_ref.at[pl.ds(i * step, step)],
+            sem.at[i],
+        )
+        for i in range(4)
+    ]
+    for c in fetches:
+        c.start()
     dsl = out_ref.shape[0]
     main, first, _ = layout(dsl)
     tail = dsl - main
     picks = pickers(routes_ref[...], experts, cap)
     weight = weight_ref[...]
-    fetch.wait()
+    for c in fetches:
+        c.wait()
     rows = tiles(ret_ref, 0, experts, cap, range(2 * len(first) - 1))
     out = back = None
     for k, pick in enumerate(picks):
@@ -392,32 +401,34 @@
     )(*sums, *(in_hbm(w) for w in w_own + w_other))
     ret = exchange(ret)
 
-    def grads(kernel, part, *more):
-        whole = pl.BlockSpec((dsl, half), lambda i: (0, 0))
+    def grads(part, dtype):
         return pl.pallas_call(
-            functools.partial(kernel, dsl, cap),
+            functools.partial(grads_kernel, dsl, cap),
             grid=(1,),
-            out_shape=[shape((dsl, half), BF)] * 3,
+            out_shape=[shape((dsl, half), dtype)] * 3,
             in_specs=[
                 pl.BlockSpec(block.shape, lambda i: (0, 0, 0)),
                 pl.BlockSpec((rows, 3 * half), lambda i: (0, part)),
-            ]
-            + [whole] * len(more),
-            out_specs=[whole] * 3,
+            ],
+            out_specs=[pl.BlockSpec((dsl, half), lambda i: (0, 0))] * 3,
             compiler_params=params(),
             cost_estimate=cost(3 * flops, 2 * rows * (dsl * 2 + 3 * half)),
-        )(got, acts, *more)
-
-    theirs = [
-        lax.ppermute(g, "expert", swap) for g in grads(other_grads_kernel, 1)
-    ]
-    grad_gate, grad_up, grad_down_t = grads(own_grads_kernel, 0, *theirs)
+        )(got, acts)
+
+    theirs = [lax.ppermute(g, "expert", swap) for g in grads(1, BF)]
+    mine = grads(0, F32)
+    grad_gate, grad_up, grad_down_t = pl.pallas_call(
+        add_kernel,
+        out_shape=[shape((dsl, half), BF)] * 3,
+        compiler_params=params(),
+        cost_estimate=cost(3 * dsl * half, 24 * dsl * half),
+    )(*mine, *theirs)
     output_t, grad_tokens_t = pl.pallas_call(
         functools.partial(combine_kernel, experts, cap),
         out_shape=[shape((dsl, ntok), BF)] * 2,
         in_specs=[hbm, vmem, vmem],
         out_specs=[vmem] * 2,
-        scratch_shapes=[pltpu.VMEM(block.shape, BF), pltpu.SemaphoreType.DMA(())],
+        scratch_shapes=[pltpu.VMEM(block.shape, BF), pltpu.SemaphoreType.DMA((4,))],
         compiler_params=params(),
         cost_estimate=cost(6 * rows * ntok * dsl, 2 * rows * dsl * 4),
     )(in_hbm(ret), routes_t, weight_t)

time: 144 us -> 143 us (level)
    pallas_call x2 -> x3, Pallas kernels: 2.79 us -> 3.26 us  [the longest x2 2.01 us: grads(): pl.pallas_call(functools.partial(grads_kernel, dsl, cap), grid=(1,), out_...]
where the time goes in v9:
time: 143 us
  blocking collectives  81.1 us (57%)
  starting transfers between devices  36.5 us (26%)
  Pallas kernels  20 us (14%)
  waiting for transfers between devices  2.95 us (2%)
    psum x1, blocking collectives, per_device(): sums = [in_hbm(a) for a in lax.psum(list(pieces), 'dp')]  81.1 us
    ppermute x3, starting transfers between devices, per_device(): theirs = [lax.ppermute(g, 'expert', swap) for g in grads(1, BF)]  15.4 us
    all_to_all x2, starting transfers between devices, exchange(): lax.all_to_all(a, 'expert', 0, 0, axis_index_groups=cores, tiled=True)  11.9 us
    ppermute x3, starting transfers between devices, per_device(): w_other = [lax.ppermute(w, 'expert', swap) for w in w_own]  9.17 us
    pallas_call x1, Pallas kernels, per_device(): pl.pallas_call(functools.partial(back_kernel, dsl, cap, n), out_shape=[sh...  6.31 us
    pallas_call x1, Pallas kernels, per_device(): pl.pallas_call(functools.partial(terms_kernel, cap), out_shape=[pltpu.HBM...  4.15 us
  transfers between devices with their start and end apart: 8, of which 3 were waited for; matrix products, arithmetic and copies ran while one was open for 0% of the time, Pallas kernels for 3%

profile of v9, /device:TPU:1, one launch (start us, length us, event | category | flops | bytes accessed | tf_op | source)
XLA Modules:
  0.0 142.6 jit_solution(16652595440396542844)
XLA Ops:
  0.6 2.5 %shard_map.110 = bf16[16,224,128]{2,1,0:T(8,128)(2,1)} custom-call(bf16[448,128]{1,0:T(8,128)(2,1)} %bitcast.15, bf16[448,128]{1,0:T(8,128)(2,1)} %bitcast.16, s32[2,128]{1,0:T(2,128)} %bitcast.8, f32[2,128]{1,0:T(2,128)} %bitcast.10), custom_call_target="tpu_custom_call" | custom-call | flops 117440512 | bytes 1835008 | tf_op jit(solution)/shard_map/pallas_call | solution.py:344
  3.1 7.6 %all-to-all-start = ((bf16[16,224,128]{2,1,0:T(8,128)(2,1)}), bf16[16,224,128]{2,1,0:T(8,128)(2,1)S(1)}, u32[]{:S(2)}, u32[]{:S(2)}) async-start(bf16[16,224,128]{2,1,0:T(8,128)(2,1)} %shard_map.110), calls=%async_computation | async-start | bytes 1835008 | tf_op jit(solution)/shard_map/all_to_all | solution.py:337
  10.7 4.8 %collective-permute-start.2 = (bf16[448,512]{1,0:T(8,128)(2,1)}, bf16[448,512]{1,0:T(8,128)(2,1)S(1)}, u32[]{:S(2)}, u32[]{:S(2)}) collective-permute-start(bf16[448,512]{1,0:T(8,128)(2,1)} %bitcast.12), channel_id=1, source_target_pairs={{0,16},{16,0},{32,48},{48,32},{64,80},{80,64},{96,112},{112,96},{1... | collective-permute-start | bytes 1376264 | tf_op jit(solution)/shard_map/ppermute | solution.py:361
  15.5 1.9 %collective-permute-start = (bf16[448,512]{1,0:T(8,128)(2,1)}, bf16[448,512]{1,0:T(8,128)(2,1)S(1)}, u32[]{:S(2)}, u32[]{:S(2)}) collective-permute-start(bf16[448,512]{1,0:T(8,128)(2,1)} %refs_96_.1), channel_id=1, source_target_pairs={{0,16},{16,0},{32,48},{48,32},{64,80},{80,64},{96,112},{112,96},{1... | collective-permute-start | bytes 1376264 | tf_op jit(solution)/shard_map/ppermute | solution.py:361
  17.5 2.4 %collective-permute-start.1 = (bf16[448,512]{1,0:T(8,128)(2,1)}, bf16[448,512]{1,0:T(8,128)(2,1)S(1)}, u32[]{:S(2)}, u32[]{:S(2)}) collective-permute-start(bf16[448,512]{1,0:T(8,128)(2,1)} %refs_97_.1), channel_id=1, source_target_pairs={{0,16},{16,0},{32,48},{48,32},{64,80},{80,64},{96,112},{112,96},{1... | collective-permute-start | bytes 1376264 | tf_op jit(solution)/shard_map/ppermute | solution.py:361
  19.9 1.2 shard_map.111.near_ref
  21.1 0.0 copy-start.2
  21.1 0.0 copy-start.3
  21.1 0.4 collective-permute-done.1.rest_1_.refs_100_
  21.5 2.1 %all-to-all-done.rows_ref = bf16[16,224,128]{2,1,0:T(8,128)(2,1)S(1)} async-done(((bf16[16,224,128]{2,1,0:T(8,128)(2,1)}), bf16[16,224,128]{2,1,0:T(8,128)(2,1)S(1)}, u32[]{:S(2)}, u32[]{:S(2)}) %all-to-all-start) | async-done | bytes 917536 | tf_op jit(solution)/shard_map/all_to_all | solution.py:337
  23.7 4.1 %shard_map.112 = (bf16[32,512]{1,0:T(8,128)(2,1)}, bf16[32,512]{1,0:T(8,128)(2,1)}, bf16[32,512]{1,0:T(8,128)(2,1)}, bf16[32,512]{1,0:T(8,128)(2,1)}, bf16[32,51...) custom-call(bf16[16,224,128]{2,1,0:T(8,128)(2,1)S(1)} %all-to-all-do, ...), custom_call_target="tpu_custom_call" | custom-call | flops 1409286144 | bytes 4063232 | tf_op jit(solution)/shard_map/pallas_call | solution.py:373
  27.8 81.1 %all-reduce.2 = (bf16[32,512]{1,0:T(8,128)(2,1)}, bf16[32,512]{1,0:T(8,128)(2,1)}, bf16[32,512]{1,0:T(8,128)(2,1)}, bf16[32,512]{1,0:T(8,128)(2,1)}, bf16[32,512...) all-reduce(bf16[32,512]{1,0:T(8,128)(2,1)} %get-tuple-element.114, ...), channel_id=1, replica_groups=mesh['expert'=32,'dp'=16] {'dp'}, use_global_device_ids=true, to_apply=%region_0.0 | all-reduce | flops 1572864 | bytes 6291456 | tf_op jit(solution)/shard_map/psum | solution.py:386
  108.9 6.3 %shard_map.113 = (bf16[512,3072]{1,0:T(8,128)(2,1)S(1)}, bf16[16,224,128]{2,1,0:T(8,128)(2,1)}) custom-call(bf16[32,512]{1,0:T(8,128)(2,1)} %get-tuple-element.223.refs_0_, bf16[32,512]{1,0:T(8,128)(2,1)} %get-tuple-element.224.refs_1_, bf16[32,512]{1,0:T(8,128)(2,1)} %get-tuple-element.225.refs_2_, bf16[32,512]{1,0:T(8,128)(2,1)} %get-tuple-element.226.refs_3_, ...), custom_call_target="tpu_custom_call" | custom-call | flops 1409286144 | bytes 7208960 | tf_op jit(solution)/shard_map/pallas_call | solution.py:387
  115.3 4.3 %all-to-all-start.1 = ((bf16[16,224,128]{2,1,0:T(8,128)(2,1)}), bf16[16,224,128]{2,1,0:T(8,128)(2,1)}, u32[]{:S(2)}, u32[]{:S(2)}) async-start(bf16[16,224,128]{2,1,0:T(8,128)(2,1)} %get-tuple-element.210), calls=%async_computation.1 | async-start | bytes 1835008 | tf_op jit(solution)/shard_map/all_to_all | solution.py:337
  119.6 1.2 copy-done.1
  120.8 1.0 shard_map.116
  121.8 11.1 %collective-permute-start.3 = (bf16[448,512]{1,0:T(8,128)(2,1)S(1)}, bf16[448,512]{1,0:T(8,128)(2,1)S(1)}, u32[]{:S(2)}, u32[]{:S(2)}) collective-permute-start(bf16[448,512]{1,0:T(8,128)(2,1)S(1)} %get-tuple-element.217), channel_id=1, source_target_pairs={{0,16},{16,0},{32,48},{48,32},{64,80},{80,64},{96,112},{112,96},{1... | collective-permute-start | bytes 1376264 | tf_op jit(solution)/shard_map/ppermute | solution.py:418
  132.9 1.9 %collective-permute-start.4 = (bf16[448,512]{1,0:T(8,128)(2,1)S(1)}, bf16[448,512]{1,0:T(8,128)(2,1)S(1)}, u32[]{:S(2)}, u32[]{:S(2)}) collective-permute-start(bf16[448,512]{1,0:T(8,128)(2,1)S(1)} %get-tuple-element.218), channel_id=1, source_target_pairs={{0,16},{16,0},{32,48},{48,32},{64,80},{80,64},{96,112},{112,96},{1... | collective-permute-start | bytes 1376264 | tf_op jit(solution)/shard_map/ppermute | solution.py:418
  134.8 0.0 copy-start.5
  134.9 2.4 %collective-permute-start.5 = (bf16[448,512]{1,0:T(8,128)(2,1)S(1)}, bf16[448,512]{1,0:T(8,128)(2,1)S(1)}, u32[]{:S(2)}, u32[]{:S(2)}) collective-permute-start(bf16[448,512]{1,0:T(8,128)(2,1)S(1)} %get-tuple-element.219), channel_id=1, source_target_pairs={{0,16},{16,0},{32,48},{48,32},{64,80},{80,64},{96,112},{112,96},{1... | collective-permute-start | bytes 1376264 | tf_op jit(solution)/shard_map/ppermute | solution.py:418
  137.3 1.0 shard_map.115
  138.3 0.4 collective-permute-done.5.refs_5_
  138.7 1.2 shard_map.117
  140.0 2.7 %shard_map.114 = (bf16[448,128]{1,0:T(8,128)(2,1)}, bf16[448,128]{1,0:T(8,128)(2,1)}) custom-call(bf16[16,224,128]{2,1,0:T(8,128)(2,1)} %all-to-all-done.1.ret_hbm, s32[2,128]{1,0:T(2,128)S(1)} %bitcast.9, f32[2,128]{1,0:T(2,128)S(1)} %bitcast.11), custom_call_target="tpu_custom_call" | custom-call | flops 176160768 | bytes 1835008 | tf_op jit(solution)/shard_map/pallas_call | solution.py:426
  (15 shorter events, 0.0 us)
Async XLA Ops:
  3.1 20.6 %all-to-all-start = ((bf16[16,224,128]{2,1,0:T(8,128)(2,1)}), bf16[16,224,128]{2,1,0:T(8,128)(2,1)S(1)}, u32[]{:S(2)}, u32[]{:S(2)}) async-start(bf16[16,224,128]{2,1,0:T(8,128)(2,1)} %shard_map.110), calls=%async_computation | async-start | bytes 1835008 | tf_op jit(solution)/shard_map/all_to_all | solution.py:337
  10.7 10.4 %collective-permute-start.2 = (bf16[448,512]{1,0:T(8,128)(2,1)}, bf16[448,512]{1,0:T(8,128)(2,1)S(1)}, u32[]{:S(2)}, u32[]{:S(2)}) collective-permute-start(bf16[448,512]{1,0:T(8,128)(2,1)} %bitcast.12), channel_id=1, source_target_pairs={{0,16},{16,0},{32,48},{48,32},{64,80},{80,64},{96,112},{112,96},{1... | collective-permute-start | bytes 1376264 | tf_op jit(solution)/shard_map/ppermute | solution.py:361
  15.5 5.6 %collective-permute-start = (bf16[448,512]{1,0:T(8,128)(2,1)}, bf16[448,512]{1,0:T(8,128)(2,1)S(1)}, u32[]{:S(2)}, u32[]{:S(2)}) collective-permute-start(bf16[448,512]{1,0:T(8,128)(2,1)} %refs_96_.1), channel_id=1, source_target_pairs={{0,16},{16,0},{32,48},{48,32},{64,80},{80,64},{96,112},{112,96},{1... | collective-permute-start | bytes 1376264 | tf_op jit(solution)/shard_map/ppermute | solution.py:361
  17.5 4.0 %collective-permute-start.1 = (bf16[448,512]{1,0:T(8,128)(2,1)}, bf16[448,512]{1,0:T(8,128)(2,1)S(1)}, u32[]{:S(2)}, u32[]{:S(2)}) collective-permute-start(bf16[448,512]{1,0:T(8,128)(2,1)} %refs_97_.1), channel_id=1, source_target_pairs={{0,16},{16,0},{32,48},{48,32},{64,80},{80,64},{96,112},{112,96},{1... | collective-permute-start | bytes 1376264 | tf_op jit(solution)/shard_map/ppermute | solution.py:361
  21.1 87.8 %copy-start.2 = (bf16[448,512]{1,0:T(8,128)(2,1)}, bf16[448,512]{1,0:T(8,128)(2,1)S(1)}, u32[]{:S(2)}) copy-start(bf16[448,512]{1,0:T(8,128)(2,1)S(1)} %collective-permute-done.2.rest_2_.refs_101_) | copy-start | bytes 1376260
  21.1 87.8 %copy-start.3 = (bf16[448,512]{1,0:T(8,128)(2,1)}, bf16[448,512]{1,0:T(8,128)(2,1)S(1)}, u32[]{:S(2)}) copy-start(bf16[448,512]{1,0:T(8,128)(2,1)S(1)} %collective-permute-done.rest_0_.refs_99_) | copy-start | bytes 1376260
  21.5 87.4 %copy-start.4 = (bf16[448,512]{1,0:T(8,128)(2,1)}, bf16[448,512]{1,0:T(8,128)(2,1)S(1)}, u32[]{:S(2)}) copy-start(bf16[448,512]{1,0:T(8,128)(2,1)S(1)} %collective-permute-done.1.rest_1_.refs_100_) | copy-start | bytes 1376260
  23.7 85.3 %copy-start = (bf16[16,224,128]{2,1,0:T(8,128)(2,1)}, bf16[16,224,128]{2,1,0:T(8,128)(2,1)S(1)}, u32[]{:S(2)}) copy-start(bf16[16,224,128]{2,1,0:T(8,128)(2,1)S(1)} %all-to-all-done.rows_ref) | copy-start | bytes 2752516
  115.3 24.7 %all-to-all-start.1 = ((bf16[16,224,128]{2,1,0:T(8,128)(2,1)}), bf16[16,224,128]{2,1,0:T(8,128)(2,1)}, u32[]{:S(2)}, u32[]{:S(2)}) async-start(bf16[16,224,128]{2,1,0:T(8,128)(2,1)} %get-tuple-element.210), calls=%async_computation.1 | async-start | bytes 1835008 | tf_op jit(solution)/shard_map/all_to_all | solution.py:337
  119.6 1.2 copy-start.1
  121.8 16.5 %collective-permute-start.3 = (bf16[448,512]{1,0:T(8,128)(2,1)S(1)}, bf16[448,512]{1,0:T(8,128)(2,1)S(1)}, u32[]{:S(2)}, u32[]{:S(2)}) collective-permute-start(bf16[448,512]{1,0:T(8,128)(2,1)S(1)} %get-tuple-element.217), channel_id=1, source_target_pairs={{0,16},{16,0},{32,48},{48,32},{64,80},{80,64},{96,112},{112,96},{1... | collective-permute-start | bytes 1376264 | tf_op jit(solution)/shard_map/ppermute | solution.py:418
  132.9 5.4 %collective-permute-start.4 = (bf16[448,512]{1,0:T(8,128)(2,1)S(1)}, bf16[448,512]{1,0:T(8,128)(2,1)S(1)}, u32[]{:S(2)}, u32[]{:S(2)}) collective-permute-start(bf16[448,512]{1,0:T(8,128)(2,1)S(1)} %get-tuple-element.218), channel_id=1, source_target_pairs={{0,16},{16,0},{32,48},{48,32},{64,80},{80,64},{96,112},{112,96},{1... | collective-permute-start | bytes 1376264 | tf_op jit(solution)/shard_map/ppermute | solution.py:418
  134.8 5.1 %copy-start.5 = (s32[128,2]{0,1:T(2,128)S(1)}, s32[128,2]{0,1:T(2,128)}, u32[]{:S(2)}) copy-start(s32[128,2]{0,1:T(2,128)} %param.8) | copy-start | bytes 3076
  134.8 5.1 %copy-start.6 = (f32[128,2]{0,1:T(2,128)S(1)}, f32[128,2]{0,1:T(2,128)}, u32[]{:S(2)}) copy-start(f32[128,2]{0,1:T(2,128)} %param.9) | copy-start | bytes 3076
  134.9 3.8 %collective-permute-start.5 = (bf16[448,512]{1,0:T(8,128)(2,1)S(1)}, bf16[448,512]{1,0:T(8,128)(2,1)S(1)}, u32[]{:S(2)}, u32[]{:S(2)}) collective-permute-start(bf16[448,512]{1,0:T(8,128)(2,1)S(1)} %get-tuple-element.219), channel_id=1, source_target_pairs={{0,16},{16,0},{32,48},{48,32},{64,80},{80,64},{96,112},{112,96},{1... | collective-permute-start | bytes 1376264 | tf_op jit(solution)/shard_map/ppermute | solution.py:418
